TPU v7x, 32 devices: a whole 2x2x4 slice. The times are simulated.
32 devices in a mesh: dp: 8 (over y, x, core), expert: 4 (over z).
Axes of the slice: x: 2, y: 2, z: 4, core: 2. Of those that a mesh axis runs over, the one named last changes fastest.
Arguments:
- tokens: bfloat16 [4096, 2048], P(('dp', 'expert')), may hold values from -6 to 6
- routes: int32 [4096, 2], P(('dp', 'expert')), may hold values from 0 to 3, all different within a row; in each aligned block of 128 rows (0 to 127, 128 to 255, ...) at most 64 rows name the same one
- route_scores: float32 [4096, 2], P(('dp', 'expert')), may hold values from -4 to 4
- out_grad: bfloat16 [4096, 2048], P(('dp', 'expert')), may hold values from -6 to 6
- gate_up: bfloat16 [4, 2048, 1024], P('expert'), may hold values from -0.125 to 0.125
- down_weight: bfloat16 [4, 2048, 512], P('expert'), may hold values from -0.25 to 0.25
Outputs:
- mixed_out: bfloat16 [4096, 2048], P(('dp', 'expert'))
- token_grad: bfloat16 [4096, 2048], P(('dp', 'expert'))
- grad_gate_up: float32 [4, 2048, 1024], P('expert', 'dp')
- grad_down: float32 [4, 2048, 512], P('expert', 'dp')
Inputs may be any that keep to these rules, and one draw needn't show every extreme that they name: `routes`: the 2 experts of a token differ. Among the 128 tokens of one device no expert is named more than 64 times, and in some device's tokens an expert is named exactly 64 times.
All inputs are finite; a program needn't handle non-finite values.
Results may differ from a plain program's by a relative error of at most 0.015.
Values may be sent and summed in bfloat16 or wider, within the bound.
No kernel may reach another device: no remote copies, remote signals or barrier semaphores. Data moves between devices by JAX's collectives and lax.ppermute only.
A program may use at most 64 MiB of HBM per device.

v0:
```python
import functools

import jax
import jax.numpy as jnp
from jax import lax
from jax.experimental import pallas as pl
from jax.experimental.pallas import tpu as pltpu
from jax.sharding import PartitionSpec as P

F32 = jnp.float32
BF16 = jnp.bfloat16
BRIEF = pl.CostEstimate(flops=1024, bytes_accessed=1024, transcendentals=0)
COVER = pl.CostEstimate(flops=4 * 10**10, bytes_accessed=1024, transcendentals=0)
ROOMY = pltpu.CompilerParams(vmem_limit_bytes=16 * 1024 * 1024)
BIG = pltpu.CompilerParams(vmem_limit_bytes=28 * 1024 * 1024)
ALONE = pltpu.CompilerParams(vmem_limit_bytes=60 * 1024 * 1024)


def contract(left, right):
    return lax.dot_general(left, right, (((0,), (0,)), ((), ())), preferred_element_type=F32)


def slot_rows(first, routes, experts, capacity):
    tops, toks = routes.shape
    padded = -(-experts // 8) * 8
    rows = lax.broadcasted_iota(jnp.int32, (padded, toks), 0)
    ids = rows + first
    ids = jnp.where(ids >= experts, ids - experts, ids)
    ids = jnp.where(rows < experts, ids, -1)
    hits = [routes[k : k + 1, :] == ids for k in range(tops)]
    named = functools.reduce(jnp.logical_or, hits)
    before = lax.broadcasted_iota(jnp.int32, (toks, toks), 0) < lax.broadcasted_iota(
        jnp.int32, (toks, toks), 1
    )
    position = jnp.dot(
        named.astype(F32).astype(BF16),
        before.astype(F32).astype(BF16),
        preferred_element_type=F32,
    )
    slot = position + (rows * capacity).astype(F32)
    return [jnp.sum(jnp.where(hit, slot, 0.0), axis=0, keepdims=True) for hit in hits]


def weight_rows(scores):
    grown = jnp.exp(scores)
    return grown / jnp.sum(grown, axis=0, keepdims=True)


def to_column(row):
    toks = row.shape[1]
    same = lax.broadcasted_iota(jnp.int32, (toks, toks), 0) == lax.broadcasted_iota(
        jnp.int32, (toks, toks), 1
    )
    return jnp.sum(jnp.where(same, row, 0.0), axis=1, keepdims=True)


def put_blocks(outs, rows, columns):
    start = 0
    for out in outs:
        size = out.shape[0]
        out[:, columns] = rows[start : start + size]
        start += size


def column_steps(width):
    step = 512 if width % 512 == 0 else width
    return [slice(at, at + step) for at in range(0, width, step)]


def dispatch_kernel(experts, capacity, weighted, first, *refs):
    count = 2 + weighted
    sources, refs = refs[:count], refs[count:]
    number = (len(refs) - count - 2) // 2
    outs, ready, (*held, sems, out_sems) = refs[:number], refs[number : 2 * number], refs[2 * number :]
    copies = [
        pltpu.make_async_copy(source, place, sems.at[n])
        for n, (source, place) in enumerate(zip(sources, held))
    ]
    for copy in copies:
        copy.start()
    routes, values = held[0], held[-1]
    scores = held[1] if weighted else None
    for copy in copies[:-1]:
        copy.wait()
    slots, toks = experts * capacity, values.shape[0]
    places = lax.broadcasted_iota(jnp.int32, (slots, toks), 0).astype(F32)
    hits = [places == row for row in slot_rows(first[0], routes[...], experts, capacity)]
    picker = functools.reduce(jnp.logical_or, hits).astype(F32).astype(BF16)
    if weighted:
        weights = weight_rows(scores[...])
        scale = sum(
            jnp.sum(jnp.where(hit, weights[k : k + 1, :], 0.0), axis=1, keepdims=True)
            for k, hit in enumerate(hits)
        )
    copies[-1].wait()
    stores = []
    for c, columns in enumerate(column_steps(values.shape[1])):
        rows = jnp.dot(picker, values[:, columns], preferred_element_type=F32)
        if weighted:
            rows = rows * scale
        put_blocks(ready, rows.astype(BF16), columns)
        for n, (block, out) in enumerate(zip(ready, outs)):
            stores.append(
                pltpu.make_async_copy(block.at[:, columns], out.at[:, columns], out_sems.at[c, n])
            )
            stores[-1].start()
    for store in stores:
        store.wait()


def combine_kernel(experts, capacity, weighted, first, routes, *refs):
    scores = refs[0] if weighted else None
    blocks, out = refs[weighted:-1], refs[-1]
    slots, toks = experts * capacity, out.shape[0]
    places = lax.broadcasted_iota(jnp.int32, (toks, slots), 1).astype(F32)
    hits = [
        places == to_column(row) for row in slot_rows(first[0], routes[...], experts, capacity)
    ]
    if weighted:
        weights = weight_rows(scores[...])
        scales = [to_column(weights[k : k + 1, :]) for k in range(len(hits))]
        pickers = [hit.astype(F32).astype(BF16) for hit in hits]
    else:
        pickers = [functools.reduce(jnp.logical_or, hits).astype(F32).astype(BF16)]
    for columns in column_steps(out.shape[1]):
        rows = [block[:, columns] for block in blocks]
        rows = rows[0] if len(rows) == 1 else jnp.concatenate(rows, axis=0)
        picked = [jnp.dot(picker, rows, preferred_element_type=F32) for picker in pickers]
        if weighted:
            picked = [scale * part for scale, part in zip(scales, picked)]
        out[:, columns] = sum(picked).astype(out.dtype)


def whole(count):
    return [pl.BlockSpec(memory_space=pltpu.VMEM)] * count


def write_shares(at, rows_t, grads_t, pre_grad, hidden, out):
    share = out.shape[1]
    wide, narrow = pre_grad.shape[1] // 2, hidden.shape[1] // 2

    def write(t, half):
        own = pl.ds(pl.multiple_of(at[t] * share, share), share)
        out[t, :, :wide] = jnp.dot(
            rows_t[own, :],
            pre_grad[:, half * wide : (half + 1) * wide],
            preferred_element_type=F32,
        ).astype(out.dtype)
        out[t, :, wide:] = jnp.dot(
            grads_t[own, :],
            hidden[:, half * narrow : (half + 1) * narrow],
            preferred_element_type=F32,
        ).astype(out.dtype)

    for t in range(out.shape[0]):
        write(t, t // 2 % 2)


def transpose_into(rows, rows_t):
    width = rows.shape[1]
    step = 256 if width % 256 == 0 else width

    @pl.loop(0, width // step)
    def _(c):
        own = pl.ds(pl.multiple_of(c * step, step), step)
        rows_t[own, :] = rows[:, own].T


def join_copies(blocks, rows, sems):
    size = blocks[0].shape[0]
    joins = [
        pltpu.make_async_copy(block, rows.at[pl.ds(n * size, size)], sems.at[n])
        for n, block in enumerate(blocks)
    ]
    for join in joins:
        join.start()
    return joins


def forward_kernel(count, *refs):
    blocks, (w_in_hbm, down_hbm), (rows_t, preact, hidden), outs, scratch = (
        refs[:count],
        refs[count : count + 2],
        refs[count + 2 : count + 5],
        refs[count + 5 : 2 * count + 5],
        refs[2 * count + 5 :],
    )
    rows, w_in, down, block_sems, weight_sems, down_sem = scratch
    joins = join_copies(blocks, rows, block_sems)
    width, units = down.shape
    step = 256 if units % 256 == 0 else units
    loads = []
    for n in range(2 * units // step):
        begin = (n % 2) * units + n // 2 * step
        loads.append(
            pltpu.make_async_copy(
                w_in_hbm.at[:, pl.ds(begin, step)],
                w_in.at[:, pl.ds(begin, step)],
                weight_sems.at[n],
            )
        )
        loads[-1].start()
    load_down = pltpu.make_async_copy(down_hbm, down, down_sem)
    load_down.start()
    for join in joins:
        join.wait()
    for n in range(units // step):
        begin = n * step
        gate_at, up_at = slice(begin, begin + step), slice(units + begin, units + begin + step)
        loads[2 * n].wait()
        gate = jnp.dot(rows[...], w_in[:, gate_at], preferred_element_type=F32)
        loads[2 * n + 1].wait()
        up = jnp.dot(rows[...], w_in[:, up_at], preferred_element_type=F32)
        preact[:, gate_at] = gate
        preact[:, up_at] = up
        hidden[:, gate_at] = (gate / (1.0 + jnp.exp(-gate)) * up).astype(BF16)
    load_down.wait()
    for columns in column_steps(width):
        part = lax.dot_general(
            hidden[...], down[columns, :], (((1,), (1,)), ((), ())), preferred_element_type=F32
        )
        put_blocks(outs, part.astype(BF16), columns)
    transpose_into(rows, rows_t)


def forward(blocks, w_in, down):
    width, units = down.shape
    slots = sum(block.shape[0] for block in blocks)
    count = len(blocks)
    rows_t, preact, hidden, *outs = pl.pallas_call(
        functools.partial(forward_kernel, count),
        out_shape=(
            jax.ShapeDtypeStruct((width, slots), BF16),
            jax.ShapeDtypeStruct((slots, 2 * units), F32),
            jax.ShapeDtypeStruct((slots, units), BF16),
            *[jax.ShapeDtypeStruct(block.shape, BF16) for block in blocks],
        ),
        in_specs=anywhere(count) + in_hbm(2),
        out_specs=whole(3 + count),
        scratch_shapes=[
            pltpu.VMEM((slots, width), BF16),
            pltpu.VMEM(w_in.shape, BF16),
            pltpu.VMEM(down.shape, BF16),
            pltpu.SemaphoreType.DMA((count,)),
            pltpu.SemaphoreType.DMA((2 * units // min(units, 256),)),
            pltpu.SemaphoreType.DMA,
        ],
        compiler_params=pltpu.CompilerParams(vmem_limit_bytes=46 * 1024 * 1024),
        cost_estimate=BRIEF,
    )(*blocks, w_in, down)
    return rows_t, preact, hidden, outs


def backward_kernel(count, at, preact_hbm, w_in_hbm, rows_t, hidden, down, *refs):
    blocks, (pre_grad, grads_t, sent, w_in, *refs) = refs[:count], refs[count:]
    grads, preact, block_sems, load_sem, sem = refs
    joins = join_copies(blocks, grads, block_sems)
    fetch = pltpu.make_async_copy(preact_hbm, preact, sem)
    fetch.start()
    load = pltpu.make_async_copy(w_in_hbm, w_in, load_sem)
    load.start()
    units = down.shape[1]
    for join in joins:
        join.wait()
    fetch.wait()
    step = 256 if units % 256 == 0 else units
    for begin in range(0, units, step):
        gate = preact[:, begin : begin + step]
        up = preact[:, units + begin : units + begin + step]
        hidden_grad = jnp.dot(
            grads[...], down[:, begin : begin + step], preferred_element_type=F32
        )
        sigmoid = 1.0 / (1.0 + jnp.exp(-gate))
        gate_grad = hidden_grad * up * sigmoid * (1.0 + gate * (1.0 - sigmoid))
        up_grad = hidden_grad * gate * sigmoid
        pre_grad[:, begin : begin + step] = gate_grad.astype(BF16)
        pre_grad[:, units + begin : units + begin + step] = up_grad.astype(BF16)
    transpose_into(grads, grads_t)
    write_shares(at, rows_t, grads_t, pre_grad, hidden, sent)
    load.wait()


def return_kernel(count, alone, pre_grad, w_in, *refs):
    blocks, outs, sems = refs[:count], refs[count : 2 * count], refs[-1]
    size = blocks[0].shape[0]
    copies = [
        pltpu.make_async_copy(block, out.at[pl.ds(0, size)], sems.at[n])
        for n, (block, out) in enumerate(zip(blocks, outs))
        if n != alone
    ]
    for copy in copies:
        copy.start()
    for columns in column_steps(w_in.shape[0]):
        part = lax.dot_general(
            pre_grad[...], w_in[columns, :], (((1,), (1,)), ((), ())), preferred_element_type=F32
        ).astype(BF16)
        for n, out in enumerate(outs):
            out[out.shape[0] - size :, columns] = part[n * size : (n + 1) * size]
    for copy in copies:
        copy.wait()


def returns(pre_grad, w_in, produced, alone):
    count = len(produced)
    size, width = produced[0].shape
    return pl.pallas_call(
        functools.partial(return_kernel, count, alone),
        out_shape=[
            jax.ShapeDtypeStruct((size if n == alone else 2 * size, width), BF16)
            for n in range(count)
        ],
        in_specs=whole(2) + anywhere(count),
        out_specs=whole(count),
        scratch_shapes=[pltpu.SemaphoreType.DMA((count,))],
        compiler_params=ROOMY,
        cost_estimate=BRIEF,
    )(pre_grad, w_in, *produced)


def anywhere(count):
    return [pl.BlockSpec(memory_space=pl.ANY)] * count


def in_hbm(count):
    return [pl.BlockSpec(memory_space=pltpu.HBM)] * count


def backward(at, share, preact, w_in, rows_t, hidden, down, blocks):
    width, units = down.shape
    slots = preact.shape[0]
    count = len(blocks)
    return pl.pallas_call(
        functools.partial(backward_kernel, count),
        out_shape=(
            jax.ShapeDtypeStruct((slots, 2 * units), BF16),
            jax.ShapeDtypeStruct((width, slots), BF16),
            jax.ShapeDtypeStruct((at.shape[0], share, 3 * units // 2), BF16),
            jax.ShapeDtypeStruct(w_in.shape, BF16),
        ),
        in_specs=[pl.BlockSpec(memory_space=pltpu.SMEM)]
        + anywhere(2)
        + whole(3)
        + anywhere(count),
        out_specs=whole(4),
        scratch_shapes=[
            pltpu.VMEM((slots, width), BF16),
            pltpu.VMEM((slots, 2 * units), F32),
            pltpu.SemaphoreType.DMA((count,)),
            pltpu.SemaphoreType.DMA,
            pltpu.SemaphoreType.DMA,
        ],
        compiler_params=BIG,
        cost_estimate=BRIEF,
    )(at, preact, w_in, rows_t, hidden, down, *blocks)


def shares(at, share, rows_t, grads_t, pre_grad, hidden, cost):
    units = hidden.shape[1]
    return pl.pallas_call(
        write_shares,
        out_shape=jax.ShapeDtypeStruct((at.shape[0], share, 3 * units // 2), BF16),
        in_specs=[pl.BlockSpec(memory_space=pltpu.SMEM)] + whole(4),
        out_specs=whole(1)[0],
        compiler_params=ROOMY,
        cost_estimate=cost,
    )(at, rows_t, grads_t, pre_grad, hidden)


def add_kernel(kept, got, left, right):
    half = left.shape[0]
    left[...] = add(kept[:half], got[:half]).astype(BF16)
    right[...] = add(kept[half:], got[half : 2 * half]).astype(BF16)


def next_kernel(kept, got, left_in, right_in, left_send, right_send):
    first = got.shape[0] // 2
    left_send[...] = (add(kept[1], got[first + 1]) + left_in[1].astype(F32)).astype(BF16)
    right_send[...] = (add(kept[3], got[first + 3]) + right_in[1].astype(F32)).astype(BF16)


def own_kernel(kept, got, left_in, right_in, left, right):
    first = got.shape[0] // 2
    left[...] = add(kept[0], got[first]) + left_in[0].astype(F32)
    right[...] = add(kept[2], got[first + 2]) + right_in[0].astype(F32)


def add(left, right):
    return left.astype(F32) + right.astype(F32)


CUBE_SEND = (3, 7, 5, 7, 1, 5, 1, 3)


def swap(block, bit):
    return lax.ppermute(block, "dp", [(at, at ^ bit) for at in range(lax.axis_size("dp"))])


def cube_sum(got, kept_first, kept_later):
    _, share, columns = got.shape

    def run(kernel, out_shape, inputs, cost=BRIEF):
        return pl.pallas_call(
            kernel,
            out_shape=out_shape,
            in_specs=whole(len(inputs)),
            out_specs=whole(len(out_shape)),
            compiler_params=ROOMY,
            cost_estimate=cost,
        )(*inputs)

    half = jax.ShapeDtypeStruct((2, share, columns), BF16)
    one = jax.ShapeDtypeStruct((share, columns), BF16)
    own = jax.ShapeDtypeStruct((share, columns), F32)
    left, right = run(add_kernel, (half, half), (kept_first, got))
    parts = (kept_later, got, swap(left, 2), swap(right, 4))
    left_send, right_send = run(next_kernel, (one, one), parts)
    left, right = run(own_kernel, (own, own), parts, COVER)
    return left, swap(left_send, 4), right, swap(right_send, 2)


def after(value, *others):
    return lax.optimization_barrier((value, *others))[0]


def partial_kernel(experts, capacity, alone, late, first, routes, scores, *refs):
    (own, early, back_early), (mixed, back, late_picker, scales) = refs[:-4], refs[-4:]
    slots, toks = experts * capacity, mixed.shape[0]
    places = lax.broadcasted_iota(jnp.int32, (toks, slots), 1).astype(F32)
    hits = [
        places == to_column(row) for row in slot_rows(first[0], routes[...], experts, capacity)
    ]
    hits.append(functools.reduce(jnp.logical_or, hits))
    picker = jnp.concatenate([hit.astype(F32).astype(BF16) for hit in hits], axis=0)
    weights = weight_rows(scores[...])
    for k in range(scales.shape[0]):
        scales[k] = jnp.broadcast_to(to_column(weights[k : k + 1, :]), scales.shape[1:])

    def slots_of(blocks):
        parts = [picker[:, n * capacity : (n + 1) * capacity] for n in blocks]
        return jnp.concatenate(parts, axis=1)

    late_picker[...] = slots_of(late)
    now = slots_of((0, alone))
    for columns in column_steps(mixed.shape[1]):
        outputs = jnp.concatenate([own[:capacity, columns], early[:, columns]], axis=0)
        gradients = jnp.concatenate([own[capacity:, columns], back_early[:, columns]], axis=0)
        total, grad = sum_rows(now, scales, outputs, gradients)
        mixed[:, columns] = total
        back[:, columns] = grad


def sum_rows(picker, scales, outputs, gradients):
    tops, toks = scales.shape[:2]
    picked = jnp.dot(picker[: tops * toks], outputs, preferred_element_type=F32)
    total = sum(scales[k, :, :1] * picked[k * toks : (k + 1) * toks] for k in range(tops))
    return total, jnp.dot(picker[tops * toks :], gradients, preferred_element_type=F32)


def mean_kernel(count, left, left_last, right, right_last, wide, narrow):
    middle, edge = wide.shape[1] // 2, narrow.shape[1] // 2
    for at, (own, last) in enumerate(((left, left_last), (right, right_last))):
        total = (own[...] + last[...].astype(F32)) / count
        wide[:, at * middle : (at + 1) * middle] = total[:, :middle]
        narrow[:, at * edge : (at + 1) * edge] = total[:, middle:]


def means(count, sums):
    share, columns = sums[0].shape
    return pl.pallas_call(
        functools.partial(mean_kernel, count),
        out_shape=(
            jax.ShapeDtypeStruct((share, 4 * columns // 3), F32),
            jax.ShapeDtypeStruct((share, 2 * columns // 3), F32),
        ),
        in_specs=whole(4),
        out_specs=whole(2),
        compiler_params=ROOMY,
        cost_estimate=BRIEF,
    )(*sums)


def last_kernel(capacity, number, picker, scales, mixed_part, back_part, *refs):
    blocks, (mixed, back), (mixed_vmem, back_vmem, sems) = (
        refs[:number],
        refs[number : number + 2],
        refs[number + 2 :],
    )
    stores = []
    for c, columns in enumerate(column_steps(mixed.shape[1])):
        outputs = jnp.concatenate([block[:capacity, columns] for block in blocks], axis=0)
        gradients = jnp.concatenate([block[capacity:, columns] for block in blocks], axis=0)
        total, grad = sum_rows(picker[...], scales, outputs, gradients)
        mixed_vmem[:, columns] = (total + mixed_part[:, columns]).astype(BF16)
        back_vmem[:, columns] = (grad + back_part[:, columns]).astype(BF16)
        for n, (source, target) in enumerate(((mixed_vmem, mixed), (back_vmem, back))):
            stores.append(
                pltpu.make_async_copy(source.at[:, columns], target.at[:, columns], sems.at[c, n])
            )
            stores[-1].start()
    for stored in stores:
        stored.wait()


def last(capacity, parts, blocks):
    toks, width = parts[-1].shape
    out_shape = jax.ShapeDtypeStruct((toks, width), BF16)
    return pl.pallas_call(
        functools.partial(last_kernel, capacity, len(blocks)),
        out_shape=(out_shape, out_shape),
        in_specs=whole(4 + len(blocks)),
        out_specs=anywhere(2),
        scratch_shapes=[pltpu.VMEM((toks, width), BF16)] * 2
        + [pltpu.SemaphoreType.DMA((len(column_steps(width)), 2))],
        compiler_params=ROOMY,
        cost_estimate=BRIEF,
    )(*parts, *blocks)


def dispatch(experts, capacity, out_shape, first, *sources):
    weighted = len(sources) > 2
    return pl.pallas_call(
        functools.partial(dispatch_kernel, experts, capacity, weighted),
        out_shape=out_shape,
        in_specs=[pl.BlockSpec(memory_space=pltpu.SMEM)] + in_hbm(len(sources)),
        out_specs=anywhere(len(out_shape)),
        scratch_shapes=[pltpu.VMEM(out.shape, out.dtype) for out in out_shape]
        + [pltpu.VMEM(source.shape, source.dtype) for source in sources]
        + [
            pltpu.SemaphoreType.DMA((len(sources),)),
            pltpu.SemaphoreType.DMA((len(column_steps(out_shape[0].shape[1])), len(out_shape))),
        ],
        compiler_params=ALONE,
        cost_estimate=BRIEF,
    )(first, *sources)


def call(kernel, out_shape, inputs):
    return pl.pallas_call(
        kernel,
        out_shape=out_shape,
        in_specs=[pl.BlockSpec(memory_space=pltpu.SMEM)]
        + [pl.BlockSpec(memory_space=pltpu.VMEM)] * (len(inputs) - 1),
        compiler_params=ROOMY,
        cost_estimate=BRIEF,
    )(*inputs)


def body(tokens, routes, route_scores, out_grad, gate_up, down_weight):
    experts = lax.axis_size("expert")
    groups = lax.axis_size("dp")
    toks, width = tokens.shape
    tops = routes.shape[1]
    units = down_weight.shape[2]
    capacity = (toks * tops + experts - 1) // experts
    slots = experts * capacity
    share = width // groups
    direct = experts <= 8 and capacity % 16 == 0
    w_in, w_out = gate_up[0], down_weight[0]
    routes_t, scores_t = routes.T, route_scores.T
    me = lax.axis_index("expert") if direct else jnp.int32(0)
    first = me.astype(jnp.int32).reshape(1)
    sizes = [capacity] * experts if direct else [slots]
    block_shapes = [jax.ShapeDtypeStruct((size, width), BF16) for size in sizes]

    def travel(block, step, sign):
        pairs = [(at, (at + sign * step) % experts) for at in range(experts)]
        return lax.ppermute(block, "expert", pairs)

    def exchange(blocks, sign):
        if not direct:
            block = blocks[0].reshape(experts, capacity, width)
            moved = lax.all_to_all(block, "expert", split_axis=0, concat_axis=0, tiled=True)
            return [moved.reshape(slots, width)]
        steps = range(1, experts) if sign > 0 else range(experts - 1, 0, -1)
        moved = {step: travel(blocks[step], step, sign) for step in steps}
        return [blocks[0]] + [moved[step] for step in range(1, experts)]

    def joined(blocks):
        return blocks[0] if len(blocks) == 1 else jnp.concatenate(blocks, axis=0)

    def split(rows):
        return [rows[at : at + sizes[0]] for at in range(0, slots, sizes[0])]

    sent_rows = dispatch(experts, capacity, block_shapes, first, routes_t, tokens)
    got_rows = exchange(sent_rows, 1)
    sent_grads = dispatch(experts, capacity, block_shapes, first, routes_t, scores_t, out_grad)
    out_shape = jax.ShapeDtypeStruct((toks, width), BF16)
    cube = direct and experts == 4 and groups == 8 and share % 256 == 0
    if cube:
        sent_grads = after(sent_grads, got_rows[1], got_rows[-1])
        got_grads = exchange(sent_grads, 1)
        rows_t, preact, hidden, produced = forward(got_rows, w_in, w_out)
        got_grads = after(got_grads, hidden)
        own = lax.axis_index("dp")
        send_at = jnp.stack([jnp.bitwise_xor(own, j) for j in CUBE_SEND]).astype(jnp.int32)
        keep_at = jnp.bitwise_xor(send_at, 1)
        early = experts - 1
        early_out = travel(produced[early], early, -1)
        pre_grad, grads_t, sent, w_in_here = backward(
            send_at, share, preact, w_in, rows_t, hidden, w_out, got_grads
        )
        operands = (share, rows_t, grads_t, pre_grad, hidden)
        got = swap(sent, 1)
        blocks = returns(after(pre_grad, sent), w_in_here, produced, early)
        returned = exchange(blocks, -1)
        half = len(CUBE_SEND) // 2
        kept_first = shares(after(keep_at[:half], blocks[0]), *operands, COVER)
        kept_later = shares(after(keep_at[half:], kept_first, early_out, got), *operands, COVER)
        sums = cube_sum(got, kept_first, kept_later)
        late = [n for n in range(experts - 1, 0, -1) if n != early]
        mixed_part, back_part, picker, scales = call(
            functools.partial(partial_kernel, experts, capacity, early, late),
            (
                jax.ShapeDtypeStruct((toks, width), F32),
                jax.ShapeDtypeStruct((toks, width), F32),
                jax.ShapeDtypeStruct(((tops + 1) * toks, len(late) * capacity), BF16),
                jax.ShapeDtypeStruct((tops, toks, 128), F32),
            ),
            (after(first, sums[0]), routes_t, scores_t, returned[0], early_out, returned[early]),
        )
        grad_in, grad_down = means(groups, sums)
        parts = (after(picker, grad_in), scales, mixed_part, back_part)
        mixed_out, token_grad = last(capacity, parts, [returned[n] for n in late])
    else:
        token_rows = joined(got_rows)
        grad_rows = joined(exchange(sent_grads, 1))
        preact = jnp.dot(token_rows, w_in, preferred_element_type=F32)
        gate, up = preact[:, :units], preact[:, units:]
        hidden = (jax.nn.silu(gate) * up).astype(BF16)
        produced = jnp.dot(hidden, w_out.T, preferred_element_type=F32).astype(BF16)
        returned = exchange(split(produced), -1)
        hidden_grad = jnp.dot(grad_rows, w_out, preferred_element_type=F32)
        sigmoid = jax.nn.sigmoid(gate)
        gate_grad = hidden_grad * up * sigmoid * (1.0 + gate * (1.0 - sigmoid))
        up_grad = hidden_grad * gate * sigmoid
        pre_grad = jnp.concatenate([gate_grad, up_grad], axis=1).astype(BF16)
        input_grad = jnp.dot(pre_grad, w_in.T, preferred_element_type=F32).astype(BF16)
        sent_back = exchange(split(input_grad), -1)

        def summed(left, right):
            part = contract(left, right).astype(BF16)
            total = lax.psum_scatter(part, "dp", scatter_dimension=0, tiled=True)
            return total.astype(F32) / groups

        grad_in = summed(token_rows, pre_grad)
        grad_down = summed(grad_rows, hidden)
        mixed_out = call(
            functools.partial(combine_kernel, experts, capacity, True),
            out_shape,
            (first, routes_t, scores_t, *returned),
        )
        token_grad = call(
            functools.partial(combine_kernel, experts, capacity, False),
            out_shape,
            (first, routes_t, *sent_back),
        )
    grad_in = grad_in.reshape(1, share, 2 * units)
    grad_down = grad_down.reshape(1, share, units)
    return (mixed_out, token_grad, grad_in, grad_down)


def solution(mesh):
    in_specs = (
        P(("dp", "expert"), None),
        P(("dp", "expert"), None),
        P(("dp", "expert"), None),
        P(("dp", "expert"), None),
        P("expert", None, None),
        P("expert", None, None),
    )
    out_specs = (
        P(("dp", "expert"), None),
        P(("dp", "expert"), None),
        P("expert", "dp", None),
        P("expert", "dp", None),
    )
    return jax.shard_map(body, mesh=mesh, in_specs=in_specs, out_specs=out_specs, check_vma=False)
```

profile of v0, /device:TPU:11, one launch (start us, length us, event | category | flops | bytes accessed | tf_op | source)
XLA Modules:
  0.0 101.6 jit_solution(10531953735105678273)
XLA Ops:
  0.6 2.3 %shard_map.93 = (bf16[64,2048]{1,0:T(8,128)(2,1)}, bf16[64,2048]{1,0:T(8,128)(2,1)}, bf16[64,2048]{1,0:T(8,128)(2,1)}, bf16[64,2048]{1,0:T(8,128)(2,1)}) custom-call(s32[1]{0:T(128)} %bitcast.first, s32[2,128]{1,0:T(2,128)} %bitcast.15, bf16[128,2048]{1,0:T(8,128)(2,1)} %refs_1_.1), custom_call_target="tpu_custom_call" | custom-call | flops 1024 | bytes 1024 | tf_op jit(solution)/shard_map/pallas_call | solution.py:521
  3.0 1.3 %collective-permute-start = (bf16[64,2048]{1,0:T(8,128)(2,1)}, bf16[64,2048]{1,0:T(8,128)(2,1)S(1)}, u32[]{:S(2)}, u32[]{:S(2)}) collective-permute-start(bf16[64,2048]{1,0:T(8,128)(2,1)} %get-tuple-element.55), channel_id=1, source_target_pairs={{0,1},{1,2},{2,3},{3,0},{4,5},{5,6},{6,7},{7,4},{8,9},{9,10},{10,1... | collective-permute-start | bytes 786440 | tf_op jit(solution)/shard_map/ppermute | solution.py:567
  4.3 0.2 collective-permute-start.2
  4.5 2.3 %collective-permute-start.1 = (bf16[64,2048]{1,0:T(8,128)(2,1)}, bf16[64,2048]{1,0:T(8,128)(2,1)S(1)}, u32[]{:S(2)}, u32[]{:S(2)}) collective-permute-start(bf16[64,2048]{1,0:T(8,128)(2,1)} %get-tuple-element.56), channel_id=1, source_target_pairs={{0,2},{1,3},{2,0},{3,1},{4,6},{5,7},{6,4},{7,5},{8,10},{9,11},{10,... | collective-permute-start | bytes 786440 | tf_op jit(solution)/shard_map/ppermute | solution.py:567
  6.8 2.4 %shard_map.95 = (bf16[64,2048]{1,0:T(8,128)(2,1)}, bf16[64,2048]{1,0:T(8,128)(2,1)}, bf16[64,2048]{1,0:T(8,128)(2,1)}, bf16[64,2048]{1,0:T(8,128)(2,1)}) custom-call(s32[1]{0:T(128)} %bitcast.first, s32[2,128]{1,0:T(2,128)} %bitcast.16, f32[2,128]{1,0:T(2,128)} %bitcast.18, bf16[128,2048]{1,0:T(8,128)(2,1)} %refs_2_.1), custom_call_target="tpu_custom_call" | custom-call | flops 1024 | bytes 1024 | tf_op jit(solution)/shard_map/pallas_call | solution.py:521
  9.2 0.1 stack.23.at
  9.3 1.1 %collective-permute-done.refs_1_ = bf16[64,2048]{1,0:T(8,128)(2,1)S(1)} collective-permute-done((bf16[64,2048]{1,0:T(8,128)(2,1)}, bf16[64,2048]{1,0:T(8,128)(2,1)S(1)}, u32[]{:S(2)}, u32[]{:S(2)}) %collective-permute-start) | collective-permute-done | bytes 262176 | tf_op jit(solution)/shard_map/ppermute | solution.py:567
  10.4 8.5 %collective-permute-done.2.refs_3_ = bf16[64,2048]{1,0:T(8,128)(2,1)S(1)} collective-permute-done((bf16[64,2048]{1,0:T(8,128)(2,1)}, bf16[64,2048]{1,0:T(8,128)(2,1)S(1)}, u32[]{:S(2)}, u32[]{:S(2)}) %collective-permute-start.2) | collective-permute-done | bytes 262176 | tf_op jit(solution)/shard_map/ppermute | solution.py:567
  18.9 0.0 collective-permute-start.3
  18.9 1.1 %collective-permute-start.4 = (bf16[64,2048]{1,0:T(8,128)(2,1)}, bf16[64,2048]{1,0:T(8,128)(2,1)S(1)}, u32[]{:S(2)}, u32[]{:S(2)}) collective-permute-start(bf16[64,2048]{1,0:T(8,128)(2,1)} %get-tuple-element.67), channel_id=1, source_target_pairs={{0,2},{1,3},{2,0},{3,1},{4,6},{5,7},{6,4},{7,5},{8,10},{9,11},{10,... | collective-permute-start | bytes 786440 | tf_op jit(solution)/shard_map/ppermute | solution.py:567
  20.0 0.3 collective-permute-start.5
  20.3 0.1 fusion
  20.4 8.3 %collective-permute-done.1.refs_2_ = bf16[64,2048]{1,0:T(8,128)(2,1)S(1)} collective-permute-done((bf16[64,2048]{1,0:T(8,128)(2,1)}, bf16[64,2048]{1,0:T(8,128)(2,1)S(1)}, u32[]{:S(2)}, u32[]{:S(2)}) %collective-permute-start.1) | collective-permute-done | bytes 262176 | tf_op jit(solution)/shard_map/ppermute | solution.py:567
  28.7 1.6 %copy-done.1 = bf16[1,2048,512]{2,1,0:T(8,128)(2,1)S(1)} copy-done((bf16[1,2048,512]{2,1,0:T(8,128)(2,1)S(1)}, bf16[1,2048,512]{2,1,0:T(8,128)(2,1)}, u32[]{:S(2)}) %copy-start.1) | copy-done | bytes 2097176
  30.3 0.9 copy-done.3
  31.2 5.8 %shard_map.94 = (bf16[2048,256]{1,0:T(8,128)(2,1)S(1)}, f32[256,1024]{1,0:T(8,128)S(1)}, bf16[256,512]{1,0:T(8,128)(2,1)S(1)}, bf16[64,2048]{1,0:T(8,128)(2,1)S(...) custom-call(bf16[64,2048]{1,0:T(8,128)(2,1)S(1)} %copy-done.3, ...), custom_call_target="tpu_custom_call" | custom-call | flops 1024 | bytes 1024 | tf_op jit(solution)/shard_map/pallas_call | solution.py:230
  37.0 11.2 %collective-permute-start.6 = (bf16[64,2048]{1,0:T(8,128)(2,1)S(1)}, bf16[64,2048]{1,0:T(8,128)(2,1)S(1)}, u32[]{:S(2)}, u32[]{:S(2)}) collective-permute-start(bf16[64,2048]{1,0:T(8,128)(2,1)S(1)} %get-tuple-element.80.refs_3_), channel_id=1, source_target_pairs={{0,1},{1,2},{2,3},{3,0},{4,5},{5,6},{6,7},{7,4},{8,9},{9,10},{10,1... | collective-permute-start | bytes 786440 | tf_op jit(solution)/shard_map/ppermute | solution.py:567
  48.2 0.0 collective-permute-done.3.refs_1_
  48.2 0.7 collective-permute-done.4.refs_2_
  48.9 2.7 %collective-permute-done.5.refs_3_ = bf16[64,2048]{1,0:T(8,128)(2,1)S(1)} collective-permute-done((bf16[64,2048]{1,0:T(8,128)(2,1)}, bf16[64,2048]{1,0:T(8,128)(2,1)S(1)}, u32[]{:S(2)}, u32[]{:S(2)}) %collective-permute-start.5) | collective-permute-done | bytes 262176 | tf_op jit(solution)/shard_map/ppermute | solution.py:567
  51.7 3.6 %shard_map.96 = (bf16[256,1024]{1,0:T(8,128)(2,1)S(1)}, bf16[2048,256]{1,0:T(8,128)(2,1)S(1)}, bf16[8,256,768]{2,1,0:T(8,128)(2,1)S(1)}, bf16[2048,1024]{1,0:T(8,128)(2,1)S(1)}) custom-call(s32[8]{0:T(128)S(1)} %stack.23.at, f32[256,1024]{1,0:T(8,128)S(1)} %get-tuple-element.58.preact_hbm, bf16[2048,1024]{1,0:T(8,128)(2,1)S(1)} %bitcast.12, ...), custom_call_target="tpu_custom_call" | custom-call | flops 1024 | bytes 1024 | tf_op jit(solution)/shard_map/pallas_call | solution.py:332
  55.3 0.6 collective-permute-start.7
  55.8 1.4 %shard_map.97 = (bf16[128,2048]{1,0:T(8,128)(2,1)S(1)}, bf16[128,2048]{1,0:T(8,128)(2,1)S(1)}, bf16[128,2048]{1,0:T(8,128)(2,1)S(1)}, bf16[64,2048]{1,0:T(8,128)(2,1)S(1)}) custom-call(bf16[256,1024]{1,0:T(8,128)(2,1)S(1)} %get-tuple-element.75.pre_grad, bf16[2048,1024]{1,0:T(8,128)(2,1)S(1)} %get-tuple-element.76.w_in, ...), custom_call_target="tpu_custom_call" | custom-call | flops 1024 | bytes 1024 | tf_op jit(solution)/shard_map/pallas_call | solution.py:306
  57.2 0.2 collective-permute-start.10
  57.4 2.4 %collective-permute-start.13 = (bf16[128,2048]{1,0:T(8,128)(2,1)S(1)}, bf16[128,2048]{1,0:T(8,128)(2,1)S(1)}, u32[]{:S(2)}, u32[]{:S(2)}) collective-permute-start(bf16[128,2048]{1,0:T(8,128)(2,1)S(1)} %get-tuple-element.99), channel_id=1, source_target_pairs={{0,2},{1,3},{2,0},{3,1},{4,6},{5,7},{6,4},{7,5},{8,10},{9,11},{10,... | collective-permute-start | bytes 1572872 | tf_op jit(solution)/shard_map/ppermute | solution.py:567
  59.8 1.4 %collective-permute-start.14 = (bf16[128,2048]{1,0:T(8,128)(2,1)S(1)}, bf16[128,2048]{1,0:T(8,128)(2,1)S(1)}, u32[]{:S(2)}, u32[]{:S(2)}) collective-permute-start(bf16[128,2048]{1,0:T(8,128)(2,1)S(1)} %get-tuple-element.100), channel_id=1, source_target_pairs={{0,3},{1,0},{2,1},{3,2},{4,7},{5,4},{6,5},{7,6},{8,11},{9,8},{10,9... | collective-permute-start | bytes 1572872 | tf_op jit(solution)/shard_map/ppermute | solution.py:567
  61.2 1.1 %shard_map.98.kept = bf16[4,256,768]{2,1,0:T(8,128)(2,1)S(1)} custom-call(s32[4]{0:T(128)S(1)} %get-tuple-element.82.at, bf16[2048,256]{1,0:T(8,128)(2,1)S(1)} %get-tuple-element.59.rows_t, bf16[2048,256]{1,0:T(8,128)(2,1)S(1)} %get-tuple-element.83.grads_t, bf16[256,1024]{1,0:T(8,128)(2,1)S(1)} %get-tuple-element.75.pre_grad, ...), custom_call_target="tpu_custom_call" | custom-call | flops 40000000000 | bytes 1024 | tf_op jit(solution)/shard_map/pallas_call | solution.py:359
  62.3 0.0 collective-permute-done.7.got
  62.3 0.4 shard_map.100
  62.7 0.3 collective-permute-start.8
  63.0 0.0 collective-permute-done.6.refs_1_
  63.0 1.2 %collective-permute-start.9 = (bf16[2,256,768]{2,1,0:T(8,128)(2,1)S(1)}, bf16[2,256,768]{2,1,0:T(8,128)(2,1)S(1)}, u32[]{:S(2)}, u32[]{:S(2)}) collective-permute-start(bf16[2,256,768]{2,1,0:T(8,128)(2,1)S(1)} %get-tuple-element.86), channel_id=1, source_target_pairs={{0,16},{4,20},{8,24},{12,28},{16,0},{20,4},{24,8},{28,12},{1,17},{... | collective-permute-start | bytes 2359304 | tf_op jit(solution)/shard_map/ppermute | solution.py:395
  64.3 1.1 %shard_map.99.kept = bf16[4,256,768]{2,1,0:T(8,128)(2,1)S(1)} custom-call(s32[4]{0:T(128)S(1)} %get-tuple-element.84.at, bf16[2048,256]{1,0:T(8,128)(2,1)S(1)} %get-tuple-element.59.rows_t, bf16[2048,256]{1,0:T(8,128)(2,1)S(1)} %get-tuple-element.83.grads_t, bf16[256,1024]{1,0:T(8,128)(2,1)S(1)} %get-tuple-element.75.pre_grad, ...), custom_call_target="tpu_custom_call" | custom-call | flops 40000000000 | bytes 1024 | tf_op jit(solution)/shard_map/pallas_call | solution.py:359
  65.4 15.6 %collective-permute-done.8.left_in = bf16[2,256,768]{2,1,0:T(8,128)(2,1)S(1)} collective-permute-done((bf16[2,256,768]{2,1,0:T(8,128)(2,1)S(1)}, bf16[2,256,768]{2,1,0:T(8,128)(2,1)S(1)}, u32[]{:S(2)}, u32[]{:S(2)}) %collective-permute-start.8) | collective-permute-done | bytes 786464 | tf_op jit(solution)/shard_map/ppermute | solution.py:395
  81.0 0.0 collective-permute-done.9.right_in
  81.0 0.3 shard_map.103
  81.2 1.3 %collective-permute-start.11 = (bf16[256,768]{1,0:T(8,128)(2,1)S(1)}, bf16[256,768]{1,0:T(8,128)(2,1)S(1)}, u32[]{:S(2)}, u32[]{:S(2)}) collective-permute-start(bf16[256,768]{1,0:T(8,128)(2,1)S(1)} %get-tuple-element.91), channel_id=1, source_target_pairs={{0,16},{4,20},{8,24},{12,28},{16,0},{20,4},{24,8},{28,12},{1,17},{... | collective-permute-start | bytes 1179656 | tf_op jit(solution)/shard_map/ppermute | solution.py:395
  82.6 1.2 %collective-permute-start.12 = (bf16[256,768]{1,0:T(8,128)(2,1)S(1)}, bf16[256,768]{1,0:T(8,128)(2,1)S(1)}, u32[]{:S(2)}, u32[]{:S(2)}) collective-permute-start(bf16[256,768]{1,0:T(8,128)(2,1)S(1)} %get-tuple-element.93), channel_id=1, source_target_pairs={{0,8},{4,12},{8,0},{12,4},{16,24},{20,28},{24,16},{28,20},{1,9},{5... | collective-permute-start | bytes 1179656 | tf_op jit(solution)/shard_map/ppermute | solution.py:395
  83.7 0.3 shard_map.101
  84.0 0.0 collective-permute-done.10.refs_2_
  84.0 0.0 copy-done.4
  84.0 0.8 shard_map.102
  84.8 5.1 %collective-permute-done.11.left_last = bf16[256,768]{1,0:T(8,128)(2,1)S(1)} collective-permute-done((bf16[256,768]{1,0:T(8,128)(2,1)S(1)}, bf16[256,768]{1,0:T(8,128)(2,1)S(1)}, u32[]{:S(2)}, u32[]{:S(2)}) %collective-permute-start.11) | collective-permute-done | bytes 393248 | tf_op jit(solution)/shard_map/ppermute | solution.py:395
  89.9 1.0 collective-permute-done.12.right_last
  90.9 1.3 %shard_map.104 = (f32[256,1024]{1,0:T(8,128)}, f32[256,512]{1,0:T(8,128)}) custom-call(f32[256,768]{1,0:T(8,128)S(1)} %get-tuple-element.87.left, bf16[256,768]{1,0:T(8,128)(2,1)S(1)} %collective-permute-done.11.left_last, f32[256,768]{1,0:T(8,128)S(1)} %get-tuple-element.92.right, bf16[256,768]{1,0:T(8,128)(2,1)S(1)} %collective-permute-done.12.right_last), custom_call_target="tpu_custom_call" | custom-call | flops 1024 | bytes 1024 | tf_op jit(solution)/shard_map/pallas_call | solution.py:469
  92.1 4.7 %collective-permute-done.13.refs_0_ = bf16[128,2048]{1,0:T(8,128)(2,1)S(1)} collective-permute-done((bf16[128,2048]{1,0:T(8,128)(2,1)S(1)}, bf16[128,2048]{1,0:T(8,128)(2,1)S(1)}, u32[]{:S(2)}, u32[]{:S(2)}) %collective-permute-start.13) | collective-permute-done | bytes 524320 | tf_op jit(solution)/shard_map/ppermute | solution.py:567
  96.9 3.4 %collective-permute-done.14.refs_1_ = bf16[128,2048]{1,0:T(8,128)(2,1)S(1)} collective-permute-done((bf16[128,2048]{1,0:T(8,128)(2,1)S(1)}, bf16[128,2048]{1,0:T(8,128)(2,1)S(1)}, u32[]{:S(2)}, u32[]{:S(2)}) %collective-permute-start.14) | collective-permute-done | bytes 524320 | tf_op jit(solution)/shard_map/ppermute | solution.py:567
  100.3 1.3 %shard_map.105 = (bf16[128,2048]{1,0:T(8,128)(2,1)}, bf16[128,2048]{1,0:T(8,128)(2,1)}) custom-call(bf16[384,128]{1,0:T(8,128)(2,1)S(1)} %get-tuple-element.95.picker, f32[2,128,128]{2,1,0:T(8,128)S(1)} %get-tuple-element.96.scales, f32[128,2048]{1,0:T(8,128)S(1)} %get-tuple-element.97.mixed_part, f32[128,2048]{1,0:T(8,128)S(1)} %get-tuple-element.98.back_part, ...), custom_call_target="tpu_custom_call" | custom-call | flops 1024 | bytes 1024 | tf_op jit(solution)/shard_map/pallas_call | solution.py:507
  (10 shorter events, 0.0 us)
Async XLA Ops:
  3.0 7.4 %collective-permute-start = (bf16[64,2048]{1,0:T(8,128)(2,1)}, bf16[64,2048]{1,0:T(8,128)(2,1)S(1)}, u32[]{:S(2)}, u32[]{:S(2)}) collective-permute-start(bf16[64,2048]{1,0:T(8,128)(2,1)} %get-tuple-element.55), channel_id=1, source_target_pairs={{0,1},{1,2},{2,3},{3,0},{4,5},{5,6},{6,7},{7,4},{8,9},{9,10},{10,1... | collective-permute-start | bytes 786440 | tf_op jit(solution)/shard_map/ppermute | solution.py:567
  4.3 14.5 %collective-permute-start.2 = (bf16[64,2048]{1,0:T(8,128)(2,1)}, bf16[64,2048]{1,0:T(8,128)(2,1)S(1)}, u32[]{:S(2)}, u32[]{:S(2)}) collective-permute-start(bf16[64,2048]{1,0:T(8,128)(2,1)} %get-tuple-element.57), channel_id=1, source_target_pairs={{0,3},{1,0},{2,1},{3,2},{4,7},{5,4},{6,5},{7,6},{8,11},{9,8},{10,9... | collective-permute-start | bytes 786440 | tf_op jit(solution)/shard_map/ppermute | solution.py:567
  4.5 24.2 %collective-permute-start.1 = (bf16[64,2048]{1,0:T(8,128)(2,1)}, bf16[64,2048]{1,0:T(8,128)(2,1)S(1)}, u32[]{:S(2)}, u32[]{:S(2)}) collective-permute-start(bf16[64,2048]{1,0:T(8,128)(2,1)} %get-tuple-element.56), channel_id=1, source_target_pairs={{0,2},{1,3},{2,0},{3,1},{4,6},{5,7},{6,4},{7,5},{8,10},{9,11},{10,... | collective-permute-start | bytes 786440 | tf_op jit(solution)/shard_map/ppermute | solution.py:567
  18.9 29.3 %collective-permute-start.3 = (bf16[64,2048]{1,0:T(8,128)(2,1)}, bf16[64,2048]{1,0:T(8,128)(2,1)S(1)}, u32[]{:S(2)}, u32[]{:S(2)}) collective-permute-start(bf16[64,2048]{1,0:T(8,128)(2,1)} %get-tuple-element.66), channel_id=1, source_target_pairs={{0,1},{1,2},{2,3},{3,0},{4,5},{5,6},{6,7},{7,4},{8,9},{9,10},{10,1... | collective-permute-start | bytes 786440 | tf_op jit(solution)/shard_map/ppermute | solution.py:567
  18.9 30.1 %collective-permute-start.4 = (bf16[64,2048]{1,0:T(8,128)(2,1)}, bf16[64,2048]{1,0:T(8,128)(2,1)S(1)}, u32[]{:S(2)}, u32[]{:S(2)}) collective-permute-start(bf16[64,2048]{1,0:T(8,128)(2,1)} %get-tuple-element.67), channel_id=1, source_target_pairs={{0,2},{1,3},{2,0},{3,1},{4,6},{5,7},{6,4},{7,5},{8,10},{9,11},{10,... | collective-permute-start | bytes 786440 | tf_op jit(solution)/shard_map/ppermute | solution.py:567
  20.0 31.7 %collective-permute-start.5 = (bf16[64,2048]{1,0:T(8,128)(2,1)}, bf16[64,2048]{1,0:T(8,128)(2,1)S(1)}, u32[]{:S(2)}, u32[]{:S(2)}) collective-permute-start(bf16[64,2048]{1,0:T(8,128)(2,1)} %get-tuple-element.68), channel_id=1, source_target_pairs={{0,3},{1,0},{2,1},{3,2},{4,7},{5,4},{6,5},{7,6},{8,11},{9,8},{10,9... | collective-permute-start | bytes 786440 | tf_op jit(solution)/shard_map/ppermute | solution.py:567
  28.7 1.6 %copy-start.1 = (bf16[1,2048,512]{2,1,0:T(8,128)(2,1)S(1)}, bf16[1,2048,512]{2,1,0:T(8,128)(2,1)}, u32[]{:S(2)}) copy-start(bf16[1,2048,512]{2,1,0:T(8,128)(2,1)} %param.11) | copy-start | bytes 6291460
  30.3 0.9 copy-start.3
  31.2 20.5 %copy-start = (bf16[1,2048,1024]{2,1,0:T(8,128)(2,1)S(1)}, bf16[1,2048,1024]{2,1,0:T(8,128)(2,1)}, u32[]{:S(2)}) copy-start(bf16[1,2048,1024]{2,1,0:T(8,128)(2,1)} %param.10) | copy-start | bytes 12582916
  31.2 20.5 %copy-start.2 = (bf16[64,2048]{1,0:T(8,128)(2,1)S(1)}, bf16[64,2048]{1,0:T(8,128)(2,1)}, u32[]{:S(2)}) copy-start(bf16[64,2048]{1,0:T(8,128)(2,1)} %get-tuple-element.69.refs_0_) | copy-start | bytes 786436
  37.0 26.0 %collective-permute-start.6 = (bf16[64,2048]{1,0:T(8,128)(2,1)S(1)}, bf16[64,2048]{1,0:T(8,128)(2,1)S(1)}, u32[]{:S(2)}, u32[]{:S(2)}) collective-permute-start(bf16[64,2048]{1,0:T(8,128)(2,1)S(1)} %get-tuple-element.80.refs_3_), channel_id=1, source_target_pairs={{0,1},{1,2},{2,3},{3,0},{4,5},{5,6},{6,7},{7,4},{8,9},{9,10},{10,1... | collective-permute-start | bytes 786440 | tf_op jit(solution)/shard_map/ppermute | solution.py:567
  55.3 7.0 %collective-permute-start.7 = (bf16[8,256,768]{2,1,0:T(8,128)(2,1)S(1)}, bf16[8,256,768]{2,1,0:T(8,128)(2,1)S(1)}, u32[]{:S(2)}, u32[]{:S(2)}) collective-permute-start(bf16[8,256,768]{2,1,0:T(8,128)(2,1)S(1)} %get-tuple-element.74), channel_id=1, source_target_pairs={{0,4},{4,0},{8,12},{12,8},{16,20},{20,16},{24,28},{28,24},{1,5},{5... | collective-permute-start | bytes 9437192 | tf_op jit(solution)/shard_map/ppermute | solution.py:395
  57.2 26.8 %collective-permute-start.10 = (bf16[64,2048]{1,0:T(8,128)(2,1)S(1)}, bf16[64,2048]{1,0:T(8,128)(2,1)S(1)}, u32[]{:S(2)}, u32[]{:S(2)}) collective-permute-start(bf16[64,2048]{1,0:T(8,128)(2,1)S(1)} %get-tuple-element.89), channel_id=1, source_target_pairs={{0,1},{1,2},{2,3},{3,0},{4,5},{5,6},{6,7},{7,4},{8,9},{9,10},{10,1... | collective-permute-start | bytes 786440 | tf_op jit(solution)/shard_map/ppermute | solution.py:567
  57.4 39.4 %collective-permute-start.13 = (bf16[128,2048]{1,0:T(8,128)(2,1)S(1)}, bf16[128,2048]{1,0:T(8,128)(2,1)S(1)}, u32[]{:S(2)}, u32[]{:S(2)}) collective-permute-start(bf16[128,2048]{1,0:T(8,128)(2,1)S(1)} %get-tuple-element.99), channel_id=1, source_target_pairs={{0,2},{1,3},{2,0},{3,1},{4,6},{5,7},{6,4},{7,5},{8,10},{9,11},{10,... | collective-permute-start | bytes 1572872 | tf_op jit(solution)/shard_map/ppermute | solution.py:567
  59.8 40.5 %collective-permute-start.14 = (bf16[128,2048]{1,0:T(8,128)(2,1)S(1)}, bf16[128,2048]{1,0:T(8,128)(2,1)S(1)}, u32[]{:S(2)}, u32[]{:S(2)}) collective-permute-start(bf16[128,2048]{1,0:T(8,128)(2,1)S(1)} %get-tuple-element.100), channel_id=1, source_target_pairs={{0,3},{1,0},{2,1},{3,2},{4,7},{5,4},{6,5},{7,6},{8,11},{9,8},{10,9... | collective-permute-start | bytes 1572872 | tf_op jit(solution)/shard_map/ppermute | solution.py:567
  62.7 18.3 %collective-permute-start.8 = (bf16[2,256,768]{2,1,0:T(8,128)(2,1)S(1)}, bf16[2,256,768]{2,1,0:T(8,128)(2,1)S(1)}, u32[]{:S(2)}, u32[]{:S(2)}) collective-permute-start(bf16[2,256,768]{2,1,0:T(8,128)(2,1)S(1)} %get-tuple-element.85), channel_id=1, source_target_pairs={{0,8},{4,12},{8,0},{12,4},{16,24},{20,28},{24,16},{28,20},{1,9},{5... | collective-permute-start | bytes 2359304 | tf_op jit(solution)/shard_map/ppermute | solution.py:395
  63.0 17.9 %collective-permute-start.9 = (bf16[2,256,768]{2,1,0:T(8,128)(2,1)S(1)}, bf16[2,256,768]{2,1,0:T(8,128)(2,1)S(1)}, u32[]{:S(2)}, u32[]{:S(2)}) collective-permute-start(bf16[2,256,768]{2,1,0:T(8,128)(2,1)S(1)} %get-tuple-element.86), channel_id=1, source_target_pairs={{0,16},{4,20},{8,24},{12,28},{16,0},{20,4},{24,8},{28,12},{1,17},{... | collective-permute-start | bytes 2359304 | tf_op jit(solution)/shard_map/ppermute | solution.py:395
  81.2 8.6 %collective-permute-start.11 = (bf16[256,768]{1,0:T(8,128)(2,1)S(1)}, bf16[256,768]{1,0:T(8,128)(2,1)S(1)}, u32[]{:S(2)}, u32[]{:S(2)}) collective-permute-start(bf16[256,768]{1,0:T(8,128)(2,1)S(1)} %get-tuple-element.91), channel_id=1, source_target_pairs={{0,16},{4,20},{8,24},{12,28},{16,0},{20,4},{24,8},{28,12},{1,17},{... | collective-permute-start | bytes 1179656 | tf_op jit(solution)/shard_map/ppermute | solution.py:395
  82.6 1.4 %copy-start.4 = (s32[128,2]{0,1:T(2,128)S(1)}, s32[128,2]{0,1:T(2,128)}, u32[]{:S(2)}) copy-start(s32[128,2]{0,1:T(2,128)} %param.7) | copy-start | bytes 3076
  82.6 1.4 %copy-start.5 = (f32[128,2]{0,1:T(2,128)S(1)}, f32[128,2]{0,1:T(2,128)}, u32[]{:S(2)}) copy-start(f32[128,2]{0,1:T(2,128)} %param.8) | copy-start | bytes 3076
  82.6 8.3 %collective-permute-start.12 = (bf16[256,768]{1,0:T(8,128)(2,1)S(1)}, bf16[256,768]{1,0:T(8,128)(2,1)S(1)}, u32[]{:S(2)}, u32[]{:S(2)}) collective-permute-start(bf16[256,768]{1,0:T(8,128)(2,1)S(1)} %get-tuple-element.93), channel_id=1, source_target_pairs={{0,8},{4,12},{8,0},{12,4},{16,24},{20,28},{24,16},{28,20},{1,9},{5... | collective-permute-start | bytes 1179656 | tf_op jit(solution)/shard_map/ppermute | solution.py:395
where the time goes:
time: 102 us
  waiting for transfers between devices  51.1 us (50%)
  starting transfers between devices  25.1 us (25%)
  Pallas kernels  22 us (22%)
  local copies, waits for them, and re-layouts  2.72 us (3%)
    ppermute x10, waiting for transfers between devices, travel(): return lax.ppermute(block, 'expert', pairs)  29.5 us
    ppermute x5, waiting for transfers between devices, swap(): lax.ppermute(block, 'dp', [(at, at ^ bit) for at in range(lax.axis_size('...  21.6 us
    ppermute x10, starting transfers between devices, travel(): return lax.ppermute(block, 'expert', pairs)  20.5 us
    pallas_call x1, Pallas kernels, forward(): pl.pallas_call(functools.partial(forward_kernel, count), out_shape=(jax.S...  5.76 us
    pallas_call x2, Pallas kernels, dispatch(): pl.pallas_call(functools.partial(dispatch_kernel, experts, capacity, weig...  4.73 us
    ppermute x5, starting transfers between devices, swap(): lax.ppermute(block, 'dp', [(at, at ^ bit) for at in range(lax.axis_size('...  4.59 us
    pallas_call x1, Pallas kernels, backward(): pl.pallas_call(functools.partial(backward_kernel, count), out_shape=(jax....  3.57 us
    unnamed x12, local copies, waits for them, and re-layouts  2.55 us
  transfers between devices with their start and end apart: 15, of which 10 were waited for; matrix products, arithmetic and copies ran while one was open for 0% of the time, Pallas kernels for 18%

commit v1 on v0

--- a/solution.py
+++ b/solution.py
@@ -160,10 +160,8 @@
     width = rows.shape[1]
     step = 256 if width % 256 == 0 else width
 
-    @pl.loop(0, width // step)
-    def _(c):
-        own = pl.ds(pl.multiple_of(c * step, step), step)
-        rows_t[own, :] = rows[:, own].T
+    for begin in range(0, width, step):
+        rows_t[begin : begin + step, :] = rows[:, begin : begin + step].T
 
 
 def join_copies(blocks, rows, sems):
@@ -423,7 +421,7 @@
 
 
 def partial_kernel(experts, capacity, alone, late, first, routes, scores, *refs):
-    (own, early, back_early), (mixed, back, late_picker, scales) = refs[:-4], refs[-4:]
+    own, early, mixed, back, late_picker, scales = refs
     slots, toks = experts * capacity, mixed.shape[0]
     places = lax.broadcasted_iota(jnp.int32, (toks, slots), 1).astype(F32)
     hits = [
@@ -439,21 +437,22 @@
         parts = [picker[:, n * capacity : (n + 1) * capacity] for n in blocks]
         return jnp.concatenate(parts, axis=1)
 
-    late_picker[...] = slots_of(late)
+    late_picker[...] = slots_of(late + [alone])
     now = slots_of((0, alone))
     for columns in column_steps(mixed.shape[1]):
         outputs = jnp.concatenate([own[:capacity, columns], early[:, columns]], axis=0)
-        gradients = jnp.concatenate([own[capacity:, columns], back_early[:, columns]], axis=0)
-        total, grad = sum_rows(now, scales, outputs, gradients)
+        total, grad = sum_rows(now, scales, outputs, own[capacity:, columns])
         mixed[:, columns] = total
         back[:, columns] = grad
 
 
 def sum_rows(picker, scales, outputs, gradients):
     tops, toks = scales.shape[:2]
-    picked = jnp.dot(picker[: tops * toks], outputs, preferred_element_type=F32)
+    chosen = picker[: tops * toks, : outputs.shape[0]]
+    picked = jnp.dot(chosen, outputs, preferred_element_type=F32)
     total = sum(scales[k, :, :1] * picked[k * toks : (k + 1) * toks] for k in range(tops))
-    return total, jnp.dot(picker[tops * toks :], gradients, preferred_element_type=F32)
+    either = picker[tops * toks :, : gradients.shape[0]]
+    return total, jnp.dot(either, gradients, preferred_element_type=F32)
 
 
 def mean_kernel(count, left, left_last, right, right_last, wide, narrow):
@@ -487,8 +486,10 @@
     )
     stores = []
     for c, columns in enumerate(column_steps(mixed.shape[1])):
-        outputs = jnp.concatenate([block[:capacity, columns] for block in blocks], axis=0)
-        gradients = jnp.concatenate([block[capacity:, columns] for block in blocks], axis=0)
+        outputs = jnp.concatenate([block[:capacity, columns] for block in blocks[:-1]], axis=0)
+        gradients = jnp.concatenate(
+            [block[block.shape[0] - capacity :, columns] for block in blocks], axis=0
+        )
         total, grad = sum_rows(picker[...], scales, outputs, gradients)
         mixed_vmem[:, columns] = (total + mixed_part[:, columns]).astype(BF16)
         back_vmem[:, columns] = (grad + back_part[:, columns]).astype(BF16)
@@ -602,9 +603,9 @@
         operands = (share, rows_t, grads_t, pre_grad, hidden)
         got = swap(sent, 1)
         blocks = returns(after(pre_grad, sent), w_in_here, produced, early)
-        returned = exchange(blocks, -1)
         half = len(CUBE_SEND) // 2
         kept_first = shares(after(keep_at[:half], blocks[0]), *operands, COVER)
+        returned = exchange(blocks, -1)
         kept_later = shares(after(keep_at[half:], kept_first, early_out, got), *operands, COVER)
         sums = cube_sum(got, kept_first, kept_later)
         late = [n for n in range(experts - 1, 0, -1) if n != early]
@@ -613,14 +614,14 @@
             (
                 jax.ShapeDtypeStruct((toks, width), F32),
                 jax.ShapeDtypeStruct((toks, width), F32),
-                jax.ShapeDtypeStruct(((tops + 1) * toks, len(late) * capacity), BF16),
+                jax.ShapeDtypeStruct(((tops + 1) * toks, (len(late) + 1) * capacity), BF16),
                 jax.ShapeDtypeStruct((tops, toks, 128), F32),
             ),
-            (after(first, sums[0]), routes_t, scores_t, returned[0], early_out, returned[early]),
+            (after(first, sums[0]), routes_t, scores_t, returned[0], early_out),
         )
         grad_in, grad_down = means(groups, sums)
         parts = (after(picker, grad_in), scales, mixed_part, back_part)
-        mixed_out, token_grad = last(capacity, parts, [returned[n] for n in late])
+        mixed_out, token_grad = last(capacity, parts, [returned[n] for n in late + [early]])
     else:
         token_rows = joined(got_rows)
         grad_rows = joined(exchange(sent_grads, 1))

time: 102 us -> 99.2 us (0.973)
  Pallas kernels: 22 us -> 20.5 us
  waiting for transfers between devices: 51.1 us -> 49.8 us
    ppermute x10, waiting for transfers between devices: 29.5 us -> 28.1 us  [travel(): return lax.ppermute(block, 'expert', pairs)]
  transfers between devices with their start and end apart: 15 -> 15, of which waited for: 10 -> 10; matrix products, arithmetic and copies ran while one was open for 0% -> 0% of each run, Pallas kernels for 18% -> 17%
where the time goes in v1:
time: 99.2 us; the launch traced here: 98.9 us
  waiting for transfers between devices  49.8 us (50%)
  starting transfers between devices  25.1 us (25%)
  Pallas kernels  20.5 us (21%)
  local copies, waits for them, and re-layouts  2.72 us (3%)
    ppermute x10, waiting for transfers between devices, travel(): return lax.ppermute(block, 'expert', pairs)  28.1 us
    ppermute x5, waiting for transfers between devices, swap(): lax.ppermute(block, 'dp', [(at, at ^ bit) for at in range(lax.axis_size('...  21.6 us
    ppermute x10, starting transfers between devices, travel(): return lax.ppermute(block, 'expert', pairs)  20.5 us
    pallas_call x1, Pallas kernels, forward(): pl.pallas_call(functools.partial(forward_kernel, count), out_shape=(jax.S...  5.04 us
    pallas_call x2, Pallas kernels, dispatch(): pl.pallas_call(functools.partial(dispatch_kernel, experts, capacity, weig...  4.73 us
    ppermute x5, starting transfers between devices, swap(): lax.ppermute(block, 'dp', [(at, at ^ bit) for at in range(lax.axis_size('...  4.58 us
    pallas_call x1, Pallas kernels, backward(): pl.pallas_call(functools.partial(backward_kernel, count), out_shape=(jax....  2.85 us
    unnamed x12, local copies, waits for them, and re-layouts  2.55 us
  transfers between devices with their start and end apart: 15, of which 10 were waited for; matrix products, arithmetic and copies ran while one was open for 0% of the time, Pallas kernels for 17%

profile of v1, /device:TPU:11, one launch (start us, length us, event | category | flops | bytes accessed | tf_op | source)
XLA Modules:
  0.0 98.9 jit_solution(15369340234448110634)
XLA Ops:
  0.6 2.3 %shard_map.93 = (bf16[64,2048]{1,0:T(8,128)(2,1)}, bf16[64,2048]{1,0:T(8,128)(2,1)}, bf16[64,2048]{1,0:T(8,128)(2,1)}, bf16[64,2048]{1,0:T(8,128)(2,1)}) custom-call(s32[1]{0:T(128)} %bitcast.first, s32[2,128]{1,0:T(2,128)} %bitcast.15, bf16[128,2048]{1,0:T(8,128)(2,1)} %refs_1_.1), custom_call_target="tpu_custom_call" | custom-call | flops 1024 | bytes 1024 | tf_op jit(solution)/shard_map/pallas_call | solution.py:522
  3.0 1.3 %collective-permute-start = (bf16[64,2048]{1,0:T(8,128)(2,1)}, bf16[64,2048]{1,0:T(8,128)(2,1)S(1)}, u32[]{:S(2)}, u32[]{:S(2)}) collective-permute-start(bf16[64,2048]{1,0:T(8,128)(2,1)} %get-tuple-element.55), channel_id=1, source_target_pairs={{0,1},{1,2},{2,3},{3,0},{4,5},{5,6},{6,7},{7,4},{8,9},{9,10},{10,1... | collective-permute-start | bytes 786440 | tf_op jit(solution)/shard_map/ppermute | solution.py:568
  4.3 0.2 collective-permute-start.2
  4.5 2.3 %collective-permute-start.1 = (bf16[64,2048]{1,0:T(8,128)(2,1)}, bf16[64,2048]{1,0:T(8,128)(2,1)S(1)}, u32[]{:S(2)}, u32[]{:S(2)}) collective-permute-start(bf16[64,2048]{1,0:T(8,128)(2,1)} %get-tuple-element.56), channel_id=1, source_target_pairs={{0,2},{1,3},{2,0},{3,1},{4,6},{5,7},{6,4},{7,5},{8,10},{9,11},{10,... | collective-permute-start | bytes 786440 | tf_op jit(solution)/shard_map/ppermute | solution.py:568
  6.8 2.4 %shard_map.95 = (bf16[64,2048]{1,0:T(8,128)(2,1)}, bf16[64,2048]{1,0:T(8,128)(2,1)}, bf16[64,2048]{1,0:T(8,128)(2,1)}, bf16[64,2048]{1,0:T(8,128)(2,1)}) custom-call(s32[1]{0:T(128)} %bitcast.first, s32[2,128]{1,0:T(2,128)} %bitcast.16, f32[2,128]{1,0:T(2,128)} %bitcast.18, bf16[128,2048]{1,0:T(8,128)(2,1)} %refs_2_.1), custom_call_target="tpu_custom_call" | custom-call | flops 1024 | bytes 1024 | tf_op jit(solution)/shard_map/pallas_call | solution.py:522
  9.2 0.1 stack.23.at
  9.3 1.1 %collective-permute-done.refs_1_ = bf16[64,2048]{1,0:T(8,128)(2,1)S(1)} collective-permute-done((bf16[64,2048]{1,0:T(8,128)(2,1)}, bf16[64,2048]{1,0:T(8,128)(2,1)S(1)}, u32[]{:S(2)}, u32[]{:S(2)}) %collective-permute-start) | collective-permute-done | bytes 262176 | tf_op jit(solution)/shard_map/ppermute | solution.py:568
  10.4 8.5 %collective-permute-done.2.refs_3_ = bf16[64,2048]{1,0:T(8,128)(2,1)S(1)} collective-permute-done((bf16[64,2048]{1,0:T(8,128)(2,1)}, bf16[64,2048]{1,0:T(8,128)(2,1)S(1)}, u32[]{:S(2)}, u32[]{:S(2)}) %collective-permute-start.2) | collective-permute-done | bytes 262176 | tf_op jit(solution)/shard_map/ppermute | solution.py:568
  18.9 0.0 collective-permute-start.3
  18.9 1.1 %collective-permute-start.4 = (bf16[64,2048]{1,0:T(8,128)(2,1)}, bf16[64,2048]{1,0:T(8,128)(2,1)S(1)}, u32[]{:S(2)}, u32[]{:S(2)}) collective-permute-start(bf16[64,2048]{1,0:T(8,128)(2,1)} %get-tuple-element.67), channel_id=1, source_target_pairs={{0,2},{1,3},{2,0},{3,1},{4,6},{5,7},{6,4},{7,5},{8,10},{9,11},{10,... | collective-permute-start | bytes 786440 | tf_op jit(solution)/shard_map/ppermute | solution.py:568
  20.0 0.3 collective-permute-start.5
  20.3 0.1 fusion
  20.4 8.3 %collective-permute-done.1.refs_2_ = bf16[64,2048]{1,0:T(8,128)(2,1)S(1)} collective-permute-done((bf16[64,2048]{1,0:T(8,128)(2,1)}, bf16[64,2048]{1,0:T(8,128)(2,1)S(1)}, u32[]{:S(2)}, u32[]{:S(2)}) %collective-permute-start.1) | collective-permute-done | bytes 262176 | tf_op jit(solution)/shard_map/ppermute | solution.py:568
  28.7 1.6 %copy-done.1 = bf16[1,2048,512]{2,1,0:T(8,128)(2,1)S(1)} copy-done((bf16[1,2048,512]{2,1,0:T(8,128)(2,1)S(1)}, bf16[1,2048,512]{2,1,0:T(8,128)(2,1)}, u32[]{:S(2)}) %copy-start.1) | copy-done | bytes 2097176
  30.3 0.9 copy-done.3
  31.2 5.0 %shard_map.94 = (bf16[2048,256]{1,0:T(8,128)(2,1)S(1)}, f32[256,1024]{1,0:T(8,128)S(1)}, bf16[256,512]{1,0:T(8,128)(2,1)S(1)}, bf16[64,2048]{1,0:T(8,128)(2,1)S(...) custom-call(bf16[64,2048]{1,0:T(8,128)(2,1)S(1)} %copy-done.3, ...), custom_call_target="tpu_custom_call" | custom-call | flops 1024 | bytes 1024 | tf_op jit(solution)/shard_map/pallas_call | solution.py:228
  36.3 11.2 %collective-permute-start.6 = (bf16[64,2048]{1,0:T(8,128)(2,1)S(1)}, bf16[64,2048]{1,0:T(8,128)(2,1)S(1)}, u32[]{:S(2)}, u32[]{:S(2)}) collective-permute-start(bf16[64,2048]{1,0:T(8,128)(2,1)S(1)} %get-tuple-element.80.refs_3_), channel_id=1, source_target_pairs={{0,1},{1,2},{2,3},{3,0},{4,5},{5,6},{6,7},{7,4},{8,9},{9,10},{10,1... | collective-permute-start | bytes 786440 | tf_op jit(solution)/shard_map/ppermute | solution.py:568
  47.5 0.0 collective-permute-done.3.refs_1_
  47.5 1.5 %collective-permute-done.4.refs_2_ = bf16[64,2048]{1,0:T(8,128)(2,1)S(1)} collective-permute-done((bf16[64,2048]{1,0:T(8,128)(2,1)}, bf16[64,2048]{1,0:T(8,128)(2,1)S(1)}, u32[]{:S(2)}, u32[]{:S(2)}) %collective-permute-start.4) | collective-permute-done | bytes 262176 | tf_op jit(solution)/shard_map/ppermute | solution.py:568
  49.0 2.7 %collective-permute-done.5.refs_3_ = bf16[64,2048]{1,0:T(8,128)(2,1)S(1)} collective-permute-done((bf16[64,2048]{1,0:T(8,128)(2,1)}, bf16[64,2048]{1,0:T(8,128)(2,1)S(1)}, u32[]{:S(2)}, u32[]{:S(2)}) %collective-permute-start.5) | collective-permute-done | bytes 262176 | tf_op jit(solution)/shard_map/ppermute | solution.py:568
  51.7 0.0 copy-done.2
  51.7 2.9 %shard_map.96 = (bf16[256,1024]{1,0:T(8,128)(2,1)S(1)}, bf16[2048,256]{1,0:T(8,128)(2,1)S(1)}, bf16[8,256,768]{2,1,0:T(8,128)(2,1)S(1)}, bf16[2048,1024]{1,0:T(8,128)(2,1)S(1)}) custom-call(s32[8]{0:T(128)S(1)} %stack.23.at, f32[256,1024]{1,0:T(8,128)S(1)} %get-tuple-element.58.preact_hbm, bf16[2048,1024]{1,0:T(8,128)(2,1)S(1)} %bitcast.12, ...), custom_call_target="tpu_custom_call" | custom-call | flops 1024 | bytes 1024 | tf_op jit(solution)/shard_map/pallas_call | solution.py:330
  54.5 0.6 collective-permute-start.7
  55.1 1.4 %shard_map.97 = (bf16[128,2048]{1,0:T(8,128)(2,1)S(1)}, bf16[128,2048]{1,0:T(8,128)(2,1)S(1)}, bf16[128,2048]{1,0:T(8,128)(2,1)S(1)}, bf16[64,2048]{1,0:T(8,128)(2,1)S(1)}) custom-call(bf16[256,1024]{1,0:T(8,128)(2,1)S(1)} %get-tuple-element.75.pre_grad, bf16[2048,1024]{1,0:T(8,128)(2,1)S(1)} %get-tuple-element.76.w_in, ...), custom_call_target="tpu_custom_call" | custom-call | flops 1024 | bytes 1024 | tf_op jit(solution)/shard_map/pallas_call | solution.py:304
  56.5 2.6 %collective-permute-start.12 = (bf16[128,2048]{1,0:T(8,128)(2,1)S(1)}, bf16[128,2048]{1,0:T(8,128)(2,1)S(1)}, u32[]{:S(2)}, u32[]{:S(2)}) collective-permute-start(bf16[128,2048]{1,0:T(8,128)(2,1)S(1)} %get-tuple-element.98), channel_id=1, source_target_pairs={{0,2},{1,3},{2,0},{3,1},{4,6},{5,7},{6,4},{7,5},{8,10},{9,11},{10,... | collective-permute-start | bytes 1572872 | tf_op jit(solution)/shard_map/ppermute | solution.py:568
  59.1 0.0 collective-permute-start.13
  59.1 1.5 %collective-permute-start.14 = (bf16[64,2048]{1,0:T(8,128)(2,1)S(1)}, bf16[64,2048]{1,0:T(8,128)(2,1)S(1)}, u32[]{:S(2)}, u32[]{:S(2)}) collective-permute-start(bf16[64,2048]{1,0:T(8,128)(2,1)S(1)} %get-tuple-element.100), channel_id=1, source_target_pairs={{0,1},{1,2},{2,3},{3,0},{4,5},{5,6},{6,7},{7,4},{8,9},{9,10},{10,1... | collective-permute-start | bytes 786440 | tf_op jit(solution)/shard_map/ppermute | solution.py:568
  60.5 1.1 %shard_map.98.kept = bf16[4,256,768]{2,1,0:T(8,128)(2,1)S(1)} custom-call(s32[4]{0:T(128)S(1)} %get-tuple-element.82.at, bf16[2048,256]{1,0:T(8,128)(2,1)S(1)} %get-tuple-element.59.rows_t, bf16[2048,256]{1,0:T(8,128)(2,1)S(1)} %get-tuple-element.83.grads_t, bf16[256,1024]{1,0:T(8,128)(2,1)S(1)} %get-tuple-element.75.pre_grad, ...), custom_call_target="tpu_custom_call" | custom-call | flops 40000000000 | bytes 1024 | tf_op jit(solution)/shard_map/pallas_call | solution.py:357
  61.7 0.0 collective-permute-done.7.got
  61.7 0.4 shard_map.100
  62.0 0.3 collective-permute-start.8
  62.4 0.0 collective-permute-done.6.refs_1_
  62.4 1.2 %collective-permute-start.9 = (bf16[2,256,768]{2,1,0:T(8,128)(2,1)S(1)}, bf16[2,256,768]{2,1,0:T(8,128)(2,1)S(1)}, u32[]{:S(2)}, u32[]{:S(2)}) collective-permute-start(bf16[2,256,768]{2,1,0:T(8,128)(2,1)S(1)} %get-tuple-element.86), channel_id=1, source_target_pairs={{0,16},{4,20},{8,24},{12,28},{16,0},{20,4},{24,8},{28,12},{1,17},{... | collective-permute-start | bytes 2359304 | tf_op jit(solution)/shard_map/ppermute | solution.py:393
  63.6 1.1 %shard_map.99.kept = bf16[4,256,768]{2,1,0:T(8,128)(2,1)S(1)} custom-call(s32[4]{0:T(128)S(1)} %get-tuple-element.84.at, bf16[2048,256]{1,0:T(8,128)(2,1)S(1)} %get-tuple-element.59.rows_t, bf16[2048,256]{1,0:T(8,128)(2,1)S(1)} %get-tuple-element.83.grads_t, bf16[256,1024]{1,0:T(8,128)(2,1)S(1)} %get-tuple-element.75.pre_grad, ...), custom_call_target="tpu_custom_call" | custom-call | flops 40000000000 | bytes 1024 | tf_op jit(solution)/shard_map/pallas_call | solution.py:357
  64.7 15.6 %collective-permute-done.8.left_in = bf16[2,256,768]{2,1,0:T(8,128)(2,1)S(1)} collective-permute-done((bf16[2,256,768]{2,1,0:T(8,128)(2,1)S(1)}, bf16[2,256,768]{2,1,0:T(8,128)(2,1)S(1)}, u32[]{:S(2)}, u32[]{:S(2)}) %collective-permute-start.8) | collective-permute-done | bytes 786464 | tf_op jit(solution)/shard_map/ppermute | solution.py:393
  80.3 0.0 collective-permute-done.9.right_in
  80.3 0.3 shard_map.103
  80.6 1.3 %collective-permute-start.10 = (bf16[256,768]{1,0:T(8,128)(2,1)S(1)}, bf16[256,768]{1,0:T(8,128)(2,1)S(1)}, u32[]{:S(2)}, u32[]{:S(2)}) collective-permute-start(bf16[256,768]{1,0:T(8,128)(2,1)S(1)} %get-tuple-element.90), channel_id=1, source_target_pairs={{0,16},{4,20},{8,24},{12,28},{16,0},{20,4},{24,8},{28,12},{1,17},{... | collective-permute-start | bytes 1179656 | tf_op jit(solution)/shard_map/ppermute | solution.py:393
  81.9 1.2 %collective-permute-start.11 = (bf16[256,768]{1,0:T(8,128)(2,1)S(1)}, bf16[256,768]{1,0:T(8,128)(2,1)S(1)}, u32[]{:S(2)}, u32[]{:S(2)}) collective-permute-start(bf16[256,768]{1,0:T(8,128)(2,1)S(1)} %get-tuple-element.92), channel_id=1, source_target_pairs={{0,8},{4,12},{8,0},{12,4},{16,24},{20,28},{24,16},{28,20},{1,9},{5... | collective-permute-start | bytes 1179656 | tf_op jit(solution)/shard_map/ppermute | solution.py:393
  83.1 0.3 shard_map.101
  83.3 0.8 shard_map.102
  84.1 5.1 %collective-permute-done.10.left_last = bf16[256,768]{1,0:T(8,128)(2,1)S(1)} collective-permute-done((bf16[256,768]{1,0:T(8,128)(2,1)S(1)}, bf16[256,768]{1,0:T(8,128)(2,1)S(1)}, u32[]{:S(2)}, u32[]{:S(2)}) %collective-permute-start.10) | collective-permute-done | bytes 393248 | tf_op jit(solution)/shard_map/ppermute | solution.py:393
  89.2 1.0 collective-permute-done.11.right_last
  90.2 1.3 %shard_map.104 = (f32[256,1024]{1,0:T(8,128)}, f32[256,512]{1,0:T(8,128)}) custom-call(f32[256,768]{1,0:T(8,128)S(1)} %get-tuple-element.87.left, bf16[256,768]{1,0:T(8,128)(2,1)S(1)} %collective-permute-done.10.left_last, f32[256,768]{1,0:T(8,128)S(1)} %get-tuple-element.91.right, bf16[256,768]{1,0:T(8,128)(2,1)S(1)} %collective-permute-done.11.right_last), custom_call_target="tpu_custom_call" | custom-call | flops 1024 | bytes 1024 | tf_op jit(solution)/shard_map/pallas_call | solution.py:468
  91.5 5.2 %collective-permute-done.14.refs_2_ = bf16[64,2048]{1,0:T(8,128)(2,1)S(1)} collective-permute-done((bf16[64,2048]{1,0:T(8,128)(2,1)S(1)}, bf16[64,2048]{1,0:T(8,128)(2,1)S(1)}, u32[]{:S(2)}, u32[]{:S(2)}) %collective-permute-start.14) | collective-permute-done | bytes 262176 | tf_op jit(solution)/shard_map/ppermute | solution.py:568
  96.7 0.0 collective-permute-done.12.refs_0_
  96.7 0.9 collective-permute-done.13.refs_1_
  97.6 1.3 %shard_map.105 = (bf16[128,2048]{1,0:T(8,128)(2,1)}, bf16[128,2048]{1,0:T(8,128)(2,1)}) custom-call(bf16[384,192]{1,0:T(8,128)(2,1)S(1)} %get-tuple-element.94.picker, f32[2,128,128]{2,1,0:T(8,128)S(1)} %get-tuple-element.95.scales, f32[128,2048]{1,0:T(8,128)S(1)} %get-tuple-element.96.mixed_part, f32[128,2048]{1,0:T(8,128)S(1)} %get-tuple-element.97.back_part, ...), custom_call_target="tpu_custom_call" | custom-call | flops 1024 | bytes 1024 | tf_op jit(solution)/shard_map/pallas_call | solution.py:508
  (10 shorter events, 0.0 us)
Async XLA Ops:
  3.0 7.4 %collective-permute-start = (bf16[64,2048]{1,0:T(8,128)(2,1)}, bf16[64,2048]{1,0:T(8,128)(2,1)S(1)}, u32[]{:S(2)}, u32[]{:S(2)}) collective-permute-start(bf16[64,2048]{1,0:T(8,128)(2,1)} %get-tuple-element.55), channel_id=1, source_target_pairs={{0,1},{1,2},{2,3},{3,0},{4,5},{5,6},{6,7},{7,4},{8,9},{9,10},{10,1... | collective-permute-start | bytes 786440 | tf_op jit(solution)/shard_map/ppermute | solution.py:568
  4.3 14.5 %collective-permute-start.2 = (bf16[64,2048]{1,0:T(8,128)(2,1)}, bf16[64,2048]{1,0:T(8,128)(2,1)S(1)}, u32[]{:S(2)}, u32[]{:S(2)}) collective-permute-start(bf16[64,2048]{1,0:T(8,128)(2,1)} %get-tuple-element.57), channel_id=1, source_target_pairs={{0,3},{1,0},{2,1},{3,2},{4,7},{5,4},{6,5},{7,6},{8,11},{9,8},{10,9... | collective-permute-start | bytes 786440 | tf_op jit(solution)/shard_map/ppermute | solution.py:568
  4.5 24.2 %collective-permute-start.1 = (bf16[64,2048]{1,0:T(8,128)(2,1)}, bf16[64,2048]{1,0:T(8,128)(2,1)S(1)}, u32[]{:S(2)}, u32[]{:S(2)}) collective-permute-start(bf16[64,2048]{1,0:T(8,128)(2,1)} %get-tuple-element.56), channel_id=1, source_target_pairs={{0,2},{1,3},{2,0},{3,1},{4,6},{5,7},{6,4},{7,5},{8,10},{9,11},{10,... | collective-permute-start | bytes 786440 | tf_op jit(solution)/shard_map/ppermute | solution.py:568
  18.9 28.6 %collective-permute-start.3 = (bf16[64,2048]{1,0:T(8,128)(2,1)}, bf16[64,2048]{1,0:T(8,128)(2,1)S(1)}, u32[]{:S(2)}, u32[]{:S(2)}) collective-permute-start(bf16[64,2048]{1,0:T(8,128)(2,1)} %get-tuple-element.66), channel_id=1, source_target_pairs={{0,1},{1,2},{2,3},{3,0},{4,5},{5,6},{6,7},{7,4},{8,9},{9,10},{10,1... | collective-permute-start | bytes 786440 | tf_op jit(solution)/shard_map/ppermute | solution.py:568
  18.9 30.1 %collective-permute-start.4 = (bf16[64,2048]{1,0:T(8,128)(2,1)}, bf16[64,2048]{1,0:T(8,128)(2,1)S(1)}, u32[]{:S(2)}, u32[]{:S(2)}) collective-permute-start(bf16[64,2048]{1,0:T(8,128)(2,1)} %get-tuple-element.67), channel_id=1, source_target_pairs={{0,2},{1,3},{2,0},{3,1},{4,6},{5,7},{6,4},{7,5},{8,10},{9,11},{10,... | collective-permute-start | bytes 786440 | tf_op jit(solution)/shard_map/ppermute | solution.py:568
  20.0 31.7 %collective-permute-start.5 = (bf16[64,2048]{1,0:T(8,128)(2,1)}, bf16[64,2048]{1,0:T(8,128)(2,1)S(1)}, u32[]{:S(2)}, u32[]{:S(2)}) collective-permute-start(bf16[64,2048]{1,0:T(8,128)(2,1)} %get-tuple-element.68), channel_id=1, source_target_pairs={{0,3},{1,0},{2,1},{3,2},{4,7},{5,4},{6,5},{7,6},{8,11},{9,8},{10,9... | collective-permute-start | bytes 786440 | tf_op jit(solution)/shard_map/ppermute | solution.py:568
  28.7 1.6 %copy-start.1 = (bf16[1,2048,512]{2,1,0:T(8,128)(2,1)S(1)}, bf16[1,2048,512]{2,1,0:T(8,128)(2,1)}, u32[]{:S(2)}) copy-start(bf16[1,2048,512]{2,1,0:T(8,128)(2,1)} %param.11) | copy-start | bytes 6291460
  30.3 0.9 copy-start.3
  31.2 20.5 %copy-start = (bf16[1,2048,1024]{2,1,0:T(8,128)(2,1)S(1)}, bf16[1,2048,1024]{2,1,0:T(8,128)(2,1)}, u32[]{:S(2)}) copy-start(bf16[1,2048,1024]{2,1,0:T(8,128)(2,1)} %param.10) | copy-start | bytes 12582916
  31.2 20.5 %copy-start.2 = (bf16[64,2048]{1,0:T(8,128)(2,1)S(1)}, bf16[64,2048]{1,0:T(8,128)(2,1)}, u32[]{:S(2)}) copy-start(bf16[64,2048]{1,0:T(8,128)(2,1)} %get-tuple-element.69.refs_0_) | copy-start | bytes 786436
  36.3 26.1 %collective-permute-start.6 = (bf16[64,2048]{1,0:T(8,128)(2,1)S(1)}, bf16[64,2048]{1,0:T(8,128)(2,1)S(1)}, u32[]{:S(2)}, u32[]{:S(2)}) collective-permute-start(bf16[64,2048]{1,0:T(8,128)(2,1)S(1)} %get-tuple-element.80.refs_3_), channel_id=1, source_target_pairs={{0,1},{1,2},{2,3},{3,0},{4,5},{5,6},{6,7},{7,4},{8,9},{9,10},{10,1... | collective-permute-start | bytes 786440 | tf_op jit(solution)/shard_map/ppermute | solution.py:568
  54.5 7.1 %collective-permute-start.7 = (bf16[8,256,768]{2,1,0:T(8,128)(2,1)S(1)}, bf16[8,256,768]{2,1,0:T(8,128)(2,1)S(1)}, u32[]{:S(2)}, u32[]{:S(2)}) collective-permute-start(bf16[8,256,768]{2,1,0:T(8,128)(2,1)S(1)} %get-tuple-element.74), channel_id=1, source_target_pairs={{0,4},{4,0},{8,12},{12,8},{16,20},{20,16},{24,28},{28,24},{1,5},{5... | collective-permute-start | bytes 9437192 | tf_op jit(solution)/shard_map/ppermute | solution.py:393
  56.5 40.2 %collective-permute-start.12 = (bf16[128,2048]{1,0:T(8,128)(2,1)S(1)}, bf16[128,2048]{1,0:T(8,128)(2,1)S(1)}, u32[]{:S(2)}, u32[]{:S(2)}) collective-permute-start(bf16[128,2048]{1,0:T(8,128)(2,1)S(1)} %get-tuple-element.98), channel_id=1, source_target_pairs={{0,2},{1,3},{2,0},{3,1},{4,6},{5,7},{6,4},{7,5},{8,10},{9,11},{10,... | collective-permute-start | bytes 1572872 | tf_op jit(solution)/shard_map/ppermute | solution.py:568
  59.1 38.5 %collective-permute-start.13 = (bf16[128,2048]{1,0:T(8,128)(2,1)S(1)}, bf16[128,2048]{1,0:T(8,128)(2,1)S(1)}, u32[]{:S(2)}, u32[]{:S(2)}) collective-permute-start(bf16[128,2048]{1,0:T(8,128)(2,1)S(1)} %get-tuple-element.99), channel_id=1, source_target_pairs={{0,3},{1,0},{2,1},{3,2},{4,7},{5,4},{6,5},{7,6},{8,11},{9,8},{10,9... | collective-permute-start | bytes 1572872 | tf_op jit(solution)/shard_map/ppermute | solution.py:568
  59.1 37.6 %collective-permute-start.14 = (bf16[64,2048]{1,0:T(8,128)(2,1)S(1)}, bf16[64,2048]{1,0:T(8,128)(2,1)S(1)}, u32[]{:S(2)}, u32[]{:S(2)}) collective-permute-start(bf16[64,2048]{1,0:T(8,128)(2,1)S(1)} %get-tuple-element.100), channel_id=1, source_target_pairs={{0,1},{1,2},{2,3},{3,0},{4,5},{5,6},{6,7},{7,4},{8,9},{9,10},{10,1... | collective-permute-start | bytes 786440 | tf_op jit(solution)/shard_map/ppermute | solution.py:568
  62.0 18.3 %collective-permute-start.8 = (bf16[2,256,768]{2,1,0:T(8,128)(2,1)S(1)}, bf16[2,256,768]{2,1,0:T(8,128)(2,1)S(1)}, u32[]{:S(2)}, u32[]{:S(2)}) collective-permute-start(bf16[2,256,768]{2,1,0:T(8,128)(2,1)S(1)} %get-tuple-element.85), channel_id=1, source_target_pairs={{0,8},{4,12},{8,0},{12,4},{16,24},{20,28},{24,16},{28,20},{1,9},{5... | collective-permute-start | bytes 2359304 | tf_op jit(solution)/shard_map/ppermute | solution.py:393
  62.4 17.9 %collective-permute-start.9 = (bf16[2,256,768]{2,1,0:T(8,128)(2,1)S(1)}, bf16[2,256,768]{2,1,0:T(8,128)(2,1)S(1)}, u32[]{:S(2)}, u32[]{:S(2)}) collective-permute-start(bf16[2,256,768]{2,1,0:T(8,128)(2,1)S(1)} %get-tuple-element.86), channel_id=1, source_target_pairs={{0,16},{4,20},{8,24},{12,28},{16,0},{20,4},{24,8},{28,12},{1,17},{... | collective-permute-start | bytes 2359304 | tf_op jit(solution)/shard_map/ppermute | solution.py:393
  80.6 8.6 %collective-permute-start.10 = (bf16[256,768]{1,0:T(8,128)(2,1)S(1)}, bf16[256,768]{1,0:T(8,128)(2,1)S(1)}, u32[]{:S(2)}, u32[]{:S(2)}) collective-permute-start(bf16[256,768]{1,0:T(8,128)(2,1)S(1)} %get-tuple-element.90), channel_id=1, source_target_pairs={{0,16},{4,20},{8,24},{12,28},{16,0},{20,4},{24,8},{28,12},{1,17},{... | collective-permute-start | bytes 1179656 | tf_op jit(solution)/shard_map/ppermute | solution.py:393
  81.9 1.4 %copy-start.4 = (s32[128,2]{0,1:T(2,128)S(1)}, s32[128,2]{0,1:T(2,128)}, u32[]{:S(2)}) copy-start(s32[128,2]{0,1:T(2,128)} %param.7) | copy-start | bytes 3076
  81.9 1.4 %copy-start.5 = (f32[128,2]{0,1:T(2,128)S(1)}, f32[128,2]{0,1:T(2,128)}, u32[]{:S(2)}) copy-start(f32[128,2]{0,1:T(2,128)} %param.8) | copy-start | bytes 3076
  81.9 8.3 %collective-permute-start.11 = (bf16[256,768]{1,0:T(8,128)(2,1)S(1)}, bf16[256,768]{1,0:T(8,128)(2,1)S(1)}, u32[]{:S(2)}, u32[]{:S(2)}) collective-permute-start(bf16[256,768]{1,0:T(8,128)(2,1)S(1)} %get-tuple-element.92), channel_id=1, source_target_pairs={{0,8},{4,12},{8,0},{12,4},{16,24},{20,28},{24,16},{28,20},{1,9},{5... | collective-permute-start | bytes 1179656 | tf_op jit(solution)/shard_map/ppermute | solution.py:393

commit v2 on v1

--- a/solution.py
+++ b/solution.py
@@ -156,12 +156,18 @@
         write(t, t // 2 % 2)
 
 
-def transpose_into(rows, rows_t):
-    width = rows.shape[1]
+def side_by_side(blocks, columns):
+    if len(blocks) == 1:
+        return blocks[0][:, columns]
+    return jnp.concatenate([block[:, columns] for block in blocks], axis=0)
+
+
+def transpose_into(blocks, rows_t):
+    width = rows_t.shape[0]
     step = 256 if width % 256 == 0 else width
 
     for begin in range(0, width, step):
-        rows_t[begin : begin + step, :] = rows[:, begin : begin + step].T
+        rows_t[begin : begin + step, :] = side_by_side(blocks, slice(begin, begin + step)).T
 
 
 def join_copies(blocks, rows, sems):
@@ -218,7 +224,7 @@
             hidden[...], down[columns, :], (((1,), (1,)), ((), ())), preferred_element_type=F32
         )
         put_blocks(outs, part.astype(BF16), columns)
-    transpose_into(rows, rows_t)
+    transpose_into([rows], rows_t)
 
 
 def forward(blocks, w_in, down):
@@ -251,29 +257,26 @@
 
 def backward_kernel(count, at, preact_hbm, w_in_hbm, rows_t, hidden, down, *refs):
     blocks, (pre_grad, grads_t, sent, w_in, *refs) = refs[:count], refs[count:]
-    grads, preact, block_sems, load_sem, sem = refs
-    joins = join_copies(blocks, grads, block_sems)
+    preact, load_sem, sem = refs
     fetch = pltpu.make_async_copy(preact_hbm, preact, sem)
     fetch.start()
     load = pltpu.make_async_copy(w_in_hbm, w_in, load_sem)
     load.start()
     units = down.shape[1]
-    for join in joins:
-        join.wait()
-    fetch.wait()
+    grads = side_by_side(blocks, slice(0, down.shape[0]))
     step = 256 if units % 256 == 0 else units
     for begin in range(0, units, step):
+        hidden_grad = jnp.dot(grads, down[:, begin : begin + step], preferred_element_type=F32)
+        if begin == 0:
+            fetch.wait()
         gate = preact[:, begin : begin + step]
         up = preact[:, units + begin : units + begin + step]
-        hidden_grad = jnp.dot(
-            grads[...], down[:, begin : begin + step], preferred_element_type=F32
-        )
         sigmoid = 1.0 / (1.0 + jnp.exp(-gate))
         gate_grad = hidden_grad * up * sigmoid * (1.0 + gate * (1.0 - sigmoid))
         up_grad = hidden_grad * gate * sigmoid
         pre_grad[:, begin : begin + step] = gate_grad.astype(BF16)
         pre_grad[:, units + begin : units + begin + step] = up_grad.astype(BF16)
-    transpose_into(grads, grads_t)
+    transpose_into(blocks, grads_t)
     write_shares(at, rows_t, grads_t, pre_grad, hidden, sent)
     load.wait()
 
@@ -337,13 +340,10 @@
         ),
         in_specs=[pl.BlockSpec(memory_space=pltpu.SMEM)]
         + anywhere(2)
-        + whole(3)
-        + anywhere(count),
+        + whole(3 + count),
         out_specs=whole(4),
         scratch_shapes=[
-            pltpu.VMEM((slots, width), BF16),
             pltpu.VMEM((slots, 2 * units), F32),
-            pltpu.SemaphoreType.DMA((count,)),
             pltpu.SemaphoreType.DMA,
             pltpu.SemaphoreType.DMA,
         ],

time: 99.2 us -> 99.6 us (level)
  no operation moved by 1% of the time
where the time goes in v2:
time: 99.6 us; the launch traced here: 98.9 us
  waiting for transfers between devices  49.4 us (50%)
  starting transfers between devices  25.1 us (25%)
  Pallas kernels  20.9 us (21%)
  local copies, waits for them, and re-layouts  2.72 us (3%)
    ppermute x10, waiting for transfers between devices, travel(): return lax.ppermute(block, 'expert', pairs)  27.7 us
    ppermute x5, waiting for transfers between devices, swap(): lax.ppermute(block, 'dp', [(at, at ^ bit) for at in range(lax.axis_size('...  21.6 us
    ppermute x10, starting transfers between devices, travel(): return lax.ppermute(block, 'expert', pairs)  20.5 us
    pallas_call x1, Pallas kernels, forward(): pl.pallas_call(functools.partial(forward_kernel, count), out_shape=(jax.S...  5.04 us
    pallas_call x2, Pallas kernels, dispatch(): pl.pallas_call(functools.partial(dispatch_kernel, experts, capacity, weig...  4.73 us
    ppermute x5, starting transfers between devices, swap(): lax.ppermute(block, 'dp', [(at, at ^ bit) for at in range(lax.axis_size('...  4.59 us
    pallas_call x1, Pallas kernels, backward(): pl.pallas_call(functools.partial(backward_kernel, count), out_shape=(jax....  3.28 us
    unnamed x12, local copies, waits for them, and re-layouts  2.55 us
  transfers between devices with their start and end apart: 15, of which 10 were waited for; matrix products, arithmetic and copies ran while one was open for 0% of the time, Pallas kernels for 17%

profile of v2, /device:TPU:11, one launch (start us, length us, event | category | flops | bytes accessed | tf_op | source)
XLA Modules:
  0.0 98.9 jit_solution(9755035869047612805)
XLA Ops:
  0.6 2.3 %shard_map.93 = (bf16[64,2048]{1,0:T(8,128)(2,1)}, bf16[64,2048]{1,0:T(8,128)(2,1)}, bf16[64,2048]{1,0:T(8,128)(2,1)}, bf16[64,2048]{1,0:T(8,128)(2,1)}) custom-call(s32[1]{0:T(128)} %bitcast.first, s32[2,128]{1,0:T(2,128)} %bitcast.15, bf16[128,2048]{1,0:T(8,128)(2,1)} %refs_1_.1), custom_call_target="tpu_custom_call" | custom-call | flops 1024 | bytes 1024 | tf_op jit(solution)/shard_map/pallas_call | solution.py:522
  3.0 1.3 %collective-permute-start = (bf16[64,2048]{1,0:T(8,128)(2,1)}, bf16[64,2048]{1,0:T(8,128)(2,1)S(1)}, u32[]{:S(2)}, u32[]{:S(2)}) collective-permute-start(bf16[64,2048]{1,0:T(8,128)(2,1)} %get-tuple-element.55), channel_id=1, source_target_pairs={{0,1},{1,2},{2,3},{3,0},{4,5},{5,6},{6,7},{7,4},{8,9},{9,10},{10,1... | collective-permute-start | bytes 786440 | tf_op jit(solution)/shard_map/ppermute | solution.py:568
  4.3 0.2 collective-permute-start.2
  4.5 2.3 %collective-permute-start.1 = (bf16[64,2048]{1,0:T(8,128)(2,1)}, bf16[64,2048]{1,0:T(8,128)(2,1)S(1)}, u32[]{:S(2)}, u32[]{:S(2)}) collective-permute-start(bf16[64,2048]{1,0:T(8,128)(2,1)} %get-tuple-element.56), channel_id=1, source_target_pairs={{0,2},{1,3},{2,0},{3,1},{4,6},{5,7},{6,4},{7,5},{8,10},{9,11},{10,... | collective-permute-start | bytes 786440 | tf_op jit(solution)/shard_map/ppermute | solution.py:568
  6.8 2.4 %shard_map.95 = (bf16[64,2048]{1,0:T(8,128)(2,1)}, bf16[64,2048]{1,0:T(8,128)(2,1)}, bf16[64,2048]{1,0:T(8,128)(2,1)}, bf16[64,2048]{1,0:T(8,128)(2,1)}) custom-call(s32[1]{0:T(128)} %bitcast.first, s32[2,128]{1,0:T(2,128)} %bitcast.16, f32[2,128]{1,0:T(2,128)} %bitcast.18, bf16[128,2048]{1,0:T(8,128)(2,1)} %refs_2_.1), custom_call_target="tpu_custom_call" | custom-call | flops 1024 | bytes 1024 | tf_op jit(solution)/shard_map/pallas_call | solution.py:522
  9.2 0.1 stack.23.at
  9.3 1.1 %collective-permute-done.refs_1_ = bf16[64,2048]{1,0:T(8,128)(2,1)S(1)} collective-permute-done((bf16[64,2048]{1,0:T(8,128)(2,1)}, bf16[64,2048]{1,0:T(8,128)(2,1)S(1)}, u32[]{:S(2)}, u32[]{:S(2)}) %collective-permute-start) | collective-permute-done | bytes 262176 | tf_op jit(solution)/shard_map/ppermute | solution.py:568
  10.4 8.5 %collective-permute-done.2.refs_3_ = bf16[64,2048]{1,0:T(8,128)(2,1)S(1)} collective-permute-done((bf16[64,2048]{1,0:T(8,128)(2,1)}, bf16[64,2048]{1,0:T(8,128)(2,1)S(1)}, u32[]{:S(2)}, u32[]{:S(2)}) %collective-permute-start.2) | collective-permute-done | bytes 262176 | tf_op jit(solution)/shard_map/ppermute | solution.py:568
  18.9 0.0 collective-permute-start.3
  18.9 1.1 %collective-permute-start.4 = (bf16[64,2048]{1,0:T(8,128)(2,1)}, bf16[64,2048]{1,0:T(8,128)(2,1)S(1)}, u32[]{:S(2)}, u32[]{:S(2)}) collective-permute-start(bf16[64,2048]{1,0:T(8,128)(2,1)} %get-tuple-element.67), channel_id=1, source_target_pairs={{0,2},{1,3},{2,0},{3,1},{4,6},{5,7},{6,4},{7,5},{8,10},{9,11},{10,... | collective-permute-start | bytes 786440 | tf_op jit(solution)/shard_map/ppermute | solution.py:568
  20.0 0.3 collective-permute-start.5
  20.3 0.1 fusion
  20.4 8.3 %collective-permute-done.1.refs_2_ = bf16[64,2048]{1,0:T(8,128)(2,1)S(1)} collective-permute-done((bf16[64,2048]{1,0:T(8,128)(2,1)}, bf16[64,2048]{1,0:T(8,128)(2,1)S(1)}, u32[]{:S(2)}, u32[]{:S(2)}) %collective-permute-start.1) | collective-permute-done | bytes 262176 | tf_op jit(solution)/shard_map/ppermute | solution.py:568
  28.7 1.6 %copy-done.1 = bf16[1,2048,512]{2,1,0:T(8,128)(2,1)S(1)} copy-done((bf16[1,2048,512]{2,1,0:T(8,128)(2,1)S(1)}, bf16[1,2048,512]{2,1,0:T(8,128)(2,1)}, u32[]{:S(2)}) %copy-start.1) | copy-done | bytes 2097176
  30.3 0.9 copy-done.3
  31.2 5.0 %shard_map.94 = (bf16[2048,256]{1,0:T(8,128)(2,1)S(1)}, f32[256,1024]{1,0:T(8,128)S(1)}, bf16[256,512]{1,0:T(8,128)(2,1)S(1)}, bf16[64,2048]{1,0:T(8,128)(2,1)S(...) custom-call(bf16[64,2048]{1,0:T(8,128)(2,1)S(1)} %copy-done.3, ...), custom_call_target="tpu_custom_call" | custom-call | flops 1024 | bytes 1024 | tf_op jit(solution)/shard_map/pallas_call | solution.py:234
  36.3 11.2 %collective-permute-start.6 = (bf16[64,2048]{1,0:T(8,128)(2,1)S(1)}, bf16[64,2048]{1,0:T(8,128)(2,1)S(1)}, u32[]{:S(2)}, u32[]{:S(2)}) collective-permute-start(bf16[64,2048]{1,0:T(8,128)(2,1)S(1)} %get-tuple-element.80.refs_3_), channel_id=1, source_target_pairs={{0,1},{1,2},{2,3},{3,0},{4,5},{5,6},{6,7},{7,4},{8,9},{9,10},{10,1... | collective-permute-start | bytes 786440 | tf_op jit(solution)/shard_map/ppermute | solution.py:568
  47.5 0.0 collective-permute-done.3.refs_1_
  47.5 1.5 %collective-permute-done.4.refs_2_ = bf16[64,2048]{1,0:T(8,128)(2,1)S(1)} collective-permute-done((bf16[64,2048]{1,0:T(8,128)(2,1)}, bf16[64,2048]{1,0:T(8,128)(2,1)S(1)}, u32[]{:S(2)}, u32[]{:S(2)}) %collective-permute-start.4) | collective-permute-done | bytes 262176 | tf_op jit(solution)/shard_map/ppermute | solution.py:568
  49.0 2.7 %collective-permute-done.5.refs_3_ = bf16[64,2048]{1,0:T(8,128)(2,1)S(1)} collective-permute-done((bf16[64,2048]{1,0:T(8,128)(2,1)}, bf16[64,2048]{1,0:T(8,128)(2,1)S(1)}, u32[]{:S(2)}, u32[]{:S(2)}) %collective-permute-start.5) | collective-permute-done | bytes 262176 | tf_op jit(solution)/shard_map/ppermute | solution.py:568
  51.7 0.0 copy-done
  51.7 3.3 %shard_map.96 = (bf16[256,1024]{1,0:T(8,128)(2,1)S(1)}, bf16[2048,256]{1,0:T(8,128)(2,1)S(1)}, bf16[8,256,768]{2,1,0:T(8,128)(2,1)S(1)}, bf16[2048,1024]{1,0:T(8,128)(2,1)S(1)}) custom-call(s32[8]{0:T(128)S(1)} %stack.23.at, f32[256,1024]{1,0:T(8,128)S(1)} %get-tuple-element.58.preact_hbm, bf16[2048,1024]{1,0:T(8,128)(2,1)S(1)} %bitcast.12, ...), custom_call_target="tpu_custom_call" | custom-call | flops 1024 | bytes 1024 | tf_op jit(solution)/shard_map/pallas_call | solution.py:333
  55.0 0.6 collective-permute-start.7
  55.5 1.4 %shard_map.97 = (bf16[128,2048]{1,0:T(8,128)(2,1)S(1)}, bf16[128,2048]{1,0:T(8,128)(2,1)S(1)}, bf16[128,2048]{1,0:T(8,128)(2,1)S(1)}, bf16[64,2048]{1,0:T(8,128)(2,1)S(1)}) custom-call(bf16[256,1024]{1,0:T(8,128)(2,1)S(1)} %get-tuple-element.75.pre_grad, bf16[2048,1024]{1,0:T(8,128)(2,1)S(1)} %get-tuple-element.76.w_in, ...), custom_call_target="tpu_custom_call" | custom-call | flops 1024 | bytes 1024 | tf_op jit(solution)/shard_map/pallas_call | solution.py:307
  56.9 2.6 %collective-permute-start.12 = (bf16[128,2048]{1,0:T(8,128)(2,1)S(1)}, bf16[128,2048]{1,0:T(8,128)(2,1)S(1)}, u32[]{:S(2)}, u32[]{:S(2)}) collective-permute-start(bf16[128,2048]{1,0:T(8,128)(2,1)S(1)} %get-tuple-element.98), channel_id=1, source_target_pairs={{0,2},{1,3},{2,0},{3,1},{4,6},{5,7},{6,4},{7,5},{8,10},{9,11},{10,... | collective-permute-start | bytes 1572872 | tf_op jit(solution)/shard_map/ppermute | solution.py:568
  59.5 0.0 collective-permute-start.13
  59.5 1.5 %collective-permute-start.14 = (bf16[64,2048]{1,0:T(8,128)(2,1)S(1)}, bf16[64,2048]{1,0:T(8,128)(2,1)S(1)}, u32[]{:S(2)}, u32[]{:S(2)}) collective-permute-start(bf16[64,2048]{1,0:T(8,128)(2,1)S(1)} %get-tuple-element.100), channel_id=1, source_target_pairs={{0,1},{1,2},{2,3},{3,0},{4,5},{5,6},{6,7},{7,4},{8,9},{9,10},{10,1... | collective-permute-start | bytes 786440 | tf_op jit(solution)/shard_map/ppermute | solution.py:568
  61.0 1.1 %shard_map.98.kept = bf16[4,256,768]{2,1,0:T(8,128)(2,1)S(1)} custom-call(s32[4]{0:T(128)S(1)} %get-tuple-element.82.at, bf16[2048,256]{1,0:T(8,128)(2,1)S(1)} %get-tuple-element.59.rows_t, bf16[2048,256]{1,0:T(8,128)(2,1)S(1)} %get-tuple-element.83.grads_t, bf16[256,1024]{1,0:T(8,128)(2,1)S(1)} %get-tuple-element.75.pre_grad, ...), custom_call_target="tpu_custom_call" | custom-call | flops 40000000000 | bytes 1024 | tf_op jit(solution)/shard_map/pallas_call | solution.py:357
  62.1 0.0 collective-permute-done.7.got
  62.1 0.4 shard_map.100
  62.5 0.3 collective-permute-start.8
  62.8 0.0 collective-permute-done.6.refs_1_
  62.8 1.2 %collective-permute-start.9 = (bf16[2,256,768]{2,1,0:T(8,128)(2,1)S(1)}, bf16[2,256,768]{2,1,0:T(8,128)(2,1)S(1)}, u32[]{:S(2)}, u32[]{:S(2)}) collective-permute-start(bf16[2,256,768]{2,1,0:T(8,128)(2,1)S(1)} %get-tuple-element.86), channel_id=1, source_target_pairs={{0,16},{4,20},{8,24},{12,28},{16,0},{20,4},{24,8},{28,12},{1,17},{... | collective-permute-start | bytes 2359304 | tf_op jit(solution)/shard_map/ppermute | solution.py:393
  64.0 1.1 %shard_map.99.kept = bf16[4,256,768]{2,1,0:T(8,128)(2,1)S(1)} custom-call(s32[4]{0:T(128)S(1)} %get-tuple-element.84.at, bf16[2048,256]{1,0:T(8,128)(2,1)S(1)} %get-tuple-element.59.rows_t, bf16[2048,256]{1,0:T(8,128)(2,1)S(1)} %get-tuple-element.83.grads_t, bf16[256,1024]{1,0:T(8,128)(2,1)S(1)} %get-tuple-element.75.pre_grad, ...), custom_call_target="tpu_custom_call" | custom-call | flops 40000000000 | bytes 1024 | tf_op jit(solution)/shard_map/pallas_call | solution.py:357
  65.1 15.6 %collective-permute-done.8.left_in = bf16[2,256,768]{2,1,0:T(8,128)(2,1)S(1)} collective-permute-done((bf16[2,256,768]{2,1,0:T(8,128)(2,1)S(1)}, bf16[2,256,768]{2,1,0:T(8,128)(2,1)S(1)}, u32[]{:S(2)}, u32[]{:S(2)}) %collective-permute-start.8) | collective-permute-done | bytes 786464 | tf_op jit(solution)/shard_map/ppermute | solution.py:393
  80.7 0.0 collective-permute-done.9.right_in
  80.7 0.3 shard_map.103
  81.0 1.3 %collective-permute-start.10 = (bf16[256,768]{1,0:T(8,128)(2,1)S(1)}, bf16[256,768]{1,0:T(8,128)(2,1)S(1)}, u32[]{:S(2)}, u32[]{:S(2)}) collective-permute-start(bf16[256,768]{1,0:T(8,128)(2,1)S(1)} %get-tuple-element.90), channel_id=1, source_target_pairs={{0,16},{4,20},{8,24},{12,28},{16,0},{20,4},{24,8},{28,12},{1,17},{... | collective-permute-start | bytes 1179656 | tf_op jit(solution)/shard_map/ppermute | solution.py:393
  82.3 1.2 %collective-permute-start.11 = (bf16[256,768]{1,0:T(8,128)(2,1)S(1)}, bf16[256,768]{1,0:T(8,128)(2,1)S(1)}, u32[]{:S(2)}, u32[]{:S(2)}) collective-permute-start(bf16[256,768]{1,0:T(8,128)(2,1)S(1)} %get-tuple-element.92), channel_id=1, source_target_pairs={{0,8},{4,12},{8,0},{12,4},{16,24},{20,28},{24,16},{28,20},{1,9},{5... | collective-permute-start | bytes 1179656 | tf_op jit(solution)/shard_map/ppermute | solution.py:393
  83.5 0.3 shard_map.101
  83.8 0.8 shard_map.102
  84.6 5.1 %collective-permute-done.10.left_last = bf16[256,768]{1,0:T(8,128)(2,1)S(1)} collective-permute-done((bf16[256,768]{1,0:T(8,128)(2,1)S(1)}, bf16[256,768]{1,0:T(8,128)(2,1)S(1)}, u32[]{:S(2)}, u32[]{:S(2)}) %collective-permute-start.10) | collective-permute-done | bytes 393248 | tf_op jit(solution)/shard_map/ppermute | solution.py:393
  89.7 1.0 collective-permute-done.11.right_last
  90.6 1.3 %shard_map.104 = (f32[256,1024]{1,0:T(8,128)}, f32[256,512]{1,0:T(8,128)}) custom-call(f32[256,768]{1,0:T(8,128)S(1)} %get-tuple-element.87.left, bf16[256,768]{1,0:T(8,128)(2,1)S(1)} %collective-permute-done.10.left_last, f32[256,768]{1,0:T(8,128)S(1)} %get-tuple-element.91.right, bf16[256,768]{1,0:T(8,128)(2,1)S(1)} %collective-permute-done.11.right_last), custom_call_target="tpu_custom_call" | custom-call | flops 1024 | bytes 1024 | tf_op jit(solution)/shard_map/pallas_call | solution.py:468
  91.9 5.2 %collective-permute-done.14.refs_2_ = bf16[64,2048]{1,0:T(8,128)(2,1)S(1)} collective-permute-done((bf16[64,2048]{1,0:T(8,128)(2,1)S(1)}, bf16[64,2048]{1,0:T(8,128)(2,1)S(1)}, u32[]{:S(2)}, u32[]{:S(2)}) %collective-permute-start.14) | collective-permute-done | bytes 262176 | tf_op jit(solution)/shard_map/ppermute | solution.py:568
  97.1 0.0 collective-permute-done.12.refs_0_
  97.1 0.4 collective-permute-done.13.refs_1_
  97.6 1.3 %shard_map.105 = (bf16[128,2048]{1,0:T(8,128)(2,1)}, bf16[128,2048]{1,0:T(8,128)(2,1)}) custom-call(bf16[384,192]{1,0:T(8,128)(2,1)S(1)} %get-tuple-element.94.picker, f32[2,128,128]{2,1,0:T(8,128)S(1)} %get-tuple-element.95.scales, f32[128,2048]{1,0:T(8,128)S(1)} %get-tuple-element.96.mixed_part, f32[128,2048]{1,0:T(8,128)S(1)} %get-tuple-element.97.back_part, ...), custom_call_target="tpu_custom_call" | custom-call | flops 1024 | bytes 1024 | tf_op jit(solution)/shard_map/pallas_call | solution.py:508
  (10 shorter events, 0.0 us)
Async XLA Ops:
  3.0 7.4 %collective-permute-start = (bf16[64,2048]{1,0:T(8,128)(2,1)}, bf16[64,2048]{1,0:T(8,128)(2,1)S(1)}, u32[]{:S(2)}, u32[]{:S(2)}) collective-permute-start(bf16[64,2048]{1,0:T(8,128)(2,1)} %get-tuple-element.55), channel_id=1, source_target_pairs={{0,1},{1,2},{2,3},{3,0},{4,5},{5,6},{6,7},{7,4},{8,9},{9,10},{10,1... | collective-permute-start | bytes 786440 | tf_op jit(solution)/shard_map/ppermute | solution.py:568
  4.3 14.5 %collective-permute-start.2 = (bf16[64,2048]{1,0:T(8,128)(2,1)}, bf16[64,2048]{1,0:T(8,128)(2,1)S(1)}, u32[]{:S(2)}, u32[]{:S(2)}) collective-permute-start(bf16[64,2048]{1,0:T(8,128)(2,1)} %get-tuple-element.57), channel_id=1, source_target_pairs={{0,3},{1,0},{2,1},{3,2},{4,7},{5,4},{6,5},{7,6},{8,11},{9,8},{10,9... | collective-permute-start | bytes 786440 | tf_op jit(solution)/shard_map/ppermute | solution.py:568
  4.5 24.2 %collective-permute-start.1 = (bf16[64,2048]{1,0:T(8,128)(2,1)}, bf16[64,2048]{1,0:T(8,128)(2,1)S(1)}, u32[]{:S(2)}, u32[]{:S(2)}) collective-permute-start(bf16[64,2048]{1,0:T(8,128)(2,1)} %get-tuple-element.56), channel_id=1, source_target_pairs={{0,2},{1,3},{2,0},{3,1},{4,6},{5,7},{6,4},{7,5},{8,10},{9,11},{10,... | collective-permute-start | bytes 786440 | tf_op jit(solution)/shard_map/ppermute | solution.py:568
  18.9 28.6 %collective-permute-start.3 = (bf16[64,2048]{1,0:T(8,128)(2,1)}, bf16[64,2048]{1,0:T(8,128)(2,1)S(1)}, u32[]{:S(2)}, u32[]{:S(2)}) collective-permute-start(bf16[64,2048]{1,0:T(8,128)(2,1)} %get-tuple-element.66), channel_id=1, source_target_pairs={{0,1},{1,2},{2,3},{3,0},{4,5},{5,6},{6,7},{7,4},{8,9},{9,10},{10,1... | collective-permute-start | bytes 786440 | tf_op jit(solution)/shard_map/ppermute | solution.py:568
  18.9 30.1 %collective-permute-start.4 = (bf16[64,2048]{1,0:T(8,128)(2,1)}, bf16[64,2048]{1,0:T(8,128)(2,1)S(1)}, u32[]{:S(2)}, u32[]{:S(2)}) collective-permute-start(bf16[64,2048]{1,0:T(8,128)(2,1)} %get-tuple-element.67), channel_id=1, source_target_pairs={{0,2},{1,3},{2,0},{3,1},{4,6},{5,7},{6,4},{7,5},{8,10},{9,11},{10,... | collective-permute-start | bytes 786440 | tf_op jit(solution)/shard_map/ppermute | solution.py:568
  20.0 31.7 %collective-permute-start.5 = (bf16[64,2048]{1,0:T(8,128)(2,1)}, bf16[64,2048]{1,0:T(8,128)(2,1)S(1)}, u32[]{:S(2)}, u32[]{:S(2)}) collective-permute-start(bf16[64,2048]{1,0:T(8,128)(2,1)} %get-tuple-element.68), channel_id=1, source_target_pairs={{0,3},{1,0},{2,1},{3,2},{4,7},{5,4},{6,5},{7,6},{8,11},{9,8},{10,9... | collective-permute-start | bytes 786440 | tf_op jit(solution)/shard_map/ppermute | solution.py:568
  28.7 1.6 %copy-start.1 = (bf16[1,2048,512]{2,1,0:T(8,128)(2,1)S(1)}, bf16[1,2048,512]{2,1,0:T(8,128)(2,1)}, u32[]{:S(2)}) copy-start(bf16[1,2048,512]{2,1,0:T(8,128)(2,1)} %param.11) | copy-start | bytes 6291460
  30.3 0.9 copy-start.3
  31.2 20.5 %copy-start = (bf16[1,2048,1024]{2,1,0:T(8,128)(2,1)S(1)}, bf16[1,2048,1024]{2,1,0:T(8,128)(2,1)}, u32[]{:S(2)}) copy-start(bf16[1,2048,1024]{2,1,0:T(8,128)(2,1)} %param.10) | copy-start | bytes 12582916
  31.2 20.5 %copy-start.2 = (bf16[64,2048]{1,0:T(8,128)(2,1)S(1)}, bf16[64,2048]{1,0:T(8,128)(2,1)}, u32[]{:S(2)}) copy-start(bf16[64,2048]{1,0:T(8,128)(2,1)} %get-tuple-element.69.refs_0_) | copy-start | bytes 786436
  36.3 26.5 %collective-permute-start.6 = (bf16[64,2048]{1,0:T(8,128)(2,1)S(1)}, bf16[64,2048]{1,0:T(8,128)(2,1)S(1)}, u32[]{:S(2)}, u32[]{:S(2)}) collective-permute-start(bf16[64,2048]{1,0:T(8,128)(2,1)S(1)} %get-tuple-element.80.refs_3_), channel_id=1, source_target_pairs={{0,1},{1,2},{2,3},{3,0},{4,5},{5,6},{6,7},{7,4},{8,9},{9,10},{10,1... | collective-permute-start | bytes 786440 | tf_op jit(solution)/shard_map/ppermute | solution.py:568
  55.0 7.1 %collective-permute-start.7 = (bf16[8,256,768]{2,1,0:T(8,128)(2,1)S(1)}, bf16[8,256,768]{2,1,0:T(8,128)(2,1)S(1)}, u32[]{:S(2)}, u32[]{:S(2)}) collective-permute-start(bf16[8,256,768]{2,1,0:T(8,128)(2,1)S(1)} %get-tuple-element.74), channel_id=1, source_target_pairs={{0,4},{4,0},{8,12},{12,8},{16,20},{20,16},{24,28},{28,24},{1,5},{5... | collective-permute-start | bytes 9437192 | tf_op jit(solution)/shard_map/ppermute | solution.py:393
  56.9 40.2 %collective-permute-start.12 = (bf16[128,2048]{1,0:T(8,128)(2,1)S(1)}, bf16[128,2048]{1,0:T(8,128)(2,1)S(1)}, u32[]{:S(2)}, u32[]{:S(2)}) collective-permute-start(bf16[128,2048]{1,0:T(8,128)(2,1)S(1)} %get-tuple-element.98), channel_id=1, source_target_pairs={{0,2},{1,3},{2,0},{3,1},{4,6},{5,7},{6,4},{7,5},{8,10},{9,11},{10,... | collective-permute-start | bytes 1572872 | tf_op jit(solution)/shard_map/ppermute | solution.py:568
  59.5 38.1 %collective-permute-start.13 = (bf16[128,2048]{1,0:T(8,128)(2,1)S(1)}, bf16[128,2048]{1,0:T(8,128)(2,1)S(1)}, u32[]{:S(2)}, u32[]{:S(2)}) collective-permute-start(bf16[128,2048]{1,0:T(8,128)(2,1)S(1)} %get-tuple-element.99), channel_id=1, source_target_pairs={{0,3},{1,0},{2,1},{3,2},{4,7},{5,4},{6,5},{7,6},{8,11},{9,8},{10,9... | collective-permute-start | bytes 1572872 | tf_op jit(solution)/shard_map/ppermute | solution.py:568
  59.5 37.6 %collective-permute-start.14 = (bf16[64,2048]{1,0:T(8,128)(2,1)S(1)}, bf16[64,2048]{1,0:T(8,128)(2,1)S(1)}, u32[]{:S(2)}, u32[]{:S(2)}) collective-permute-start(bf16[64,2048]{1,0:T(8,128)(2,1)S(1)} %get-tuple-element.100), channel_id=1, source_target_pairs={{0,1},{1,2},{2,3},{3,0},{4,5},{5,6},{6,7},{7,4},{8,9},{9,10},{10,1... | collective-permute-start | bytes 786440 | tf_op jit(solution)/shard_map/ppermute | solution.py:568
  62.5 18.3 %collective-permute-start.8 = (bf16[2,256,768]{2,1,0:T(8,128)(2,1)S(1)}, bf16[2,256,768]{2,1,0:T(8,128)(2,1)S(1)}, u32[]{:S(2)}, u32[]{:S(2)}) collective-permute-start(bf16[2,256,768]{2,1,0:T(8,128)(2,1)S(1)} %get-tuple-element.85), channel_id=1, source_target_pairs={{0,8},{4,12},{8,0},{12,4},{16,24},{20,28},{24,16},{28,20},{1,9},{5... | collective-permute-start | bytes 2359304 | tf_op jit(solution)/shard_map/ppermute | solution.py:393
  62.8 17.9 %collective-permute-start.9 = (bf16[2,256,768]{2,1,0:T(8,128)(2,1)S(1)}, bf16[2,256,768]{2,1,0:T(8,128)(2,1)S(1)}, u32[]{:S(2)}, u32[]{:S(2)}) collective-permute-start(bf16[2,256,768]{2,1,0:T(8,128)(2,1)S(1)} %get-tuple-element.86), channel_id=1, source_target_pairs={{0,16},{4,20},{8,24},{12,28},{16,0},{20,4},{24,8},{28,12},{1,17},{... | collective-permute-start | bytes 2359304 | tf_op jit(solution)/shard_map/ppermute | solution.py:393
  81.0 8.7 %collective-permute-start.10 = (bf16[256,768]{1,0:T(8,128)(2,1)S(1)}, bf16[256,768]{1,0:T(8,128)(2,1)S(1)}, u32[]{:S(2)}, u32[]{:S(2)}) collective-permute-start(bf16[256,768]{1,0:T(8,128)(2,1)S(1)} %get-tuple-element.90), channel_id=1, source_target_pairs={{0,16},{4,20},{8,24},{12,28},{16,0},{20,4},{24,8},{28,12},{1,17},{... | collective-permute-start | bytes 1179656 | tf_op jit(solution)/shard_map/ppermute | solution.py:393
  82.3 1.4 %copy-start.4 = (s32[128,2]{0,1:T(2,128)S(1)}, s32[128,2]{0,1:T(2,128)}, u32[]{:S(2)}) copy-start(s32[128,2]{0,1:T(2,128)} %param.7) | copy-start | bytes 3076
  82.3 1.4 %copy-start.5 = (f32[128,2]{0,1:T(2,128)S(1)}, f32[128,2]{0,1:T(2,128)}, u32[]{:S(2)}) copy-start(f32[128,2]{0,1:T(2,128)} %param.8) | copy-start | bytes 3076
  82.3 8.3 %collective-permute-start.11 = (bf16[256,768]{1,0:T(8,128)(2,1)S(1)}, bf16[256,768]{1,0:T(8,128)(2,1)S(1)}, u32[]{:S(2)}, u32[]{:S(2)}) collective-permute-start(bf16[256,768]{1,0:T(8,128)(2,1)S(1)} %get-tuple-element.92), channel_id=1, source_target_pairs={{0,8},{4,12},{8,0},{12,4},{16,24},{20,28},{24,16},{28,20},{1,9},{5... | collective-permute-start | bytes 1179656 | tf_op jit(solution)/shard_map/ppermute | solution.py:393

commit v3 on v2

--- a/solution.py
+++ b/solution.py
@@ -263,14 +263,13 @@
     load = pltpu.make_async_copy(w_in_hbm, w_in, load_sem)
     load.start()
     units = down.shape[1]
+    fetch.wait()
     grads = side_by_side(blocks, slice(0, down.shape[0]))
     step = 256 if units % 256 == 0 else units
     for begin in range(0, units, step):
-        hidden_grad = jnp.dot(grads, down[:, begin : begin + step], preferred_element_type=F32)
-        if begin == 0:
-            fetch.wait()
         gate = preact[:, begin : begin + step]
         up = preact[:, units + begin : units + begin + step]
+        hidden_grad = jnp.dot(grads, down[:, begin : begin + step], preferred_element_type=F32)
         sigmoid = 1.0 / (1.0 + jnp.exp(-gate))
         gate_grad = hidden_grad * up * sigmoid * (1.0 + gate * (1.0 - sigmoid))
         up_grad = hidden_grad * gate * sigmoid

time: 99.6 us -> 99.1 us (level)
  no operation moved by 1% of the time
where the time goes in v3:
time: 99.1 us; the launch traced here: 98.9 us
  waiting for transfers between devices  49.9 us (50%)
  starting transfers between devices  25.1 us (25%)
  Pallas kernels  20.4 us (21%)
  local copies, waits for them, and re-layouts  2.72 us (3%)
    ppermute x10, waiting for transfers between devices, travel(): return lax.ppermute(block, 'expert', pairs)  28.3 us
    ppermute x5, waiting for transfers between devices, swap(): lax.ppermute(block, 'dp', [(at, at ^ bit) for at in range(lax.axis_size('...  21.6 us
    ppermute x10, starting transfers between devices, travel(): return lax.ppermute(block, 'expert', pairs)  20.5 us
    pallas_call x1, Pallas kernels, forward(): pl.pallas_call(functools.partial(forward_kernel, count), out_shape=(jax.S...  5.04 us
    pallas_call x2, Pallas kernels, dispatch(): pl.pallas_call(functools.partial(dispatch_kernel, experts, capacity, weig...  4.73 us
    ppermute x5, starting transfers between devices, swap(): lax.ppermute(block, 'dp', [(at, at ^ bit) for at in range(lax.axis_size('...  4.6 us
    pallas_call x1, Pallas kernels, backward(): pl.pallas_call(functools.partial(backward_kernel, count), out_shape=(jax....  2.73 us
    unnamed x12, local copies, waits for them, and re-layouts  2.55 us
  transfers between devices with their start and end apart: 15, of which 10 were waited for; matrix products, arithmetic and copies ran while one was open for 0% of the time, Pallas kernels for 17%

profile of v3, /device:TPU:11, one launch (start us, length us, event | category | flops | bytes accessed | tf_op | source)
XLA Modules:
  0.0 98.9 jit_solution(9317907167181995619)
XLA Ops:
  0.6 2.3 %shard_map.93 = (bf16[64,2048]{1,0:T(8,128)(2,1)}, bf16[64,2048]{1,0:T(8,128)(2,1)}, bf16[64,2048]{1,0:T(8,128)(2,1)}, bf16[64,2048]{1,0:T(8,128)(2,1)}) custom-call(s32[1]{0:T(128)} %bitcast.first, s32[2,128]{1,0:T(2,128)} %bitcast.15, bf16[128,2048]{1,0:T(8,128)(2,1)} %refs_1_.1), custom_call_target="tpu_custom_call" | custom-call | flops 1024 | bytes 1024 | tf_op jit(solution)/shard_map/pallas_call | solution.py:521
  3.0 1.3 %collective-permute-start = (bf16[64,2048]{1,0:T(8,128)(2,1)}, bf16[64,2048]{1,0:T(8,128)(2,1)S(1)}, u32[]{:S(2)}, u32[]{:S(2)}) collective-permute-start(bf16[64,2048]{1,0:T(8,128)(2,1)} %get-tuple-element.55), channel_id=1, source_target_pairs={{0,1},{1,2},{2,3},{3,0},{4,5},{5,6},{6,7},{7,4},{8,9},{9,10},{10,1... | collective-permute-start | bytes 786440 | tf_op jit(solution)/shard_map/ppermute | solution.py:567
  4.3 0.2 collective-permute-start.2
  4.5 2.3 %collective-permute-start.1 = (bf16[64,2048]{1,0:T(8,128)(2,1)}, bf16[64,2048]{1,0:T(8,128)(2,1)S(1)}, u32[]{:S(2)}, u32[]{:S(2)}) collective-permute-start(bf16[64,2048]{1,0:T(8,128)(2,1)} %get-tuple-element.56), channel_id=1, source_target_pairs={{0,2},{1,3},{2,0},{3,1},{4,6},{5,7},{6,4},{7,5},{8,10},{9,11},{10,... | collective-permute-start | bytes 786440 | tf_op jit(solution)/shard_map/ppermute | solution.py:567
  6.8 2.4 %shard_map.95 = (bf16[64,2048]{1,0:T(8,128)(2,1)}, bf16[64,2048]{1,0:T(8,128)(2,1)}, bf16[64,2048]{1,0:T(8,128)(2,1)}, bf16[64,2048]{1,0:T(8,128)(2,1)}) custom-call(s32[1]{0:T(128)} %bitcast.first, s32[2,128]{1,0:T(2,128)} %bitcast.16, f32[2,128]{1,0:T(2,128)} %bitcast.18, bf16[128,2048]{1,0:T(8,128)(2,1)} %refs_2_.1), custom_call_target="tpu_custom_call" | custom-call | flops 1024 | bytes 1024 | tf_op jit(solution)/shard_map/pallas_call | solution.py:521
  9.2 0.1 stack.23.at
  9.3 1.1 %collective-permute-done.refs_1_ = bf16[64,2048]{1,0:T(8,128)(2,1)S(1)} collective-permute-done((bf16[64,2048]{1,0:T(8,128)(2,1)}, bf16[64,2048]{1,0:T(8,128)(2,1)S(1)}, u32[]{:S(2)}, u32[]{:S(2)}) %collective-permute-start) | collective-permute-done | bytes 262176 | tf_op jit(solution)/shard_map/ppermute | solution.py:567
  10.4 8.5 %collective-permute-done.2.refs_3_ = bf16[64,2048]{1,0:T(8,128)(2,1)S(1)} collective-permute-done((bf16[64,2048]{1,0:T(8,128)(2,1)}, bf16[64,2048]{1,0:T(8,128)(2,1)S(1)}, u32[]{:S(2)}, u32[]{:S(2)}) %collective-permute-start.2) | collective-permute-done | bytes 262176 | tf_op jit(solution)/shard_map/ppermute | solution.py:567
  18.9 0.0 collective-permute-start.3
  18.9 1.1 %collective-permute-start.4 = (bf16[64,2048]{1,0:T(8,128)(2,1)}, bf16[64,2048]{1,0:T(8,128)(2,1)S(1)}, u32[]{:S(2)}, u32[]{:S(2)}) collective-permute-start(bf16[64,2048]{1,0:T(8,128)(2,1)} %get-tuple-element.67), channel_id=1, source_target_pairs={{0,2},{1,3},{2,0},{3,1},{4,6},{5,7},{6,4},{7,5},{8,10},{9,11},{10,... | collective-permute-start | bytes 786440 | tf_op jit(solution)/shard_map/ppermute | solution.py:567
  20.0 0.3 collective-permute-start.5
  20.3 0.1 fusion
  20.4 8.3 %collective-permute-done.1.refs_2_ = bf16[64,2048]{1,0:T(8,128)(2,1)S(1)} collective-permute-done((bf16[64,2048]{1,0:T(8,128)(2,1)}, bf16[64,2048]{1,0:T(8,128)(2,1)S(1)}, u32[]{:S(2)}, u32[]{:S(2)}) %collective-permute-start.1) | collective-permute-done | bytes 262176 | tf_op jit(solution)/shard_map/ppermute | solution.py:567
  28.7 1.6 %copy-done.1 = bf16[1,2048,512]{2,1,0:T(8,128)(2,1)S(1)} copy-done((bf16[1,2048,512]{2,1,0:T(8,128)(2,1)S(1)}, bf16[1,2048,512]{2,1,0:T(8,128)(2,1)}, u32[]{:S(2)}) %copy-start.1) | copy-done | bytes 2097176
  30.3 0.9 copy-done.3
  31.2 5.0 %shard_map.94 = (bf16[2048,256]{1,0:T(8,128)(2,1)S(1)}, f32[256,1024]{1,0:T(8,128)S(1)}, bf16[256,512]{1,0:T(8,128)(2,1)S(1)}, bf16[64,2048]{1,0:T(8,128)(2,1)S(...) custom-call(bf16[64,2048]{1,0:T(8,128)(2,1)S(1)} %copy-done.3, ...), custom_call_target="tpu_custom_call" | custom-call | flops 1024 | bytes 1024 | tf_op jit(solution)/shard_map/pallas_call | solution.py:234
  36.3 11.2 %collective-permute-start.6 = (bf16[64,2048]{1,0:T(8,128)(2,1)S(1)}, bf16[64,2048]{1,0:T(8,128)(2,1)S(1)}, u32[]{:S(2)}, u32[]{:S(2)}) collective-permute-start(bf16[64,2048]{1,0:T(8,128)(2,1)S(1)} %get-tuple-element.80.refs_3_), channel_id=1, source_target_pairs={{0,1},{1,2},{2,3},{3,0},{4,5},{5,6},{6,7},{7,4},{8,9},{9,10},{10,1... | collective-permute-start | bytes 786440 | tf_op jit(solution)/shard_map/ppermute | solution.py:567
  47.5 0.0 collective-permute-done.3.refs_1_
  47.5 1.5 %collective-permute-done.4.refs_2_ = bf16[64,2048]{1,0:T(8,128)(2,1)S(1)} collective-permute-done((bf16[64,2048]{1,0:T(8,128)(2,1)}, bf16[64,2048]{1,0:T(8,128)(2,1)S(1)}, u32[]{:S(2)}, u32[]{:S(2)}) %collective-permute-start.4) | collective-permute-done | bytes 262176 | tf_op jit(solution)/shard_map/ppermute | solution.py:567
  49.0 2.7 %collective-permute-done.5.refs_3_ = bf16[64,2048]{1,0:T(8,128)(2,1)S(1)} collective-permute-done((bf16[64,2048]{1,0:T(8,128)(2,1)}, bf16[64,2048]{1,0:T(8,128)(2,1)S(1)}, u32[]{:S(2)}, u32[]{:S(2)}) %collective-permute-start.5) | collective-permute-done | bytes 262176 | tf_op jit(solution)/shard_map/ppermute | solution.py:567
  51.7 0.0 copy-done
  51.7 2.7 %shard_map.96 = (bf16[256,1024]{1,0:T(8,128)(2,1)S(1)}, bf16[2048,256]{1,0:T(8,128)(2,1)S(1)}, bf16[8,256,768]{2,1,0:T(8,128)(2,1)S(1)}, bf16[2048,1024]{1,0:T(8,128)(2,1)S(1)}) custom-call(s32[8]{0:T(128)S(1)} %stack.23.at, f32[256,1024]{1,0:T(8,128)S(1)} %get-tuple-element.58.preact_hbm, bf16[2048,1024]{1,0:T(8,128)(2,1)S(1)} %bitcast.12, ...), custom_call_target="tpu_custom_call" | custom-call | flops 1024 | bytes 1024 | tf_op jit(solution)/shard_map/pallas_call | solution.py:332
  54.4 0.6 collective-permute-start.7
  55.0 1.4 %shard_map.97 = (bf16[128,2048]{1,0:T(8,128)(2,1)S(1)}, bf16[128,2048]{1,0:T(8,128)(2,1)S(1)}, bf16[128,2048]{1,0:T(8,128)(2,1)S(1)}, bf16[64,2048]{1,0:T(8,128)(2,1)S(1)}) custom-call(bf16[256,1024]{1,0:T(8,128)(2,1)S(1)} %get-tuple-element.75.pre_grad, bf16[2048,1024]{1,0:T(8,128)(2,1)S(1)} %get-tuple-element.76.w_in, ...), custom_call_target="tpu_custom_call" | custom-call | flops 1024 | bytes 1024 | tf_op jit(solution)/shard_map/pallas_call | solution.py:306
  56.4 2.6 %collective-permute-start.12 = (bf16[128,2048]{1,0:T(8,128)(2,1)S(1)}, bf16[128,2048]{1,0:T(8,128)(2,1)S(1)}, u32[]{:S(2)}, u32[]{:S(2)}) collective-permute-start(bf16[128,2048]{1,0:T(8,128)(2,1)S(1)} %get-tuple-element.98), channel_id=1, source_target_pairs={{0,2},{1,3},{2,0},{3,1},{4,6},{5,7},{6,4},{7,5},{8,10},{9,11},{10,... | collective-permute-start | bytes 1572872 | tf_op jit(solution)/shard_map/ppermute | solution.py:567
  58.9 0.0 collective-permute-start.13
  58.9 1.5 %collective-permute-start.14 = (bf16[64,2048]{1,0:T(8,128)(2,1)S(1)}, bf16[64,2048]{1,0:T(8,128)(2,1)S(1)}, u32[]{:S(2)}, u32[]{:S(2)}) collective-permute-start(bf16[64,2048]{1,0:T(8,128)(2,1)S(1)} %get-tuple-element.100), channel_id=1, source_target_pairs={{0,1},{1,2},{2,3},{3,0},{4,5},{5,6},{6,7},{7,4},{8,9},{9,10},{10,1... | collective-permute-start | bytes 786440 | tf_op jit(solution)/shard_map/ppermute | solution.py:567
  60.4 1.1 %shard_map.98.kept = bf16[4,256,768]{2,1,0:T(8,128)(2,1)S(1)} custom-call(s32[4]{0:T(128)S(1)} %get-tuple-element.82.at, bf16[2048,256]{1,0:T(8,128)(2,1)S(1)} %get-tuple-element.59.rows_t, bf16[2048,256]{1,0:T(8,128)(2,1)S(1)} %get-tuple-element.83.grads_t, bf16[256,1024]{1,0:T(8,128)(2,1)S(1)} %get-tuple-element.75.pre_grad, ...), custom_call_target="tpu_custom_call" | custom-call | flops 40000000000 | bytes 1024 | tf_op jit(solution)/shard_map/pallas_call | solution.py:356
  61.5 0.0 collective-permute-done.7.got
  61.5 0.4 shard_map.100
  61.9 0.3 collective-permute-start.8
  62.2 0.0 collective-permute-done.6.refs_1_
  62.2 1.2 %collective-permute-start.9 = (bf16[2,256,768]{2,1,0:T(8,128)(2,1)S(1)}, bf16[2,256,768]{2,1,0:T(8,128)(2,1)S(1)}, u32[]{:S(2)}, u32[]{:S(2)}) collective-permute-start(bf16[2,256,768]{2,1,0:T(8,128)(2,1)S(1)} %get-tuple-element.86), channel_id=1, source_target_pairs={{0,16},{4,20},{8,24},{12,28},{16,0},{20,4},{24,8},{28,12},{1,17},{... | collective-permute-start | bytes 2359304 | tf_op jit(solution)/shard_map/ppermute | solution.py:392
  63.5 1.1 %shard_map.99.kept = bf16[4,256,768]{2,1,0:T(8,128)(2,1)S(1)} custom-call(s32[4]{0:T(128)S(1)} %get-tuple-element.84.at, bf16[2048,256]{1,0:T(8,128)(2,1)S(1)} %get-tuple-element.59.rows_t, bf16[2048,256]{1,0:T(8,128)(2,1)S(1)} %get-tuple-element.83.grads_t, bf16[256,1024]{1,0:T(8,128)(2,1)S(1)} %get-tuple-element.75.pre_grad, ...), custom_call_target="tpu_custom_call" | custom-call | flops 40000000000 | bytes 1024 | tf_op jit(solution)/shard_map/pallas_call | solution.py:356
  64.6 15.6 %collective-permute-done.8.left_in = bf16[2,256,768]{2,1,0:T(8,128)(2,1)S(1)} collective-permute-done((bf16[2,256,768]{2,1,0:T(8,128)(2,1)S(1)}, bf16[2,256,768]{2,1,0:T(8,128)(2,1)S(1)}, u32[]{:S(2)}, u32[]{:S(2)}) %collective-permute-start.8) | collective-permute-done | bytes 786464 | tf_op jit(solution)/shard_map/ppermute | solution.py:392
  80.2 0.0 collective-permute-done.9.right_in
  80.2 0.3 shard_map.103
  80.5 1.3 %collective-permute-start.10 = (bf16[256,768]{1,0:T(8,128)(2,1)S(1)}, bf16[256,768]{1,0:T(8,128)(2,1)S(1)}, u32[]{:S(2)}, u32[]{:S(2)}) collective-permute-start(bf16[256,768]{1,0:T(8,128)(2,1)S(1)} %get-tuple-element.90), channel_id=1, source_target_pairs={{0,16},{4,20},{8,24},{12,28},{16,0},{20,4},{24,8},{28,12},{1,17},{... | collective-permute-start | bytes 1179656 | tf_op jit(solution)/shard_map/ppermute | solution.py:392
  81.8 1.2 %collective-permute-start.11 = (bf16[256,768]{1,0:T(8,128)(2,1)S(1)}, bf16[256,768]{1,0:T(8,128)(2,1)S(1)}, u32[]{:S(2)}, u32[]{:S(2)}) collective-permute-start(bf16[256,768]{1,0:T(8,128)(2,1)S(1)} %get-tuple-element.92), channel_id=1, source_target_pairs={{0,8},{4,12},{8,0},{12,4},{16,24},{20,28},{24,16},{28,20},{1,9},{5... | collective-permute-start | bytes 1179656 | tf_op jit(solution)/shard_map/ppermute | solution.py:392
  82.9 0.3 shard_map.101
  83.2 0.8 shard_map.102
  84.0 5.1 %collective-permute-done.10.left_last = bf16[256,768]{1,0:T(8,128)(2,1)S(1)} collective-permute-done((bf16[256,768]{1,0:T(8,128)(2,1)S(1)}, bf16[256,768]{1,0:T(8,128)(2,1)S(1)}, u32[]{:S(2)}, u32[]{:S(2)}) %collective-permute-start.10) | collective-permute-done | bytes 393248 | tf_op jit(solution)/shard_map/ppermute | solution.py:392
  89.1 1.0 collective-permute-done.11.right_last
  90.1 1.3 %shard_map.104 = (f32[256,1024]{1,0:T(8,128)}, f32[256,512]{1,0:T(8,128)}) custom-call(f32[256,768]{1,0:T(8,128)S(1)} %get-tuple-element.87.left, bf16[256,768]{1,0:T(8,128)(2,1)S(1)} %collective-permute-done.10.left_last, f32[256,768]{1,0:T(8,128)S(1)} %get-tuple-element.91.right, bf16[256,768]{1,0:T(8,128)(2,1)S(1)} %collective-permute-done.11.right_last), custom_call_target="tpu_custom_call" | custom-call | flops 1024 | bytes 1024 | tf_op jit(solution)/shard_map/pallas_call | solution.py:467
  91.3 5.2 %collective-permute-done.14.refs_2_ = bf16[64,2048]{1,0:T(8,128)(2,1)S(1)} collective-permute-done((bf16[64,2048]{1,0:T(8,128)(2,1)S(1)}, bf16[64,2048]{1,0:T(8,128)(2,1)S(1)}, u32[]{:S(2)}, u32[]{:S(2)}) %collective-permute-start.14) | collective-permute-done | bytes 262176 | tf_op jit(solution)/shard_map/ppermute | solution.py:567
  96.6 0.0 collective-permute-done.12.refs_0_
  96.6 1.0 %collective-permute-done.13.refs_1_ = bf16[128,2048]{1,0:T(8,128)(2,1)S(1)} collective-permute-done((bf16[128,2048]{1,0:T(8,128)(2,1)S(1)}, bf16[128,2048]{1,0:T(8,128)(2,1)S(1)}, u32[]{:S(2)}, u32[]{:S(2)}) %collective-permute-start.13) | collective-permute-done | bytes 524320 | tf_op jit(solution)/shard_map/ppermute | solution.py:567
  97.6 1.3 %shard_map.105 = (bf16[128,2048]{1,0:T(8,128)(2,1)}, bf16[128,2048]{1,0:T(8,128)(2,1)}) custom-call(bf16[384,192]{1,0:T(8,128)(2,1)S(1)} %get-tuple-element.94.picker, f32[2,128,128]{2,1,0:T(8,128)S(1)} %get-tuple-element.95.scales, f32[128,2048]{1,0:T(8,128)S(1)} %get-tuple-element.96.mixed_part, f32[128,2048]{1,0:T(8,128)S(1)} %get-tuple-element.97.back_part, ...), custom_call_target="tpu_custom_call" | custom-call | flops 1024 | bytes 1024 | tf_op jit(solution)/shard_map/pallas_call | solution.py:507
  (10 shorter events, 0.0 us)
Async XLA Ops:
  3.0 7.4 %collective-permute-start = (bf16[64,2048]{1,0:T(8,128)(2,1)}, bf16[64,2048]{1,0:T(8,128)(2,1)S(1)}, u32[]{:S(2)}, u32[]{:S(2)}) collective-permute-start(bf16[64,2048]{1,0:T(8,128)(2,1)} %get-tuple-element.55), channel_id=1, source_target_pairs={{0,1},{1,2},{2,3},{3,0},{4,5},{5,6},{6,7},{7,4},{8,9},{9,10},{10,1... | collective-permute-start | bytes 786440 | tf_op jit(solution)/shard_map/ppermute | solution.py:567
  4.3 14.5 %collective-permute-start.2 = (bf16[64,2048]{1,0:T(8,128)(2,1)}, bf16[64,2048]{1,0:T(8,128)(2,1)S(1)}, u32[]{:S(2)}, u32[]{:S(2)}) collective-permute-start(bf16[64,2048]{1,0:T(8,128)(2,1)} %get-tuple-element.57), channel_id=1, source_target_pairs={{0,3},{1,0},{2,1},{3,2},{4,7},{5,4},{6,5},{7,6},{8,11},{9,8},{10,9... | collective-permute-start | bytes 786440 | tf_op jit(solution)/shard_map/ppermute | solution.py:567
  4.5 24.2 %collective-permute-start.1 = (bf16[64,2048]{1,0:T(8,128)(2,1)}, bf16[64,2048]{1,0:T(8,128)(2,1)S(1)}, u32[]{:S(2)}, u32[]{:S(2)}) collective-permute-start(bf16[64,2048]{1,0:T(8,128)(2,1)} %get-tuple-element.56), channel_id=1, source_target_pairs={{0,2},{1,3},{2,0},{3,1},{4,6},{5,7},{6,4},{7,5},{8,10},{9,11},{10,... | collective-permute-start | bytes 786440 | tf_op jit(solution)/shard_map/ppermute | solution.py:567
  18.9 28.6 %collective-permute-start.3 = (bf16[64,2048]{1,0:T(8,128)(2,1)}, bf16[64,2048]{1,0:T(8,128)(2,1)S(1)}, u32[]{:S(2)}, u32[]{:S(2)}) collective-permute-start(bf16[64,2048]{1,0:T(8,128)(2,1)} %get-tuple-element.66), channel_id=1, source_target_pairs={{0,1},{1,2},{2,3},{3,0},{4,5},{5,6},{6,7},{7,4},{8,9},{9,10},{10,1... | collective-permute-start | bytes 786440 | tf_op jit(solution)/shard_map/ppermute | solution.py:567
  18.9 30.1 %collective-permute-start.4 = (bf16[64,2048]{1,0:T(8,128)(2,1)}, bf16[64,2048]{1,0:T(8,128)(2,1)S(1)}, u32[]{:S(2)}, u32[]{:S(2)}) collective-permute-start(bf16[64,2048]{1,0:T(8,128)(2,1)} %get-tuple-element.67), channel_id=1, source_target_pairs={{0,2},{1,3},{2,0},{3,1},{4,6},{5,7},{6,4},{7,5},{8,10},{9,11},{10,... | collective-permute-start | bytes 786440 | tf_op jit(solution)/shard_map/ppermute | solution.py:567
  20.0 31.7 %collective-permute-start.5 = (bf16[64,2048]{1,0:T(8,128)(2,1)}, bf16[64,2048]{1,0:T(8,128)(2,1)S(1)}, u32[]{:S(2)}, u32[]{:S(2)}) collective-permute-start(bf16[64,2048]{1,0:T(8,128)(2,1)} %get-tuple-element.68), channel_id=1, source_target_pairs={{0,3},{1,0},{2,1},{3,2},{4,7},{5,4},{6,5},{7,6},{8,11},{9,8},{10,9... | collective-permute-start | bytes 786440 | tf_op jit(solution)/shard_map/ppermute | solution.py:567
  28.7 1.6 %copy-start.1 = (bf16[1,2048,512]{2,1,0:T(8,128)(2,1)S(1)}, bf16[1,2048,512]{2,1,0:T(8,128)(2,1)}, u32[]{:S(2)}) copy-start(bf16[1,2048,512]{2,1,0:T(8,128)(2,1)} %param.11) | copy-start | bytes 6291460
  30.3 0.9 copy-start.3
  31.2 20.5 %copy-start = (bf16[1,2048,1024]{2,1,0:T(8,128)(2,1)S(1)}, bf16[1,2048,1024]{2,1,0:T(8,128)(2,1)}, u32[]{:S(2)}) copy-start(bf16[1,2048,1024]{2,1,0:T(8,128)(2,1)} %param.10) | copy-start | bytes 12582916
  31.2 20.5 %copy-start.2 = (bf16[64,2048]{1,0:T(8,128)(2,1)S(1)}, bf16[64,2048]{1,0:T(8,128)(2,1)}, u32[]{:S(2)}) copy-start(bf16[64,2048]{1,0:T(8,128)(2,1)} %get-tuple-element.69.refs_0_) | copy-start | bytes 786436
  36.3 26.0 %collective-permute-start.6 = (bf16[64,2048]{1,0:T(8,128)(2,1)S(1)}, bf16[64,2048]{1,0:T(8,128)(2,1)S(1)}, u32[]{:S(2)}, u32[]{:S(2)}) collective-permute-start(bf16[64,2048]{1,0:T(8,128)(2,1)S(1)} %get-tuple-element.80.refs_3_), channel_id=1, source_target_pairs={{0,1},{1,2},{2,3},{3,0},{4,5},{5,6},{6,7},{7,4},{8,9},{9,10},{10,1... | collective-permute-start | bytes 786440 | tf_op jit(solution)/shard_map/ppermute | solution.py:567
  54.4 7.1 %collective-permute-start.7 = (bf16[8,256,768]{2,1,0:T(8,128)(2,1)S(1)}, bf16[8,256,768]{2,1,0:T(8,128)(2,1)S(1)}, u32[]{:S(2)}, u32[]{:S(2)}) collective-permute-start(bf16[8,256,768]{2,1,0:T(8,128)(2,1)S(1)} %get-tuple-element.74), channel_id=1, source_target_pairs={{0,4},{4,0},{8,12},{12,8},{16,20},{20,16},{24,28},{28,24},{1,5},{5... | collective-permute-start | bytes 9437192 | tf_op jit(solution)/shard_map/ppermute | solution.py:392
  56.4 40.2 %collective-permute-start.12 = (bf16[128,2048]{1,0:T(8,128)(2,1)S(1)}, bf16[128,2048]{1,0:T(8,128)(2,1)S(1)}, u32[]{:S(2)}, u32[]{:S(2)}) collective-permute-start(bf16[128,2048]{1,0:T(8,128)(2,1)S(1)} %get-tuple-element.98), channel_id=1, source_target_pairs={{0,2},{1,3},{2,0},{3,1},{4,6},{5,7},{6,4},{7,5},{8,10},{9,11},{10,... | collective-permute-start | bytes 1572872 | tf_op jit(solution)/shard_map/ppermute | solution.py:567
  58.9 38.6 %collective-permute-start.13 = (bf16[128,2048]{1,0:T(8,128)(2,1)S(1)}, bf16[128,2048]{1,0:T(8,128)(2,1)S(1)}, u32[]{:S(2)}, u32[]{:S(2)}) collective-permute-start(bf16[128,2048]{1,0:T(8,128)(2,1)S(1)} %get-tuple-element.99), channel_id=1, source_target_pairs={{0,3},{1,0},{2,1},{3,2},{4,7},{5,4},{6,5},{7,6},{8,11},{9,8},{10,9... | collective-permute-start | bytes 1572872 | tf_op jit(solution)/shard_map/ppermute | solution.py:567
  58.9 37.6 %collective-permute-start.14 = (bf16[64,2048]{1,0:T(8,128)(2,1)S(1)}, bf16[64,2048]{1,0:T(8,128)(2,1)S(1)}, u32[]{:S(2)}, u32[]{:S(2)}) collective-permute-start(bf16[64,2048]{1,0:T(8,128)(2,1)S(1)} %get-tuple-element.100), channel_id=1, source_target_pairs={{0,1},{1,2},{2,3},{3,0},{4,5},{5,6},{6,7},{7,4},{8,9},{9,10},{10,1... | collective-permute-start | bytes 786440 | tf_op jit(solution)/shard_map/ppermute | solution.py:567
  61.9 18.3 %collective-permute-start.8 = (bf16[2,256,768]{2,1,0:T(8,128)(2,1)S(1)}, bf16[2,256,768]{2,1,0:T(8,128)(2,1)S(1)}, u32[]{:S(2)}, u32[]{:S(2)}) collective-permute-start(bf16[2,256,768]{2,1,0:T(8,128)(2,1)S(1)} %get-tuple-element.85), channel_id=1, source_target_pairs={{0,8},{4,12},{8,0},{12,4},{16,24},{20,28},{24,16},{28,20},{1,9},{5... | collective-permute-start | bytes 2359304 | tf_op jit(solution)/shard_map/ppermute | solution.py:392
  62.2 17.9 %collective-permute-start.9 = (bf16[2,256,768]{2,1,0:T(8,128)(2,1)S(1)}, bf16[2,256,768]{2,1,0:T(8,128)(2,1)S(1)}, u32[]{:S(2)}, u32[]{:S(2)}) collective-permute-start(bf16[2,256,768]{2,1,0:T(8,128)(2,1)S(1)} %get-tuple-element.86), channel_id=1, source_target_pairs={{0,16},{4,20},{8,24},{12,28},{16,0},{20,4},{24,8},{28,12},{1,17},{... | collective-permute-start | bytes 2359304 | tf_op jit(solution)/shard_map/ppermute | solution.py:392
  80.5 8.6 %collective-permute-start.10 = (bf16[256,768]{1,0:T(8,128)(2,1)S(1)}, bf16[256,768]{1,0:T(8,128)(2,1)S(1)}, u32[]{:S(2)}, u32[]{:S(2)}) collective-permute-start(bf16[256,768]{1,0:T(8,128)(2,1)S(1)} %get-tuple-element.90), channel_id=1, source_target_pairs={{0,16},{4,20},{8,24},{12,28},{16,0},{20,4},{24,8},{28,12},{1,17},{... | collective-permute-start | bytes 1179656 | tf_op jit(solution)/shard_map/ppermute | solution.py:392
  81.8 1.4 %copy-start.4 = (s32[128,2]{0,1:T(2,128)S(1)}, s32[128,2]{0,1:T(2,128)}, u32[]{:S(2)}) copy-start(s32[128,2]{0,1:T(2,128)} %param.7) | copy-start | bytes 3076
  81.8 1.4 %copy-start.5 = (f32[128,2]{0,1:T(2,128)S(1)}, f32[128,2]{0,1:T(2,128)}, u32[]{:S(2)}) copy-start(f32[128,2]{0,1:T(2,128)} %param.8) | copy-start | bytes 3076
  81.8 8.3 %collective-permute-start.11 = (bf16[256,768]{1,0:T(8,128)(2,1)S(1)}, bf16[256,768]{1,0:T(8,128)(2,1)S(1)}, u32[]{:S(2)}, u32[]{:S(2)}) collective-permute-start(bf16[256,768]{1,0:T(8,128)(2,1)S(1)} %get-tuple-element.92), channel_id=1, source_target_pairs={{0,8},{4,12},{8,0},{12,4},{16,24},{20,28},{24,16},{28,20},{1,9},{5... | collective-permute-start | bytes 1179656 | tf_op jit(solution)/shard_map/ppermute | solution.py:392

commit v4 on v3

--- a/solution.py
+++ b/solution.py
@@ -62,8 +62,8 @@
         start += size
 
 
-def column_steps(width):
-    step = 512 if width % 512 == 0 else width
+def column_steps(width, step=512):
+    step = step if width % step == 0 else width
     return [slice(at, at + step) for at in range(0, width, step)]
 
 
@@ -94,7 +94,7 @@
         )
     copies[-1].wait()
     stores = []
-    for c, columns in enumerate(column_steps(values.shape[1])):
+    for c, columns in enumerate(column_steps(values.shape[1], 1024)):
         rows = jnp.dot(picker, values[:, columns], preferred_element_type=F32)
         if weighted:
             rows = rows * scale
@@ -527,7 +527,7 @@
         + [pltpu.VMEM(source.shape, source.dtype) for source in sources]
         + [
             pltpu.SemaphoreType.DMA((len(sources),)),
-            pltpu.SemaphoreType.DMA((len(column_steps(out_shape[0].shape[1])), len(out_shape))),
+            pltpu.SemaphoreType.DMA((len(column_steps(out_shape[0].shape[1], 1024)), len(out_shape))),
         ],
         compiler_params=ALONE,
         cost_estimate=BRIEF,

time: 99.1 us -> 99.1 us (level)
  no operation moved by 1% of the time
where the time goes in v4:
time: 99.1 us; the launch traced here: 98.9 us
  waiting for transfers between devices  49.9 us (50%)
  starting transfers between devices  25.1 us (25%)
  Pallas kernels  20.4 us (21%)
  local copies, waits for them, and re-layouts  2.72 us (3%)
    ppermute x10, waiting for transfers between devices, travel(): return lax.ppermute(block, 'expert', pairs)  28.3 us
    ppermute x5, waiting for transfers between devices, swap(): lax.ppermute(block, 'dp', [(at, at ^ bit) for at in range(lax.axis_size('...  21.7 us
    ppermute x10, starting transfers between devices, travel(): return lax.ppermute(block, 'expert', pairs)  20.5 us
    pallas_call x1, Pallas kernels, forward(): pl.pallas_call(functools.partial(forward_kernel, count), out_shape=(jax.S...  5.04 us
    pallas_call x2, Pallas kernels, dispatch(): pl.pallas_call(functools.partial(dispatch_kernel, experts, capacity, weig...  4.72 us
    ppermute x5, starting transfers between devices, swap(): lax.ppermute(block, 'dp', [(at, at ^ bit) for at in range(lax.axis_size('...  4.6 us
    pallas_call x1, Pallas kernels, backward(): pl.pallas_call(functools.partial(backward_kernel, count), out_shape=(jax....  2.74 us
    unnamed x12, local copies, waits for them, and re-layouts  2.55 us
  transfers between devices with their start and end apart: 15, of which 10 were waited for; matrix products, arithmetic and copies ran while one was open for 0% of the time, Pallas kernels for 17%

profile of v4, /device:TPU:11, one launch (start us, length us, event | category | flops | bytes accessed | tf_op | source)
XLA Modules:
  0.0 98.9 jit_solution(14308626727077409505)
XLA Ops:
  0.6 2.3 %shard_map.93 = (bf16[64,2048]{1,0:T(8,128)(2,1)}, bf16[64,2048]{1,0:T(8,128)(2,1)}, bf16[64,2048]{1,0:T(8,128)(2,1)}, bf16[64,2048]{1,0:T(8,128)(2,1)}) custom-call(s32[1]{0:T(128)} %bitcast.first, s32[2,128]{1,0:T(2,128)} %bitcast.15, bf16[128,2048]{1,0:T(8,128)(2,1)} %refs_1_.1), custom_call_target="tpu_custom_call" | custom-call | flops 1024 | bytes 1024 | tf_op jit(solution)/shard_map/pallas_call | solution.py:521
  3.0 1.3 %collective-permute-start = (bf16[64,2048]{1,0:T(8,128)(2,1)}, bf16[64,2048]{1,0:T(8,128)(2,1)S(1)}, u32[]{:S(2)}, u32[]{:S(2)}) collective-permute-start(bf16[64,2048]{1,0:T(8,128)(2,1)} %get-tuple-element.55), channel_id=1, source_target_pairs={{0,1},{1,2},{2,3},{3,0},{4,5},{5,6},{6,7},{7,4},{8,9},{9,10},{10,1... | collective-permute-start | bytes 786440 | tf_op jit(solution)/shard_map/ppermute | solution.py:567
  4.3 0.2 collective-permute-start.2
  4.5 2.3 %collective-permute-start.1 = (bf16[64,2048]{1,0:T(8,128)(2,1)}, bf16[64,2048]{1,0:T(8,128)(2,1)S(1)}, u32[]{:S(2)}, u32[]{:S(2)}) collective-permute-start(bf16[64,2048]{1,0:T(8,128)(2,1)} %get-tuple-element.56), channel_id=1, source_target_pairs={{0,2},{1,3},{2,0},{3,1},{4,6},{5,7},{6,4},{7,5},{8,10},{9,11},{10,... | collective-permute-start | bytes 786440 | tf_op jit(solution)/shard_map/ppermute | solution.py:567
  6.8 2.4 %shard_map.95 = (bf16[64,2048]{1,0:T(8,128)(2,1)}, bf16[64,2048]{1,0:T(8,128)(2,1)}, bf16[64,2048]{1,0:T(8,128)(2,1)}, bf16[64,2048]{1,0:T(8,128)(2,1)}) custom-call(s32[1]{0:T(128)} %bitcast.first, s32[2,128]{1,0:T(2,128)} %bitcast.16, f32[2,128]{1,0:T(2,128)} %bitcast.18, bf16[128,2048]{1,0:T(8,128)(2,1)} %refs_2_.1), custom_call_target="tpu_custom_call" | custom-call | flops 1024 | bytes 1024 | tf_op jit(solution)/shard_map/pallas_call | solution.py:521
  9.2 0.1 stack.23.at
  9.3 1.1 %collective-permute-done.refs_1_ = bf16[64,2048]{1,0:T(8,128)(2,1)S(1)} collective-permute-done((bf16[64,2048]{1,0:T(8,128)(2,1)}, bf16[64,2048]{1,0:T(8,128)(2,1)S(1)}, u32[]{:S(2)}, u32[]{:S(2)}) %collective-permute-start) | collective-permute-done | bytes 262176 | tf_op jit(solution)/shard_map/ppermute | solution.py:567
  10.4 8.5 %collective-permute-done.2.refs_3_ = bf16[64,2048]{1,0:T(8,128)(2,1)S(1)} collective-permute-done((bf16[64,2048]{1,0:T(8,128)(2,1)}, bf16[64,2048]{1,0:T(8,128)(2,1)S(1)}, u32[]{:S(2)}, u32[]{:S(2)}) %collective-permute-start.2) | collective-permute-done | bytes 262176 | tf_op jit(solution)/shard_map/ppermute | solution.py:567
  18.9 0.0 collective-permute-start.3
  18.9 1.1 %collective-permute-start.4 = (bf16[64,2048]{1,0:T(8,128)(2,1)}, bf16[64,2048]{1,0:T(8,128)(2,1)S(1)}, u32[]{:S(2)}, u32[]{:S(2)}) collective-permute-start(bf16[64,2048]{1,0:T(8,128)(2,1)} %get-tuple-element.67), channel_id=1, source_target_pairs={{0,2},{1,3},{2,0},{3,1},{4,6},{5,7},{6,4},{7,5},{8,10},{9,11},{10,... | collective-permute-start | bytes 786440 | tf_op jit(solution)/shard_map/ppermute | solution.py:567
  20.0 0.3 collective-permute-start.5
  20.3 0.1 fusion
  20.4 8.3 %collective-permute-done.1.refs_2_ = bf16[64,2048]{1,0:T(8,128)(2,1)S(1)} collective-permute-done((bf16[64,2048]{1,0:T(8,128)(2,1)}, bf16[64,2048]{1,0:T(8,128)(2,1)S(1)}, u32[]{:S(2)}, u32[]{:S(2)}) %collective-permute-start.1) | collective-permute-done | bytes 262176 | tf_op jit(solution)/shard_map/ppermute | solution.py:567
  28.7 1.6 %copy-done.1 = bf16[1,2048,512]{2,1,0:T(8,128)(2,1)S(1)} copy-done((bf16[1,2048,512]{2,1,0:T(8,128)(2,1)S(1)}, bf16[1,2048,512]{2,1,0:T(8,128)(2,1)}, u32[]{:S(2)}) %copy-start.1) | copy-done | bytes 2097176
  30.3 0.9 copy-done.3
  31.2 5.0 %shard_map.94 = (bf16[2048,256]{1,0:T(8,128)(2,1)S(1)}, f32[256,1024]{1,0:T(8,128)S(1)}, bf16[256,512]{1,0:T(8,128)(2,1)S(1)}, bf16[64,2048]{1,0:T(8,128)(2,1)S(...) custom-call(bf16[64,2048]{1,0:T(8,128)(2,1)S(1)} %copy-done.3, ...), custom_call_target="tpu_custom_call" | custom-call | flops 1024 | bytes 1024 | tf_op jit(solution)/shard_map/pallas_call | solution.py:234
  36.3 11.2 %collective-permute-start.6 = (bf16[64,2048]{1,0:T(8,128)(2,1)S(1)}, bf16[64,2048]{1,0:T(8,128)(2,1)S(1)}, u32[]{:S(2)}, u32[]{:S(2)}) collective-permute-start(bf16[64,2048]{1,0:T(8,128)(2,1)S(1)} %get-tuple-element.80.refs_3_), channel_id=1, source_target_pairs={{0,1},{1,2},{2,3},{3,0},{4,5},{5,6},{6,7},{7,4},{8,9},{9,10},{10,1... | collective-permute-start | bytes 786440 | tf_op jit(solution)/shard_map/ppermute | solution.py:567
  47.5 0.0 collective-permute-done.3.refs_1_
  47.5 1.5 %collective-permute-done.4.refs_2_ = bf16[64,2048]{1,0:T(8,128)(2,1)S(1)} collective-permute-done((bf16[64,2048]{1,0:T(8,128)(2,1)}, bf16[64,2048]{1,0:T(8,128)(2,1)S(1)}, u32[]{:S(2)}, u32[]{:S(2)}) %collective-permute-start.4) | collective-permute-done | bytes 262176 | tf_op jit(solution)/shard_map/ppermute | solution.py:567
  49.0 2.7 %collective-permute-done.5.refs_3_ = bf16[64,2048]{1,0:T(8,128)(2,1)S(1)} collective-permute-done((bf16[64,2048]{1,0:T(8,128)(2,1)}, bf16[64,2048]{1,0:T(8,128)(2,1)S(1)}, u32[]{:S(2)}, u32[]{:S(2)}) %collective-permute-start.5) | collective-permute-done | bytes 262176 | tf_op jit(solution)/shard_map/ppermute | solution.py:567
  51.7 0.0 copy-done
  51.7 2.7 %shard_map.96 = (bf16[256,1024]{1,0:T(8,128)(2,1)S(1)}, bf16[2048,256]{1,0:T(8,128)(2,1)S(1)}, bf16[8,256,768]{2,1,0:T(8,128)(2,1)S(1)}, bf16[2048,1024]{1,0:T(8,128)(2,1)S(1)}) custom-call(s32[8]{0:T(128)S(1)} %stack.23.at, f32[256,1024]{1,0:T(8,128)S(1)} %get-tuple-element.58.preact_hbm, bf16[2048,1024]{1,0:T(8,128)(2,1)S(1)} %bitcast.12, ...), custom_call_target="tpu_custom_call" | custom-call | flops 1024 | bytes 1024 | tf_op jit(solution)/shard_map/pallas_call | solution.py:332
  54.4 0.6 collective-permute-start.7
  55.0 1.4 %shard_map.97 = (bf16[128,2048]{1,0:T(8,128)(2,1)S(1)}, bf16[128,2048]{1,0:T(8,128)(2,1)S(1)}, bf16[128,2048]{1,0:T(8,128)(2,1)S(1)}, bf16[64,2048]{1,0:T(8,128)(2,1)S(1)}) custom-call(bf16[256,1024]{1,0:T(8,128)(2,1)S(1)} %get-tuple-element.75.pre_grad, bf16[2048,1024]{1,0:T(8,128)(2,1)S(1)} %get-tuple-element.76.w_in, ...), custom_call_target="tpu_custom_call" | custom-call | flops 1024 | bytes 1024 | tf_op jit(solution)/shard_map/pallas_call | solution.py:306
  56.4 2.6 %collective-permute-start.12 = (bf16[128,2048]{1,0:T(8,128)(2,1)S(1)}, bf16[128,2048]{1,0:T(8,128)(2,1)S(1)}, u32[]{:S(2)}, u32[]{:S(2)}) collective-permute-start(bf16[128,2048]{1,0:T(8,128)(2,1)S(1)} %get-tuple-element.98), channel_id=1, source_target_pairs={{0,2},{1,3},{2,0},{3,1},{4,6},{5,7},{6,4},{7,5},{8,10},{9,11},{10,... | collective-permute-start | bytes 1572872 | tf_op jit(solution)/shard_map/ppermute | solution.py:567
  58.9 0.0 collective-permute-start.13
  58.9 1.5 %collective-permute-start.14 = (bf16[64,2048]{1,0:T(8,128)(2,1)S(1)}, bf16[64,2048]{1,0:T(8,128)(2,1)S(1)}, u32[]{:S(2)}, u32[]{:S(2)}) collective-permute-start(bf16[64,2048]{1,0:T(8,128)(2,1)S(1)} %get-tuple-element.100), channel_id=1, source_target_pairs={{0,1},{1,2},{2,3},{3,0},{4,5},{5,6},{6,7},{7,4},{8,9},{9,10},{10,1... | collective-permute-start | bytes 786440 | tf_op jit(solution)/shard_map/ppermute | solution.py:567
  60.4 1.1 %shard_map.98.kept = bf16[4,256,768]{2,1,0:T(8,128)(2,1)S(1)} custom-call(s32[4]{0:T(128)S(1)} %get-tuple-element.82.at, bf16[2048,256]{1,0:T(8,128)(2,1)S(1)} %get-tuple-element.59.rows_t, bf16[2048,256]{1,0:T(8,128)(2,1)S(1)} %get-tuple-element.83.grads_t, bf16[256,1024]{1,0:T(8,128)(2,1)S(1)} %get-tuple-element.75.pre_grad, ...), custom_call_target="tpu_custom_call" | custom-call | flops 40000000000 | bytes 1024 | tf_op jit(solution)/shard_map/pallas_call | solution.py:356
  61.5 0.0 collective-permute-done.7.got
  61.5 0.4 shard_map.100
  61.9 0.3 collective-permute-start.8
  62.2 0.0 collective-permute-done.6.refs_1_
  62.2 1.2 %collective-permute-start.9 = (bf16[2,256,768]{2,1,0:T(8,128)(2,1)S(1)}, bf16[2,256,768]{2,1,0:T(8,128)(2,1)S(1)}, u32[]{:S(2)}, u32[]{:S(2)}) collective-permute-start(bf16[2,256,768]{2,1,0:T(8,128)(2,1)S(1)} %get-tuple-element.86), channel_id=1, source_target_pairs={{0,16},{4,20},{8,24},{12,28},{16,0},{20,4},{24,8},{28,12},{1,17},{... | collective-permute-start | bytes 2359304 | tf_op jit(solution)/shard_map/ppermute | solution.py:392
  63.5 1.1 %shard_map.99.kept = bf16[4,256,768]{2,1,0:T(8,128)(2,1)S(1)} custom-call(s32[4]{0:T(128)S(1)} %get-tuple-element.84.at, bf16[2048,256]{1,0:T(8,128)(2,1)S(1)} %get-tuple-element.59.rows_t, bf16[2048,256]{1,0:T(8,128)(2,1)S(1)} %get-tuple-element.83.grads_t, bf16[256,1024]{1,0:T(8,128)(2,1)S(1)} %get-tuple-element.75.pre_grad, ...), custom_call_target="tpu_custom_call" | custom-call | flops 40000000000 | bytes 1024 | tf_op jit(solution)/shard_map/pallas_call | solution.py:356
  64.6 15.6 %collective-permute-done.8.left_in = bf16[2,256,768]{2,1,0:T(8,128)(2,1)S(1)} collective-permute-done((bf16[2,256,768]{2,1,0:T(8,128)(2,1)S(1)}, bf16[2,256,768]{2,1,0:T(8,128)(2,1)S(1)}, u32[]{:S(2)}, u32[]{:S(2)}) %collective-permute-start.8) | collective-permute-done | bytes 786464 | tf_op jit(solution)/shard_map/ppermute | solution.py:392
  80.2 0.0 collective-permute-done.9.right_in
  80.2 0.3 shard_map.103
  80.5 1.3 %collective-permute-start.10 = (bf16[256,768]{1,0:T(8,128)(2,1)S(1)}, bf16[256,768]{1,0:T(8,128)(2,1)S(1)}, u32[]{:S(2)}, u32[]{:S(2)}) collective-permute-start(bf16[256,768]{1,0:T(8,128)(2,1)S(1)} %get-tuple-element.90), channel_id=1, source_target_pairs={{0,16},{4,20},{8,24},{12,28},{16,0},{20,4},{24,8},{28,12},{1,17},{... | collective-permute-start | bytes 1179656 | tf_op jit(solution)/shard_map/ppermute | solution.py:392
  81.8 1.2 %collective-permute-start.11 = (bf16[256,768]{1,0:T(8,128)(2,1)S(1)}, bf16[256,768]{1,0:T(8,128)(2,1)S(1)}, u32[]{:S(2)}, u32[]{:S(2)}) collective-permute-start(bf16[256,768]{1,0:T(8,128)(2,1)S(1)} %get-tuple-element.92), channel_id=1, source_target_pairs={{0,8},{4,12},{8,0},{12,4},{16,24},{20,28},{24,16},{28,20},{1,9},{5... | collective-permute-start | bytes 1179656 | tf_op jit(solution)/shard_map/ppermute | solution.py:392
  83.0 0.3 shard_map.101
  83.2 0.8 shard_map.102
  84.0 5.1 %collective-permute-done.10.left_last = bf16[256,768]{1,0:T(8,128)(2,1)S(1)} collective-permute-done((bf16[256,768]{1,0:T(8,128)(2,1)S(1)}, bf16[256,768]{1,0:T(8,128)(2,1)S(1)}, u32[]{:S(2)}, u32[]{:S(2)}) %collective-permute-start.10) | collective-permute-done | bytes 393248 | tf_op jit(solution)/shard_map/ppermute | solution.py:392
  89.1 1.0 collective-permute-done.11.right_last
  90.1 1.3 %shard_map.104 = (f32[256,1024]{1,0:T(8,128)}, f32[256,512]{1,0:T(8,128)}) custom-call(f32[256,768]{1,0:T(8,128)S(1)} %get-tuple-element.87.left, bf16[256,768]{1,0:T(8,128)(2,1)S(1)} %collective-permute-done.10.left_last, f32[256,768]{1,0:T(8,128)S(1)} %get-tuple-element.91.right, bf16[256,768]{1,0:T(8,128)(2,1)S(1)} %collective-permute-done.11.right_last), custom_call_target="tpu_custom_call" | custom-call | flops 1024 | bytes 1024 | tf_op jit(solution)/shard_map/pallas_call | solution.py:467
  91.4 5.2 %collective-permute-done.14.refs_2_ = bf16[64,2048]{1,0:T(8,128)(2,1)S(1)} collective-permute-done((bf16[64,2048]{1,0:T(8,128)(2,1)S(1)}, bf16[64,2048]{1,0:T(8,128)(2,1)S(1)}, u32[]{:S(2)}, u32[]{:S(2)}) %collective-permute-start.14) | collective-permute-done | bytes 262176 | tf_op jit(solution)/shard_map/ppermute | solution.py:567
  96.6 0.0 collective-permute-done.12.refs_0_
  96.6 1.0 collective-permute-done.13.refs_1_
  97.6 1.3 %shard_map.105 = (bf16[128,2048]{1,0:T(8,128)(2,1)}, bf16[128,2048]{1,0:T(8,128)(2,1)}) custom-call(bf16[384,192]{1,0:T(8,128)(2,1)S(1)} %get-tuple-element.94.picker, f32[2,128,128]{2,1,0:T(8,128)S(1)} %get-tuple-element.95.scales, f32[128,2048]{1,0:T(8,128)S(1)} %get-tuple-element.96.mixed_part, f32[128,2048]{1,0:T(8,128)S(1)} %get-tuple-element.97.back_part, ...), custom_call_target="tpu_custom_call" | custom-call | flops 1024 | bytes 1024 | tf_op jit(solution)/shard_map/pallas_call | solution.py:507
  (10 shorter events, 0.0 us)
Async XLA Ops:
  3.0 7.4 %collective-permute-start = (bf16[64,2048]{1,0:T(8,128)(2,1)}, bf16[64,2048]{1,0:T(8,128)(2,1)S(1)}, u32[]{:S(2)}, u32[]{:S(2)}) collective-permute-start(bf16[64,2048]{1,0:T(8,128)(2,1)} %get-tuple-element.55), channel_id=1, source_target_pairs={{0,1},{1,2},{2,3},{3,0},{4,5},{5,6},{6,7},{7,4},{8,9},{9,10},{10,1... | collective-permute-start | bytes 786440 | tf_op jit(solution)/shard_map/ppermute | solution.py:567
  4.3 14.5 %collective-permute-start.2 = (bf16[64,2048]{1,0:T(8,128)(2,1)}, bf16[64,2048]{1,0:T(8,128)(2,1)S(1)}, u32[]{:S(2)}, u32[]{:S(2)}) collective-permute-start(bf16[64,2048]{1,0:T(8,128)(2,1)} %get-tuple-element.57), channel_id=1, source_target_pairs={{0,3},{1,0},{2,1},{3,2},{4,7},{5,4},{6,5},{7,6},{8,11},{9,8},{10,9... | collective-permute-start | bytes 786440 | tf_op jit(solution)/shard_map/ppermute | solution.py:567
  4.5 24.2 %collective-permute-start.1 = (bf16[64,2048]{1,0:T(8,128)(2,1)}, bf16[64,2048]{1,0:T(8,128)(2,1)S(1)}, u32[]{:S(2)}, u32[]{:S(2)}) collective-permute-start(bf16[64,2048]{1,0:T(8,128)(2,1)} %get-tuple-element.56), channel_id=1, source_target_pairs={{0,2},{1,3},{2,0},{3,1},{4,6},{5,7},{6,4},{7,5},{8,10},{9,11},{10,... | collective-permute-start | bytes 786440 | tf_op jit(solution)/shard_map/ppermute | solution.py:567
  18.9 28.6 %collective-permute-start.3 = (bf16[64,2048]{1,0:T(8,128)(2,1)}, bf16[64,2048]{1,0:T(8,128)(2,1)S(1)}, u32[]{:S(2)}, u32[]{:S(2)}) collective-permute-start(bf16[64,2048]{1,0:T(8,128)(2,1)} %get-tuple-element.66), channel_id=1, source_target_pairs={{0,1},{1,2},{2,3},{3,0},{4,5},{5,6},{6,7},{7,4},{8,9},{9,10},{10,1... | collective-permute-start | bytes 786440 | tf_op jit(solution)/shard_map/ppermute | solution.py:567
  18.9 30.1 %collective-permute-start.4 = (bf16[64,2048]{1,0:T(8,128)(2,1)}, bf16[64,2048]{1,0:T(8,128)(2,1)S(1)}, u32[]{:S(2)}, u32[]{:S(2)}) collective-permute-start(bf16[64,2048]{1,0:T(8,128)(2,1)} %get-tuple-element.67), channel_id=1, source_target_pairs={{0,2},{1,3},{2,0},{3,1},{4,6},{5,7},{6,4},{7,5},{8,10},{9,11},{10,... | collective-permute-start | bytes 786440 | tf_op jit(solution)/shard_map/ppermute | solution.py:567
  20.0 31.7 %collective-permute-start.5 = (bf16[64,2048]{1,0:T(8,128)(2,1)}, bf16[64,2048]{1,0:T(8,128)(2,1)S(1)}, u32[]{:S(2)}, u32[]{:S(2)}) collective-permute-start(bf16[64,2048]{1,0:T(8,128)(2,1)} %get-tuple-element.68), channel_id=1, source_target_pairs={{0,3},{1,0},{2,1},{3,2},{4,7},{5,4},{6,5},{7,6},{8,11},{9,8},{10,9... | collective-permute-start | bytes 786440 | tf_op jit(solution)/shard_map/ppermute | solution.py:567
  28.7 1.6 %copy-start.1 = (bf16[1,2048,512]{2,1,0:T(8,128)(2,1)S(1)}, bf16[1,2048,512]{2,1,0:T(8,128)(2,1)}, u32[]{:S(2)}) copy-start(bf16[1,2048,512]{2,1,0:T(8,128)(2,1)} %param.11) | copy-start | bytes 6291460
  30.3 0.9 copy-start.3
  31.2 20.5 %copy-start = (bf16[1,2048,1024]{2,1,0:T(8,128)(2,1)S(1)}, bf16[1,2048,1024]{2,1,0:T(8,128)(2,1)}, u32[]{:S(2)}) copy-start(bf16[1,2048,1024]{2,1,0:T(8,128)(2,1)} %param.10) | copy-start | bytes 12582916
  31.2 20.5 %copy-start.2 = (bf16[64,2048]{1,0:T(8,128)(2,1)S(1)}, bf16[64,2048]{1,0:T(8,128)(2,1)}, u32[]{:S(2)}) copy-start(bf16[64,2048]{1,0:T(8,128)(2,1)} %get-tuple-element.69.refs_0_) | copy-start | bytes 786436
  36.3 26.0 %collective-permute-start.6 = (bf16[64,2048]{1,0:T(8,128)(2,1)S(1)}, bf16[64,2048]{1,0:T(8,128)(2,1)S(1)}, u32[]{:S(2)}, u32[]{:S(2)}) collective-permute-start(bf16[64,2048]{1,0:T(8,128)(2,1)S(1)} %get-tuple-element.80.refs_3_), channel_id=1, source_target_pairs={{0,1},{1,2},{2,3},{3,0},{4,5},{5,6},{6,7},{7,4},{8,9},{9,10},{10,1... | collective-permute-start | bytes 786440 | tf_op jit(solution)/shard_map/ppermute | solution.py:567
  54.4 7.1 %collective-permute-start.7 = (bf16[8,256,768]{2,1,0:T(8,128)(2,1)S(1)}, bf16[8,256,768]{2,1,0:T(8,128)(2,1)S(1)}, u32[]{:S(2)}, u32[]{:S(2)}) collective-permute-start(bf16[8,256,768]{2,1,0:T(8,128)(2,1)S(1)} %get-tuple-element.74), channel_id=1, source_target_pairs={{0,4},{4,0},{8,12},{12,8},{16,20},{20,16},{24,28},{28,24},{1,5},{5... | collective-permute-start | bytes 9437192 | tf_op jit(solution)/shard_map/ppermute | solution.py:392
  56.4 40.2 %collective-permute-start.12 = (bf16[128,2048]{1,0:T(8,128)(2,1)S(1)}, bf16[128,2048]{1,0:T(8,128)(2,1)S(1)}, u32[]{:S(2)}, u32[]{:S(2)}) collective-permute-start(bf16[128,2048]{1,0:T(8,128)(2,1)S(1)} %get-tuple-element.98), channel_id=1, source_target_pairs={{0,2},{1,3},{2,0},{3,1},{4,6},{5,7},{6,4},{7,5},{8,10},{9,11},{10,... | collective-permute-start | bytes 1572872 | tf_op jit(solution)/shard_map/ppermute | solution.py:567
  58.9 38.6 %collective-permute-start.13 = (bf16[128,2048]{1,0:T(8,128)(2,1)S(1)}, bf16[128,2048]{1,0:T(8,128)(2,1)S(1)}, u32[]{:S(2)}, u32[]{:S(2)}) collective-permute-start(bf16[128,2048]{1,0:T(8,128)(2,1)S(1)} %get-tuple-element.99), channel_id=1, source_target_pairs={{0,3},{1,0},{2,1},{3,2},{4,7},{5,4},{6,5},{7,6},{8,11},{9,8},{10,9... | collective-permute-start | bytes 1572872 | tf_op jit(solution)/shard_map/ppermute | solution.py:567
  58.9 37.6 %collective-permute-start.14 = (bf16[64,2048]{1,0:T(8,128)(2,1)S(1)}, bf16[64,2048]{1,0:T(8,128)(2,1)S(1)}, u32[]{:S(2)}, u32[]{:S(2)}) collective-permute-start(bf16[64,2048]{1,0:T(8,128)(2,1)S(1)} %get-tuple-element.100), channel_id=1, source_target_pairs={{0,1},{1,2},{2,3},{3,0},{4,5},{5,6},{6,7},{7,4},{8,9},{9,10},{10,1... | collective-permute-start | bytes 786440 | tf_op jit(solution)/shard_map/ppermute | solution.py:567
  61.9 18.3 %collective-permute-start.8 = (bf16[2,256,768]{2,1,0:T(8,128)(2,1)S(1)}, bf16[2,256,768]{2,1,0:T(8,128)(2,1)S(1)}, u32[]{:S(2)}, u32[]{:S(2)}) collective-permute-start(bf16[2,256,768]{2,1,0:T(8,128)(2,1)S(1)} %get-tuple-element.85), channel_id=1, source_target_pairs={{0,8},{4,12},{8,0},{12,4},{16,24},{20,28},{24,16},{28,20},{1,9},{5... | collective-permute-start | bytes 2359304 | tf_op jit(solution)/shard_map/ppermute | solution.py:392
  62.2 17.9 %collective-permute-start.9 = (bf16[2,256,768]{2,1,0:T(8,128)(2,1)S(1)}, bf16[2,256,768]{2,1,0:T(8,128)(2,1)S(1)}, u32[]{:S(2)}, u32[]{:S(2)}) collective-permute-start(bf16[2,256,768]{2,1,0:T(8,128)(2,1)S(1)} %get-tuple-element.86), channel_id=1, source_target_pairs={{0,16},{4,20},{8,24},{12,28},{16,0},{20,4},{24,8},{28,12},{1,17},{... | collective-permute-start | bytes 2359304 | tf_op jit(solution)/shard_map/ppermute | solution.py:392
  80.5 8.7 %collective-permute-start.10 = (bf16[256,768]{1,0:T(8,128)(2,1)S(1)}, bf16[256,768]{1,0:T(8,128)(2,1)S(1)}, u32[]{:S(2)}, u32[]{:S(2)}) collective-permute-start(bf16[256,768]{1,0:T(8,128)(2,1)S(1)} %get-tuple-element.90), channel_id=1, source_target_pairs={{0,16},{4,20},{8,24},{12,28},{16,0},{20,4},{24,8},{28,12},{1,17},{... | collective-permute-start | bytes 1179656 | tf_op jit(solution)/shard_map/ppermute | solution.py:392
  81.8 1.4 %copy-start.4 = (s32[128,2]{0,1:T(2,128)S(1)}, s32[128,2]{0,1:T(2,128)}, u32[]{:S(2)}) copy-start(s32[128,2]{0,1:T(2,128)} %param.7) | copy-start | bytes 3076
  81.8 1.4 %copy-start.5 = (f32[128,2]{0,1:T(2,128)S(1)}, f32[128,2]{0,1:T(2,128)}, u32[]{:S(2)}) copy-start(f32[128,2]{0,1:T(2,128)} %param.8) | copy-start | bytes 3076
  81.8 8.3 %collective-permute-start.11 = (bf16[256,768]{1,0:T(8,128)(2,1)S(1)}, bf16[256,768]{1,0:T(8,128)(2,1)S(1)}, u32[]{:S(2)}, u32[]{:S(2)}) collective-permute-start(bf16[256,768]{1,0:T(8,128)(2,1)S(1)} %get-tuple-element.92), channel_id=1, source_target_pairs={{0,8},{4,12},{8,0},{12,4},{16,24},{20,28},{24,16},{28,20},{1,9},{5... | collective-permute-start | bytes 1179656 | tf_op jit(solution)/shard_map/ppermute | solution.py:392

commit v5 on v4

--- a/solution.py
+++ b/solution.py
@@ -484,7 +484,7 @@
         refs[number + 2 :],
     )
     stores = []
-    for c, columns in enumerate(column_steps(mixed.shape[1])):
+    for c, columns in enumerate(column_steps(mixed.shape[1], 1024)):
         outputs = jnp.concatenate([block[:capacity, columns] for block in blocks[:-1]], axis=0)
         gradients = jnp.concatenate(
             [block[block.shape[0] - capacity :, columns] for block in blocks], axis=0
@@ -510,7 +510,7 @@
         in_specs=whole(4 + len(blocks)),
         out_specs=anywhere(2),
         scratch_shapes=[pltpu.VMEM((toks, width), BF16)] * 2
-        + [pltpu.SemaphoreType.DMA((len(column_steps(width)), 2))],
+        + [pltpu.SemaphoreType.DMA((len(column_steps(width, 1024)), 2))],
         compiler_params=ROOMY,
         cost_estimate=BRIEF,
     )(*parts, *blocks)

time: 99.1 us -> 99.1 us (level)
  no operation moved by 1% of the time
where the time goes in v5:
time: 99.1 us; the launch traced here: 98.9 us
  waiting for transfers between devices  49.9 us (50%)
  starting transfers between devices  25.1 us (25%)
  Pallas kernels  20.4 us (21%)
  local copies, waits for them, and re-layouts  2.72 us (3%)
    ppermute x10, waiting for transfers between devices, travel(): return lax.ppermute(block, 'expert', pairs)  28.3 us
    ppermute x5, waiting for transfers between devices, swap(): lax.ppermute(block, 'dp', [(at, at ^ bit) for at in range(lax.axis_size('...  21.7 us
    ppermute x10, starting transfers between devices, travel(): return lax.ppermute(block, 'expert', pairs)  20.5 us
    pallas_call x1, Pallas kernels, forward(): pl.pallas_call(functools.partial(forward_kernel, count), out_shape=(jax.S...  5.04 us
    pallas_call x2, Pallas kernels, dispatch(): pl.pallas_call(functools.partial(dispatch_kernel, experts, capacity, weig...  4.72 us
    ppermute x5, starting transfers between devices, swap(): lax.ppermute(block, 'dp', [(at, at ^ bit) for at in range(lax.axis_size('...  4.6 us
    pallas_call x1, Pallas kernels, backward(): pl.pallas_call(functools.partial(backward_kernel, count), out_shape=(jax....  2.74 us
    unnamed x12, local copies, waits for them, and re-layouts  2.55 us
  transfers between devices with their start and end apart: 15, of which 10 were waited for; matrix products, arithmetic and copies ran while one was open for 0% of the time, Pallas kernels for 17%

profile of v5, /device:TPU:11, one launch (start us, length us, event | category | flops | bytes accessed | tf_op | source)
XLA Modules:
  0.0 98.9 jit_solution(16688830974501902533)
XLA Ops:
  0.6 2.3 %shard_map.93 = (bf16[64,2048]{1,0:T(8,128)(2,1)}, bf16[64,2048]{1,0:T(8,128)(2,1)}, bf16[64,2048]{1,0:T(8,128)(2,1)}, bf16[64,2048]{1,0:T(8,128)(2,1)}) custom-call(s32[1]{0:T(128)} %bitcast.first, s32[2,128]{1,0:T(2,128)} %bitcast.15, bf16[128,2048]{1,0:T(8,128)(2,1)} %refs_1_.1), custom_call_target="tpu_custom_call" | custom-call | flops 1024 | bytes 1024 | tf_op jit(solution)/shard_map/pallas_call | solution.py:521
  3.0 1.3 %collective-permute-start = (bf16[64,2048]{1,0:T(8,128)(2,1)}, bf16[64,2048]{1,0:T(8,128)(2,1)S(1)}, u32[]{:S(2)}, u32[]{:S(2)}) collective-permute-start(bf16[64,2048]{1,0:T(8,128)(2,1)} %get-tuple-element.55), channel_id=1, source_target_pairs={{0,1},{1,2},{2,3},{3,0},{4,5},{5,6},{6,7},{7,4},{8,9},{9,10},{10,1... | collective-permute-start | bytes 786440 | tf_op jit(solution)/shard_map/ppermute | solution.py:567
  4.3 0.2 collective-permute-start.2
  4.5 2.3 %collective-permute-start.1 = (bf16[64,2048]{1,0:T(8,128)(2,1)}, bf16[64,2048]{1,0:T(8,128)(2,1)S(1)}, u32[]{:S(2)}, u32[]{:S(2)}) collective-permute-start(bf16[64,2048]{1,0:T(8,128)(2,1)} %get-tuple-element.56), channel_id=1, source_target_pairs={{0,2},{1,3},{2,0},{3,1},{4,6},{5,7},{6,4},{7,5},{8,10},{9,11},{10,... | collective-permute-start | bytes 786440 | tf_op jit(solution)/shard_map/ppermute | solution.py:567
  6.8 2.4 %shard_map.95 = (bf16[64,2048]{1,0:T(8,128)(2,1)}, bf16[64,2048]{1,0:T(8,128)(2,1)}, bf16[64,2048]{1,0:T(8,128)(2,1)}, bf16[64,2048]{1,0:T(8,128)(2,1)}) custom-call(s32[1]{0:T(128)} %bitcast.first, s32[2,128]{1,0:T(2,128)} %bitcast.16, f32[2,128]{1,0:T(2,128)} %bitcast.18, bf16[128,2048]{1,0:T(8,128)(2,1)} %refs_2_.1), custom_call_target="tpu_custom_call" | custom-call | flops 1024 | bytes 1024 | tf_op jit(solution)/shard_map/pallas_call | solution.py:521
  9.2 0.1 stack.23.at
  9.3 1.1 %collective-permute-done.refs_1_ = bf16[64,2048]{1,0:T(8,128)(2,1)S(1)} collective-permute-done((bf16[64,2048]{1,0:T(8,128)(2,1)}, bf16[64,2048]{1,0:T(8,128)(2,1)S(1)}, u32[]{:S(2)}, u32[]{:S(2)}) %collective-permute-start) | collective-permute-done | bytes 262176 | tf_op jit(solution)/shard_map/ppermute | solution.py:567
  10.4 8.5 %collective-permute-done.2.refs_3_ = bf16[64,2048]{1,0:T(8,128)(2,1)S(1)} collective-permute-done((bf16[64,2048]{1,0:T(8,128)(2,1)}, bf16[64,2048]{1,0:T(8,128)(2,1)S(1)}, u32[]{:S(2)}, u32[]{:S(2)}) %collective-permute-start.2) | collective-permute-done | bytes 262176 | tf_op jit(solution)/shard_map/ppermute | solution.py:567
  18.9 0.0 collective-permute-start.3
  18.9 1.1 %collective-permute-start.4 = (bf16[64,2048]{1,0:T(8,128)(2,1)}, bf16[64,2048]{1,0:T(8,128)(2,1)S(1)}, u32[]{:S(2)}, u32[]{:S(2)}) collective-permute-start(bf16[64,2048]{1,0:T(8,128)(2,1)} %get-tuple-element.67), channel_id=1, source_target_pairs={{0,2},{1,3},{2,0},{3,1},{4,6},{5,7},{6,4},{7,5},{8,10},{9,11},{10,... | collective-permute-start | bytes 786440 | tf_op jit(solution)/shard_map/ppermute | solution.py:567
  20.0 0.3 collective-permute-start.5
  20.3 0.1 fusion
  20.4 8.3 %collective-permute-done.1.refs_2_ = bf16[64,2048]{1,0:T(8,128)(2,1)S(1)} collective-permute-done((bf16[64,2048]{1,0:T(8,128)(2,1)}, bf16[64,2048]{1,0:T(8,128)(2,1)S(1)}, u32[]{:S(2)}, u32[]{:S(2)}) %collective-permute-start.1) | collective-permute-done | bytes 262176 | tf_op jit(solution)/shard_map/ppermute | solution.py:567
  28.7 1.6 %copy-done.1 = bf16[1,2048,512]{2,1,0:T(8,128)(2,1)S(1)} copy-done((bf16[1,2048,512]{2,1,0:T(8,128)(2,1)S(1)}, bf16[1,2048,512]{2,1,0:T(8,128)(2,1)}, u32[]{:S(2)}) %copy-start.1) | copy-done | bytes 2097176
  30.3 0.9 copy-done.3
  31.2 5.0 %shard_map.94 = (bf16[2048,256]{1,0:T(8,128)(2,1)S(1)}, f32[256,1024]{1,0:T(8,128)S(1)}, bf16[256,512]{1,0:T(8,128)(2,1)S(1)}, bf16[64,2048]{1,0:T(8,128)(2,1)S(...) custom-call(bf16[64,2048]{1,0:T(8,128)(2,1)S(1)} %copy-done.3, ...), custom_call_target="tpu_custom_call" | custom-call | flops 1024 | bytes 1024 | tf_op jit(solution)/shard_map/pallas_call | solution.py:234
  36.3 11.2 %collective-permute-start.6 = (bf16[64,2048]{1,0:T(8,128)(2,1)S(1)}, bf16[64,2048]{1,0:T(8,128)(2,1)S(1)}, u32[]{:S(2)}, u32[]{:S(2)}) collective-permute-start(bf16[64,2048]{1,0:T(8,128)(2,1)S(1)} %get-tuple-element.80.refs_3_), channel_id=1, source_target_pairs={{0,1},{1,2},{2,3},{3,0},{4,5},{5,6},{6,7},{7,4},{8,9},{9,10},{10,1... | collective-permute-start | bytes 786440 | tf_op jit(solution)/shard_map/ppermute | solution.py:567
  47.5 0.0 collective-permute-done.3.refs_1_
  47.5 1.5 %collective-permute-done.4.refs_2_ = bf16[64,2048]{1,0:T(8,128)(2,1)S(1)} collective-permute-done((bf16[64,2048]{1,0:T(8,128)(2,1)}, bf16[64,2048]{1,0:T(8,128)(2,1)S(1)}, u32[]{:S(2)}, u32[]{:S(2)}) %collective-permute-start.4) | collective-permute-done | bytes 262176 | tf_op jit(solution)/shard_map/ppermute | solution.py:567
  49.0 2.7 %collective-permute-done.5.refs_3_ = bf16[64,2048]{1,0:T(8,128)(2,1)S(1)} collective-permute-done((bf16[64,2048]{1,0:T(8,128)(2,1)}, bf16[64,2048]{1,0:T(8,128)(2,1)S(1)}, u32[]{:S(2)}, u32[]{:S(2)}) %collective-permute-start.5) | collective-permute-done | bytes 262176 | tf_op jit(solution)/shard_map/ppermute | solution.py:567
  51.7 0.0 copy-done.2
  51.7 2.7 %shard_map.96 = (bf16[256,1024]{1,0:T(8,128)(2,1)S(1)}, bf16[2048,256]{1,0:T(8,128)(2,1)S(1)}, bf16[8,256,768]{2,1,0:T(8,128)(2,1)S(1)}, bf16[2048,1024]{1,0:T(8,128)(2,1)S(1)}) custom-call(s32[8]{0:T(128)S(1)} %stack.23.at, f32[256,1024]{1,0:T(8,128)S(1)} %get-tuple-element.58.preact_hbm, bf16[2048,1024]{1,0:T(8,128)(2,1)S(1)} %bitcast.12, ...), custom_call_target="tpu_custom_call" | custom-call | flops 1024 | bytes 1024 | tf_op jit(solution)/shard_map/pallas_call | solution.py:332
  54.4 0.6 collective-permute-start.7
  55.0 1.4 %shard_map.97 = (bf16[128,2048]{1,0:T(8,128)(2,1)S(1)}, bf16[128,2048]{1,0:T(8,128)(2,1)S(1)}, bf16[128,2048]{1,0:T(8,128)(2,1)S(1)}, bf16[64,2048]{1,0:T(8,128)(2,1)S(1)}) custom-call(bf16[256,1024]{1,0:T(8,128)(2,1)S(1)} %get-tuple-element.75.pre_grad, bf16[2048,1024]{1,0:T(8,128)(2,1)S(1)} %get-tuple-element.76.w_in, ...), custom_call_target="tpu_custom_call" | custom-call | flops 1024 | bytes 1024 | tf_op jit(solution)/shard_map/pallas_call | solution.py:306
  56.4 2.6 %collective-permute-start.12 = (bf16[128,2048]{1,0:T(8,128)(2,1)S(1)}, bf16[128,2048]{1,0:T(8,128)(2,1)S(1)}, u32[]{:S(2)}, u32[]{:S(2)}) collective-permute-start(bf16[128,2048]{1,0:T(8,128)(2,1)S(1)} %get-tuple-element.98), channel_id=1, source_target_pairs={{0,2},{1,3},{2,0},{3,1},{4,6},{5,7},{6,4},{7,5},{8,10},{9,11},{10,... | collective-permute-start | bytes 1572872 | tf_op jit(solution)/shard_map/ppermute | solution.py:567
  58.9 0.0 collective-permute-start.13
  58.9 1.5 %collective-permute-start.14 = (bf16[64,2048]{1,0:T(8,128)(2,1)S(1)}, bf16[64,2048]{1,0:T(8,128)(2,1)S(1)}, u32[]{:S(2)}, u32[]{:S(2)}) collective-permute-start(bf16[64,2048]{1,0:T(8,128)(2,1)S(1)} %get-tuple-element.100), channel_id=1, source_target_pairs={{0,1},{1,2},{2,3},{3,0},{4,5},{5,6},{6,7},{7,4},{8,9},{9,10},{10,1... | collective-permute-start | bytes 786440 | tf_op jit(solution)/shard_map/ppermute | solution.py:567
  60.4 1.1 %shard_map.98.kept = bf16[4,256,768]{2,1,0:T(8,128)(2,1)S(1)} custom-call(s32[4]{0:T(128)S(1)} %get-tuple-element.82.at, bf16[2048,256]{1,0:T(8,128)(2,1)S(1)} %get-tuple-element.59.rows_t, bf16[2048,256]{1,0:T(8,128)(2,1)S(1)} %get-tuple-element.83.grads_t, bf16[256,1024]{1,0:T(8,128)(2,1)S(1)} %get-tuple-element.75.pre_grad, ...), custom_call_target="tpu_custom_call" | custom-call | flops 40000000000 | bytes 1024 | tf_op jit(solution)/shard_map/pallas_call | solution.py:356
  61.5 0.0 collective-permute-done.7.got
  61.5 0.4 shard_map.100
  61.9 0.3 collective-permute-start.8
  62.2 0.0 collective-permute-done.6.refs_1_
  62.2 1.2 %collective-permute-start.9 = (bf16[2,256,768]{2,1,0:T(8,128)(2,1)S(1)}, bf16[2,256,768]{2,1,0:T(8,128)(2,1)S(1)}, u32[]{:S(2)}, u32[]{:S(2)}) collective-permute-start(bf16[2,256,768]{2,1,0:T(8,128)(2,1)S(1)} %get-tuple-element.86), channel_id=1, source_target_pairs={{0,16},{4,20},{8,24},{12,28},{16,0},{20,4},{24,8},{28,12},{1,17},{... | collective-permute-start | bytes 2359304 | tf_op jit(solution)/shard_map/ppermute | solution.py:392
  63.5 1.1 %shard_map.99.kept = bf16[4,256,768]{2,1,0:T(8,128)(2,1)S(1)} custom-call(s32[4]{0:T(128)S(1)} %get-tuple-element.84.at, bf16[2048,256]{1,0:T(8,128)(2,1)S(1)} %get-tuple-element.59.rows_t, bf16[2048,256]{1,0:T(8,128)(2,1)S(1)} %get-tuple-element.83.grads_t, bf16[256,1024]{1,0:T(8,128)(2,1)S(1)} %get-tuple-element.75.pre_grad, ...), custom_call_target="tpu_custom_call" | custom-call | flops 40000000000 | bytes 1024 | tf_op jit(solution)/shard_map/pallas_call | solution.py:356
  64.6 15.6 %collective-permute-done.8.left_in = bf16[2,256,768]{2,1,0:T(8,128)(2,1)S(1)} collective-permute-done((bf16[2,256,768]{2,1,0:T(8,128)(2,1)S(1)}, bf16[2,256,768]{2,1,0:T(8,128)(2,1)S(1)}, u32[]{:S(2)}, u32[]{:S(2)}) %collective-permute-start.8) | collective-permute-done | bytes 786464 | tf_op jit(solution)/shard_map/ppermute | solution.py:392
  80.2 0.0 collective-permute-done.9.right_in
  80.2 0.3 shard_map.103
  80.5 1.3 %collective-permute-start.10 = (bf16[256,768]{1,0:T(8,128)(2,1)S(1)}, bf16[256,768]{1,0:T(8,128)(2,1)S(1)}, u32[]{:S(2)}, u32[]{:S(2)}) collective-permute-start(bf16[256,768]{1,0:T(8,128)(2,1)S(1)} %get-tuple-element.90), channel_id=1, source_target_pairs={{0,16},{4,20},{8,24},{12,28},{16,0},{20,4},{24,8},{28,12},{1,17},{... | collective-permute-start | bytes 1179656 | tf_op jit(solution)/shard_map/ppermute | solution.py:392
  81.8 1.2 %collective-permute-start.11 = (bf16[256,768]{1,0:T(8,128)(2,1)S(1)}, bf16[256,768]{1,0:T(8,128)(2,1)S(1)}, u32[]{:S(2)}, u32[]{:S(2)}) collective-permute-start(bf16[256,768]{1,0:T(8,128)(2,1)S(1)} %get-tuple-element.92), channel_id=1, source_target_pairs={{0,8},{4,12},{8,0},{12,4},{16,24},{20,28},{24,16},{28,20},{1,9},{5... | collective-permute-start | bytes 1179656 | tf_op jit(solution)/shard_map/ppermute | solution.py:392
  83.0 0.3 shard_map.101
  83.2 0.8 shard_map.102
  84.0 5.1 %collective-permute-done.10.left_last = bf16[256,768]{1,0:T(8,128)(2,1)S(1)} collective-permute-done((bf16[256,768]{1,0:T(8,128)(2,1)S(1)}, bf16[256,768]{1,0:T(8,128)(2,1)S(1)}, u32[]{:S(2)}, u32[]{:S(2)}) %collective-permute-start.10) | collective-permute-done | bytes 393248 | tf_op jit(solution)/shard_map/ppermute | solution.py:392
  89.1 1.0 collective-permute-done.11.right_last
  90.1 1.3 %shard_map.104 = (f32[256,1024]{1,0:T(8,128)}, f32[256,512]{1,0:T(8,128)}) custom-call(f32[256,768]{1,0:T(8,128)S(1)} %get-tuple-element.87.left, bf16[256,768]{1,0:T(8,128)(2,1)S(1)} %collective-permute-done.10.left_last, f32[256,768]{1,0:T(8,128)S(1)} %get-tuple-element.91.right, bf16[256,768]{1,0:T(8,128)(2,1)S(1)} %collective-permute-done.11.right_last), custom_call_target="tpu_custom_call" | custom-call | flops 1024 | bytes 1024 | tf_op jit(solution)/shard_map/pallas_call | solution.py:467
  91.4 5.2 %collective-permute-done.14.refs_2_ = bf16[64,2048]{1,0:T(8,128)(2,1)S(1)} collective-permute-done((bf16[64,2048]{1,0:T(8,128)(2,1)S(1)}, bf16[64,2048]{1,0:T(8,128)(2,1)S(1)}, u32[]{:S(2)}, u32[]{:S(2)}) %collective-permute-start.14) | collective-permute-done | bytes 262176 | tf_op jit(solution)/shard_map/ppermute | solution.py:567
  96.6 0.0 collective-permute-done.12.refs_0_
  96.6 1.0 collective-permute-done.13.refs_1_
  97.6 1.3 %shard_map.105 = (bf16[128,2048]{1,0:T(8,128)(2,1)}, bf16[128,2048]{1,0:T(8,128)(2,1)}) custom-call(bf16[384,192]{1,0:T(8,128)(2,1)S(1)} %get-tuple-element.94.picker, f32[2,128,128]{2,1,0:T(8,128)S(1)} %get-tuple-element.95.scales, f32[128,2048]{1,0:T(8,128)S(1)} %get-tuple-element.96.mixed_part, f32[128,2048]{1,0:T(8,128)S(1)} %get-tuple-element.97.back_part, ...), custom_call_target="tpu_custom_call" | custom-call | flops 1024 | bytes 1024 | tf_op jit(solution)/shard_map/pallas_call | solution.py:507
  (10 shorter events, 0.0 us)
Async XLA Ops:
  3.0 7.4 %collective-permute-start = (bf16[64,2048]{1,0:T(8,128)(2,1)}, bf16[64,2048]{1,0:T(8,128)(2,1)S(1)}, u32[]{:S(2)}, u32[]{:S(2)}) collective-permute-start(bf16[64,2048]{1,0:T(8,128)(2,1)} %get-tuple-element.55), channel_id=1, source_target_pairs={{0,1},{1,2},{2,3},{3,0},{4,5},{5,6},{6,7},{7,4},{8,9},{9,10},{10,1... | collective-permute-start | bytes 786440 | tf_op jit(solution)/shard_map/ppermute | solution.py:567
  4.3 14.5 %collective-permute-start.2 = (bf16[64,2048]{1,0:T(8,128)(2,1)}, bf16[64,2048]{1,0:T(8,128)(2,1)S(1)}, u32[]{:S(2)}, u32[]{:S(2)}) collective-permute-start(bf16[64,2048]{1,0:T(8,128)(2,1)} %get-tuple-element.57), channel_id=1, source_target_pairs={{0,3},{1,0},{2,1},{3,2},{4,7},{5,4},{6,5},{7,6},{8,11},{9,8},{10,9... | collective-permute-start | bytes 786440 | tf_op jit(solution)/shard_map/ppermute | solution.py:567
  4.5 24.2 %collective-permute-start.1 = (bf16[64,2048]{1,0:T(8,128)(2,1)}, bf16[64,2048]{1,0:T(8,128)(2,1)S(1)}, u32[]{:S(2)}, u32[]{:S(2)}) collective-permute-start(bf16[64,2048]{1,0:T(8,128)(2,1)} %get-tuple-element.56), channel_id=1, source_target_pairs={{0,2},{1,3},{2,0},{3,1},{4,6},{5,7},{6,4},{7,5},{8,10},{9,11},{10,... | collective-permute-start | bytes 786440 | tf_op jit(solution)/shard_map/ppermute | solution.py:567
  18.9 28.6 %collective-permute-start.3 = (bf16[64,2048]{1,0:T(8,128)(2,1)}, bf16[64,2048]{1,0:T(8,128)(2,1)S(1)}, u32[]{:S(2)}, u32[]{:S(2)}) collective-permute-start(bf16[64,2048]{1,0:T(8,128)(2,1)} %get-tuple-element.66), channel_id=1, source_target_pairs={{0,1},{1,2},{2,3},{3,0},{4,5},{5,6},{6,7},{7,4},{8,9},{9,10},{10,1... | collective-permute-start | bytes 786440 | tf_op jit(solution)/shard_map/ppermute | solution.py:567
  18.9 30.1 %collective-permute-start.4 = (bf16[64,2048]{1,0:T(8,128)(2,1)}, bf16[64,2048]{1,0:T(8,128)(2,1)S(1)}, u32[]{:S(2)}, u32[]{:S(2)}) collective-permute-start(bf16[64,2048]{1,0:T(8,128)(2,1)} %get-tuple-element.67), channel_id=1, source_target_pairs={{0,2},{1,3},{2,0},{3,1},{4,6},{5,7},{6,4},{7,5},{8,10},{9,11},{10,... | collective-permute-start | bytes 786440 | tf_op jit(solution)/shard_map/ppermute | solution.py:567
  20.0 31.7 %collective-permute-start.5 = (bf16[64,2048]{1,0:T(8,128)(2,1)}, bf16[64,2048]{1,0:T(8,128)(2,1)S(1)}, u32[]{:S(2)}, u32[]{:S(2)}) collective-permute-start(bf16[64,2048]{1,0:T(8,128)(2,1)} %get-tuple-element.68), channel_id=1, source_target_pairs={{0,3},{1,0},{2,1},{3,2},{4,7},{5,4},{6,5},{7,6},{8,11},{9,8},{10,9... | collective-permute-start | bytes 786440 | tf_op jit(solution)/shard_map/ppermute | solution.py:567
  28.7 1.6 %copy-start.1 = (bf16[1,2048,512]{2,1,0:T(8,128)(2,1)S(1)}, bf16[1,2048,512]{2,1,0:T(8,128)(2,1)}, u32[]{:S(2)}) copy-start(bf16[1,2048,512]{2,1,0:T(8,128)(2,1)} %param.11) | copy-start | bytes 6291460
  30.3 0.9 copy-start.3
  31.2 20.5 %copy-start = (bf16[1,2048,1024]{2,1,0:T(8,128)(2,1)S(1)}, bf16[1,2048,1024]{2,1,0:T(8,128)(2,1)}, u32[]{:S(2)}) copy-start(bf16[1,2048,1024]{2,1,0:T(8,128)(2,1)} %param.10) | copy-start | bytes 12582916
  31.2 20.5 %copy-start.2 = (bf16[64,2048]{1,0:T(8,128)(2,1)S(1)}, bf16[64,2048]{1,0:T(8,128)(2,1)}, u32[]{:S(2)}) copy-start(bf16[64,2048]{1,0:T(8,128)(2,1)} %get-tuple-element.69.refs_0_) | copy-start | bytes 786436
  36.3 26.0 %collective-permute-start.6 = (bf16[64,2048]{1,0:T(8,128)(2,1)S(1)}, bf16[64,2048]{1,0:T(8,128)(2,1)S(1)}, u32[]{:S(2)}, u32[]{:S(2)}) collective-permute-start(bf16[64,2048]{1,0:T(8,128)(2,1)S(1)} %get-tuple-element.80.refs_3_), channel_id=1, source_target_pairs={{0,1},{1,2},{2,3},{3,0},{4,5},{5,6},{6,7},{7,4},{8,9},{9,10},{10,1... | collective-permute-start | bytes 786440 | tf_op jit(solution)/shard_map/ppermute | solution.py:567
  54.4 7.1 %collective-permute-start.7 = (bf16[8,256,768]{2,1,0:T(8,128)(2,1)S(1)}, bf16[8,256,768]{2,1,0:T(8,128)(2,1)S(1)}, u32[]{:S(2)}, u32[]{:S(2)}) collective-permute-start(bf16[8,256,768]{2,1,0:T(8,128)(2,1)S(1)} %get-tuple-element.74), channel_id=1, source_target_pairs={{0,4},{4,0},{8,12},{12,8},{16,20},{20,16},{24,28},{28,24},{1,5},{5... | collective-permute-start | bytes 9437192 | tf_op jit(solution)/shard_map/ppermute | solution.py:392
  56.4 40.2 %collective-permute-start.12 = (bf16[128,2048]{1,0:T(8,128)(2,1)S(1)}, bf16[128,2048]{1,0:T(8,128)(2,1)S(1)}, u32[]{:S(2)}, u32[]{:S(2)}) collective-permute-start(bf16[128,2048]{1,0:T(8,128)(2,1)S(1)} %get-tuple-element.98), channel_id=1, source_target_pairs={{0,2},{1,3},{2,0},{3,1},{4,6},{5,7},{6,4},{7,5},{8,10},{9,11},{10,... | collective-permute-start | bytes 1572872 | tf_op jit(solution)/shard_map/ppermute | solution.py:567
  58.9 38.6 %collective-permute-start.13 = (bf16[128,2048]{1,0:T(8,128)(2,1)S(1)}, bf16[128,2048]{1,0:T(8,128)(2,1)S(1)}, u32[]{:S(2)}, u32[]{:S(2)}) collective-permute-start(bf16[128,2048]{1,0:T(8,128)(2,1)S(1)} %get-tuple-element.99), channel_id=1, source_target_pairs={{0,3},{1,0},{2,1},{3,2},{4,7},{5,4},{6,5},{7,6},{8,11},{9,8},{10,9... | collective-permute-start | bytes 1572872 | tf_op jit(solution)/shard_map/ppermute | solution.py:567
  58.9 37.6 %collective-permute-start.14 = (bf16[64,2048]{1,0:T(8,128)(2,1)S(1)}, bf16[64,2048]{1,0:T(8,128)(2,1)S(1)}, u32[]{:S(2)}, u32[]{:S(2)}) collective-permute-start(bf16[64,2048]{1,0:T(8,128)(2,1)S(1)} %get-tuple-element.100), channel_id=1, source_target_pairs={{0,1},{1,2},{2,3},{3,0},{4,5},{5,6},{6,7},{7,4},{8,9},{9,10},{10,1... | collective-permute-start | bytes 786440 | tf_op jit(solution)/shard_map/ppermute | solution.py:567
  61.9 18.3 %collective-permute-start.8 = (bf16[2,256,768]{2,1,0:T(8,128)(2,1)S(1)}, bf16[2,256,768]{2,1,0:T(8,128)(2,1)S(1)}, u32[]{:S(2)}, u32[]{:S(2)}) collective-permute-start(bf16[2,256,768]{2,1,0:T(8,128)(2,1)S(1)} %get-tuple-element.85), channel_id=1, source_target_pairs={{0,8},{4,12},{8,0},{12,4},{16,24},{20,28},{24,16},{28,20},{1,9},{5... | collective-permute-start | bytes 2359304 | tf_op jit(solution)/shard_map/ppermute | solution.py:392
  62.2 17.9 %collective-permute-start.9 = (bf16[2,256,768]{2,1,0:T(8,128)(2,1)S(1)}, bf16[2,256,768]{2,1,0:T(8,128)(2,1)S(1)}, u32[]{:S(2)}, u32[]{:S(2)}) collective-permute-start(bf16[2,256,768]{2,1,0:T(8,128)(2,1)S(1)} %get-tuple-element.86), channel_id=1, source_target_pairs={{0,16},{4,20},{8,24},{12,28},{16,0},{20,4},{24,8},{28,12},{1,17},{... | collective-permute-start | bytes 2359304 | tf_op jit(solution)/shard_map/ppermute | solution.py:392
  80.5 8.7 %collective-permute-start.10 = (bf16[256,768]{1,0:T(8,128)(2,1)S(1)}, bf16[256,768]{1,0:T(8,128)(2,1)S(1)}, u32[]{:S(2)}, u32[]{:S(2)}) collective-permute-start(bf16[256,768]{1,0:T(8,128)(2,1)S(1)} %get-tuple-element.90), channel_id=1, source_target_pairs={{0,16},{4,20},{8,24},{12,28},{16,0},{20,4},{24,8},{28,12},{1,17},{... | collective-permute-start | bytes 1179656 | tf_op jit(solution)/shard_map/ppermute | solution.py:392
  81.8 1.4 %copy-start.4 = (s32[128,2]{0,1:T(2,128)S(1)}, s32[128,2]{0,1:T(2,128)}, u32[]{:S(2)}) copy-start(s32[128,2]{0,1:T(2,128)} %param.7) | copy-start | bytes 3076
  81.8 1.4 %copy-start.5 = (f32[128,2]{0,1:T(2,128)S(1)}, f32[128,2]{0,1:T(2,128)}, u32[]{:S(2)}) copy-start(f32[128,2]{0,1:T(2,128)} %param.8) | copy-start | bytes 3076
  81.8 8.3 %collective-permute-start.11 = (bf16[256,768]{1,0:T(8,128)(2,1)S(1)}, bf16[256,768]{1,0:T(8,128)(2,1)S(1)}, u32[]{:S(2)}, u32[]{:S(2)}) collective-permute-start(bf16[256,768]{1,0:T(8,128)(2,1)S(1)} %get-tuple-element.92), channel_id=1, source_target_pairs={{0,8},{4,12},{8,0},{12,4},{16,24},{20,28},{24,16},{28,20},{1,9},{5... | collective-permute-start | bytes 1179656 | tf_op jit(solution)/shard_map/ppermute | solution.py:392

commit v6 on v4

--- a/solution.py
+++ b/solution.py
@@ -419,9 +419,9 @@
     return lax.optimization_barrier((value, *others))[0]
 
 
-def partial_kernel(experts, capacity, alone, late, first, routes, scores, *refs):
-    own, early, mixed, back, late_picker, scales = refs
-    slots, toks = experts * capacity, mixed.shape[0]
+def select_kernel(experts, capacity, now, late, first, routes, scores, *refs):
+    now_picker, late_picker, scales = refs
+    slots, toks = experts * capacity, scales.shape[1]
     places = lax.broadcasted_iota(jnp.int32, (toks, slots), 1).astype(F32)
     hits = [
         places == to_column(row) for row in slot_rows(first[0], routes[...], experts, capacity)
@@ -431,16 +431,15 @@
     weights = weight_rows(scores[...])
     for k in range(scales.shape[0]):
         scales[k] = jnp.broadcast_to(to_column(weights[k : k + 1, :]), scales.shape[1:])
-
-    def slots_of(blocks):
+    for out, blocks in ((now_picker, now), (late_picker, late)):
         parts = [picker[:, n * capacity : (n + 1) * capacity] for n in blocks]
-        return jnp.concatenate(parts, axis=1)
-
-    late_picker[...] = slots_of(late + [alone])
-    now = slots_of((0, alone))
+        out[...] = jnp.concatenate(parts, axis=1)
+
+
+def partial_kernel(capacity, picker, scales, own, early, mixed, back):
     for columns in column_steps(mixed.shape[1]):
         outputs = jnp.concatenate([own[:capacity, columns], early[:, columns]], axis=0)
-        total, grad = sum_rows(now, scales, outputs, own[capacity:, columns])
+        total, grad = sum_rows(picker[...], scales, outputs, own[capacity:, columns])
         mixed[:, columns] = total
         back[:, columns] = grad
 
@@ -595,7 +594,20 @@
         send_at = jnp.stack([jnp.bitwise_xor(own, j) for j in CUBE_SEND]).astype(jnp.int32)
         keep_at = jnp.bitwise_xor(send_at, 1)
         early = experts - 1
-        early_out = travel(produced[early], early, -1)
+        late = [n for n in range(experts - 1, 0, -1) if n != early]
+        chosen = ([0, early], late + [early])
+        now_picker, late_picker, scales = call(
+            functools.partial(select_kernel, experts, capacity, *chosen),
+            (
+                *[
+                    jax.ShapeDtypeStruct(((tops + 1) * toks, len(part) * capacity), BF16)
+                    for part in chosen
+                ],
+                jax.ShapeDtypeStruct((tops, toks, 128), F32),
+            ),
+            (after(first, hidden), routes_t, scores_t),
+        )
+        early_out = travel(after(produced[early], scales), early, -1)
         pre_grad, grads_t, sent, w_in_here = backward(
             send_at, share, preact, w_in, rows_t, hidden, w_out, got_grads
         )
@@ -607,19 +619,16 @@
         returned = exchange(blocks, -1)
         kept_later = shares(after(keep_at[half:], kept_first, early_out, got), *operands, COVER)
         sums = cube_sum(got, kept_first, kept_later)
-        late = [n for n in range(experts - 1, 0, -1) if n != early]
-        mixed_part, back_part, picker, scales = call(
-            functools.partial(partial_kernel, experts, capacity, early, late),
-            (
-                jax.ShapeDtypeStruct((toks, width), F32),
-                jax.ShapeDtypeStruct((toks, width), F32),
-                jax.ShapeDtypeStruct(((tops + 1) * toks, (len(late) + 1) * capacity), BF16),
-                jax.ShapeDtypeStruct((tops, toks, 128), F32),
-            ),
-            (after(first, sums[0]), routes_t, scores_t, returned[0], early_out),
-        )
+        mixed_part, back_part = pl.pallas_call(
+            functools.partial(partial_kernel, capacity),
+            out_shape=(jax.ShapeDtypeStruct((toks, width), F32),) * 2,
+            in_specs=whole(4),
+            out_specs=whole(2),
+            compiler_params=ROOMY,
+            cost_estimate=BRIEF,
+        )(after(now_picker, sums[0]), scales, returned[0], early_out)
         grad_in, grad_down = means(groups, sums)
-        parts = (after(picker, grad_in), scales, mixed_part, back_part)
+        parts = (after(late_picker, grad_in), scales, mixed_part, back_part)
         mixed_out, token_grad = last(capacity, parts, [returned[n] for n in late + [early]])
     else:
         token_rows = joined(got_rows)

time: 99.1 us -> 99.5 us (level)
  no operation moved by 1% of the time
where the time goes in v6:
time: 99.5 us; the launch traced here: 99.3 us
  waiting for transfers between devices  50.2 us (50%)
  starting transfers between devices  25.1 us (25%)
  Pallas kernels  20.6 us (21%)
  local copies, waits for them, and re-layouts  2.72 us (3%)
    ppermute x10, waiting for transfers between devices, travel(): return lax.ppermute(block, 'expert', pairs)  28.2 us
    ppermute x5, waiting for transfers between devices, swap(): lax.ppermute(block, 'dp', [(at, at ^ bit) for at in range(lax.axis_size('...  21.9 us
    ppermute x10, starting transfers between devices, travel(): return lax.ppermute(block, 'expert', pairs)  20.5 us
    pallas_call x1, Pallas kernels, forward(): pl.pallas_call(functools.partial(forward_kernel, count), out_shape=(jax.S...  5.05 us
    pallas_call x2, Pallas kernels, dispatch(): pl.pallas_call(functools.partial(dispatch_kernel, experts, capacity, weig...  4.75 us
    ppermute x5, starting transfers between devices, swap(): lax.ppermute(block, 'dp', [(at, at ^ bit) for at in range(lax.axis_size('...  4.58 us
    pallas_call x1, Pallas kernels, backward(): pl.pallas_call(functools.partial(backward_kernel, count), out_shape=(jax....  2.74 us
    unnamed x12, local copies, waits for them, and re-layouts  2.55 us
  transfers between devices with their start and end apart: 15, of which 10 were waited for; matrix products, arithmetic and copies ran while one was open for 0% of the time, Pallas kernels for 17%

profile of v6, /device:TPU:11, one launch (start us, length us, event | category | flops | bytes accessed | tf_op | source)
XLA Modules:
  0.0 99.3 jit_solution(14639526641372214819)
XLA Ops:
  0.6 2.3 %shard_map.93 = (bf16[64,2048]{1,0:T(8,128)(2,1)}, bf16[64,2048]{1,0:T(8,128)(2,1)}, bf16[64,2048]{1,0:T(8,128)(2,1)}, bf16[64,2048]{1,0:T(8,128)(2,1)}) custom-call(s32[1]{0:T(128)} %bitcast.first, s32[2,128]{1,0:T(2,128)} %bitcast.15, bf16[128,2048]{1,0:T(8,128)(2,1)} %refs_1_.1), custom_call_target="tpu_custom_call" | custom-call | flops 1024 | bytes 1024 | tf_op jit(solution)/shard_map/pallas_call | solution.py:520
  3.0 1.3 %collective-permute-start = (bf16[64,2048]{1,0:T(8,128)(2,1)}, bf16[64,2048]{1,0:T(8,128)(2,1)S(1)}, u32[]{:S(2)}, u32[]{:S(2)}) collective-permute-start(bf16[64,2048]{1,0:T(8,128)(2,1)} %get-tuple-element.58), channel_id=1, source_target_pairs={{0,1},{1,2},{2,3},{3,0},{4,5},{5,6},{6,7},{7,4},{8,9},{9,10},{10,1... | collective-permute-start | bytes 786440 | tf_op jit(solution)/shard_map/ppermute | solution.py:566
  4.3 0.2 collective-permute-start.2
  4.5 2.3 %collective-permute-start.1 = (bf16[64,2048]{1,0:T(8,128)(2,1)}, bf16[64,2048]{1,0:T(8,128)(2,1)S(1)}, u32[]{:S(2)}, u32[]{:S(2)}) collective-permute-start(bf16[64,2048]{1,0:T(8,128)(2,1)} %get-tuple-element.59), channel_id=1, source_target_pairs={{0,2},{1,3},{2,0},{3,1},{4,6},{5,7},{6,4},{7,5},{8,10},{9,11},{10,... | collective-permute-start | bytes 786440 | tf_op jit(solution)/shard_map/ppermute | solution.py:566
  6.8 2.4 %shard_map.96 = (bf16[64,2048]{1,0:T(8,128)(2,1)}, bf16[64,2048]{1,0:T(8,128)(2,1)}, bf16[64,2048]{1,0:T(8,128)(2,1)}, bf16[64,2048]{1,0:T(8,128)(2,1)}) custom-call(s32[1]{0:T(128)} %bitcast.first, s32[2,128]{1,0:T(2,128)} %bitcast.16, f32[2,128]{1,0:T(2,128)} %bitcast.18, bf16[128,2048]{1,0:T(8,128)(2,1)} %refs_2_.1), custom_call_target="tpu_custom_call" | custom-call | flops 1024 | bytes 1024 | tf_op jit(solution)/shard_map/pallas_call | solution.py:520
  9.2 0.1 stack.23.at
  9.3 1.1 %collective-permute-done.refs_1_ = bf16[64,2048]{1,0:T(8,128)(2,1)S(1)} collective-permute-done((bf16[64,2048]{1,0:T(8,128)(2,1)}, bf16[64,2048]{1,0:T(8,128)(2,1)S(1)}, u32[]{:S(2)}, u32[]{:S(2)}) %collective-permute-start) | collective-permute-done | bytes 262176 | tf_op jit(solution)/shard_map/ppermute | solution.py:566
  10.4 8.5 %collective-permute-done.2.refs_3_ = bf16[64,2048]{1,0:T(8,128)(2,1)S(1)} collective-permute-done((bf16[64,2048]{1,0:T(8,128)(2,1)}, bf16[64,2048]{1,0:T(8,128)(2,1)S(1)}, u32[]{:S(2)}, u32[]{:S(2)}) %collective-permute-start.2) | collective-permute-done | bytes 262176 | tf_op jit(solution)/shard_map/ppermute | solution.py:566
  18.9 0.0 collective-permute-start.3
  18.9 1.1 %collective-permute-start.4 = (bf16[64,2048]{1,0:T(8,128)(2,1)}, bf16[64,2048]{1,0:T(8,128)(2,1)S(1)}, u32[]{:S(2)}, u32[]{:S(2)}) collective-permute-start(bf16[64,2048]{1,0:T(8,128)(2,1)} %get-tuple-element.72), channel_id=1, source_target_pairs={{0,2},{1,3},{2,0},{3,1},{4,6},{5,7},{6,4},{7,5},{8,10},{9,11},{10,... | collective-permute-start | bytes 786440 | tf_op jit(solution)/shard_map/ppermute | solution.py:566
  20.0 0.3 collective-permute-start.5
  20.3 0.1 fusion
  20.4 8.3 %collective-permute-done.1.refs_2_ = bf16[64,2048]{1,0:T(8,128)(2,1)S(1)} collective-permute-done((bf16[64,2048]{1,0:T(8,128)(2,1)}, bf16[64,2048]{1,0:T(8,128)(2,1)S(1)}, u32[]{:S(2)}, u32[]{:S(2)}) %collective-permute-start.1) | collective-permute-done | bytes 262176 | tf_op jit(solution)/shard_map/ppermute | solution.py:566
  28.7 1.6 %copy-done.1 = bf16[1,2048,512]{2,1,0:T(8,128)(2,1)S(1)} copy-done((bf16[1,2048,512]{2,1,0:T(8,128)(2,1)S(1)}, bf16[1,2048,512]{2,1,0:T(8,128)(2,1)}, u32[]{:S(2)}) %copy-start.1) | copy-done | bytes 2097176
  30.3 0.9 copy-done.3
  31.2 5.0 %shard_map.94 = (bf16[2048,256]{1,0:T(8,128)(2,1)S(1)}, f32[256,1024]{1,0:T(8,128)S(1)}, bf16[256,512]{1,0:T(8,128)(2,1)S(1)}, bf16[64,2048]{1,0:T(8,128)(2,1)S(...) custom-call(bf16[64,2048]{1,0:T(8,128)(2,1)S(1)} %copy-done.3, ...), custom_call_target="tpu_custom_call" | custom-call | flops 1024 | bytes 1024 | tf_op jit(solution)/shard_map/pallas_call | solution.py:234
  36.3 0.3 shard_map.95
  36.7 11.2 %collective-permute-start.6 = (bf16[64,2048]{1,0:T(8,128)(2,1)S(1)}, bf16[64,2048]{1,0:T(8,128)(2,1)S(1)}, u32[]{:S(2)}, u32[]{:S(2)}) collective-permute-start(bf16[64,2048]{1,0:T(8,128)(2,1)S(1)} %get-tuple-element.90.refs_3_), channel_id=1, source_target_pairs={{0,1},{1,2},{2,3},{3,0},{4,5},{5,6},{6,7},{7,4},{8,9},{9,10},{10,1... | collective-permute-start | bytes 786440 | tf_op jit(solution)/shard_map/ppermute | solution.py:566
  47.8 0.0 collective-permute-done.3.refs_1_
  47.9 1.1 %collective-permute-done.4.refs_2_ = bf16[64,2048]{1,0:T(8,128)(2,1)S(1)} collective-permute-done((bf16[64,2048]{1,0:T(8,128)(2,1)}, bf16[64,2048]{1,0:T(8,128)(2,1)S(1)}, u32[]{:S(2)}, u32[]{:S(2)}) %collective-permute-start.4) | collective-permute-done | bytes 262176 | tf_op jit(solution)/shard_map/ppermute | solution.py:566
  49.0 2.7 %collective-permute-done.5.refs_3_ = bf16[64,2048]{1,0:T(8,128)(2,1)S(1)} collective-permute-done((bf16[64,2048]{1,0:T(8,128)(2,1)}, bf16[64,2048]{1,0:T(8,128)(2,1)S(1)}, u32[]{:S(2)}, u32[]{:S(2)}) %collective-permute-start.5) | collective-permute-done | bytes 262176 | tf_op jit(solution)/shard_map/ppermute | solution.py:566
  51.7 2.7 %shard_map.97 = (bf16[256,1024]{1,0:T(8,128)(2,1)S(1)}, bf16[2048,256]{1,0:T(8,128)(2,1)S(1)}, bf16[8,256,768]{2,1,0:T(8,128)(2,1)S(1)}, bf16[2048,1024]{1,0:T(8,128)(2,1)S(1)}) custom-call(s32[8]{0:T(128)S(1)} %stack.23.at, f32[256,1024]{1,0:T(8,128)S(1)} %get-tuple-element.64.preact_hbm, bf16[2048,1024]{1,0:T(8,128)(2,1)S(1)} %bitcast.12, ...), custom_call_target="tpu_custom_call" | custom-call | flops 1024 | bytes 1024 | tf_op jit(solution)/shard_map/pallas_call | solution.py:332
  54.4 0.6 collective-permute-start.7
  55.0 1.4 %shard_map.98 = (bf16[128,2048]{1,0:T(8,128)(2,1)S(1)}, bf16[128,2048]{1,0:T(8,128)(2,1)S(1)}, bf16[128,2048]{1,0:T(8,128)(2,1)S(1)}, bf16[64,2048]{1,0:T(8,128)(2,1)S(1)}) custom-call(bf16[256,1024]{1,0:T(8,128)(2,1)S(1)} %get-tuple-element.80.pre_grad, bf16[2048,1024]{1,0:T(8,128)(2,1)S(1)} %get-tuple-element.81.w_in, ...), custom_call_target="tpu_custom_call" | custom-call | flops 1024 | bytes 1024 | tf_op jit(solution)/shard_map/pallas_call | solution.py:306
  56.4 2.6 %collective-permute-start.12 = (bf16[128,2048]{1,0:T(8,128)(2,1)S(1)}, bf16[128,2048]{1,0:T(8,128)(2,1)S(1)}, u32[]{:S(2)}, u32[]{:S(2)}) collective-permute-start(bf16[128,2048]{1,0:T(8,128)(2,1)S(1)} %get-tuple-element.104), channel_id=1, source_target_pairs={{0,2},{1,3},{2,0},{3,1},{4,6},{5,7},{6,4},{7,5},{8,10},{9,11},{10,... | collective-permute-start | bytes 1572872 | tf_op jit(solution)/shard_map/ppermute | solution.py:566
  58.9 0.0 collective-permute-start.13
  58.9 1.5 %collective-permute-start.14 = (bf16[64,2048]{1,0:T(8,128)(2,1)S(1)}, bf16[64,2048]{1,0:T(8,128)(2,1)S(1)}, u32[]{:S(2)}, u32[]{:S(2)}) collective-permute-start(bf16[64,2048]{1,0:T(8,128)(2,1)S(1)} %get-tuple-element.106), channel_id=1, source_target_pairs={{0,1},{1,2},{2,3},{3,0},{4,5},{5,6},{6,7},{7,4},{8,9},{9,10},{10,1... | collective-permute-start | bytes 786440 | tf_op jit(solution)/shard_map/ppermute | solution.py:566
  60.4 1.1 %shard_map.99.kept = bf16[4,256,768]{2,1,0:T(8,128)(2,1)S(1)} custom-call(s32[4]{0:T(128)S(1)} %get-tuple-element.87.at, bf16[2048,256]{1,0:T(8,128)(2,1)S(1)} %get-tuple-element.65.rows_t, bf16[2048,256]{1,0:T(8,128)(2,1)S(1)} %get-tuple-element.88.grads_t, bf16[256,1024]{1,0:T(8,128)(2,1)S(1)} %get-tuple-element.80.pre_grad, ...), custom_call_target="tpu_custom_call" | custom-call | flops 40000000000 | bytes 1024 | tf_op jit(solution)/shard_map/pallas_call | solution.py:356
  61.5 0.0 collective-permute-done.7.got
  61.5 0.4 shard_map.101
  61.9 0.3 collective-permute-start.8
  62.2 0.0 collective-permute-done.6.early
  62.2 1.2 %collective-permute-start.9 = (bf16[2,256,768]{2,1,0:T(8,128)(2,1)S(1)}, bf16[2,256,768]{2,1,0:T(8,128)(2,1)S(1)}, u32[]{:S(2)}, u32[]{:S(2)}) collective-permute-start(bf16[2,256,768]{2,1,0:T(8,128)(2,1)S(1)} %get-tuple-element.93), channel_id=1, source_target_pairs={{0,16},{4,20},{8,24},{12,28},{16,0},{20,4},{24,8},{28,12},{1,17},{... | collective-permute-start | bytes 2359304 | tf_op jit(solution)/shard_map/ppermute | solution.py:392
  63.5 1.1 %shard_map.100.kept = bf16[4,256,768]{2,1,0:T(8,128)(2,1)S(1)} custom-call(s32[4]{0:T(128)S(1)} %get-tuple-element.91.at, bf16[2048,256]{1,0:T(8,128)(2,1)S(1)} %get-tuple-element.65.rows_t, bf16[2048,256]{1,0:T(8,128)(2,1)S(1)} %get-tuple-element.88.grads_t, bf16[256,1024]{1,0:T(8,128)(2,1)S(1)} %get-tuple-element.80.pre_grad, ...), custom_call_target="tpu_custom_call" | custom-call | flops 40000000000 | bytes 1024 | tf_op jit(solution)/shard_map/pallas_call | solution.py:356
  64.6 15.6 %collective-permute-done.8.left_in = bf16[2,256,768]{2,1,0:T(8,128)(2,1)S(1)} collective-permute-done((bf16[2,256,768]{2,1,0:T(8,128)(2,1)S(1)}, bf16[2,256,768]{2,1,0:T(8,128)(2,1)S(1)}, u32[]{:S(2)}, u32[]{:S(2)}) %collective-permute-start.8) | collective-permute-done | bytes 786464 | tf_op jit(solution)/shard_map/ppermute | solution.py:392
  80.2 0.0 collective-permute-done.9.right_in
  80.2 0.3 shard_map.103
  80.5 1.3 %collective-permute-start.10 = (bf16[256,768]{1,0:T(8,128)(2,1)S(1)}, bf16[256,768]{1,0:T(8,128)(2,1)S(1)}, u32[]{:S(2)}, u32[]{:S(2)}) collective-permute-start(bf16[256,768]{1,0:T(8,128)(2,1)S(1)} %get-tuple-element.95), channel_id=1, source_target_pairs={{0,16},{4,20},{8,24},{12,28},{16,0},{20,4},{24,8},{28,12},{1,17},{... | collective-permute-start | bytes 1179656 | tf_op jit(solution)/shard_map/ppermute | solution.py:392
  81.8 1.2 %collective-permute-start.11 = (bf16[256,768]{1,0:T(8,128)(2,1)S(1)}, bf16[256,768]{1,0:T(8,128)(2,1)S(1)}, u32[]{:S(2)}, u32[]{:S(2)}) collective-permute-start(bf16[256,768]{1,0:T(8,128)(2,1)S(1)} %get-tuple-element.97), channel_id=1, source_target_pairs={{0,8},{4,12},{8,0},{12,4},{16,24},{20,28},{24,16},{28,20},{1,9},{5... | collective-permute-start | bytes 1179656 | tf_op jit(solution)/shard_map/ppermute | solution.py:392
  82.9 0.3 shard_map.102
  83.2 0.6 shard_map.105
  83.8 5.4 %collective-permute-done.10.left_last = bf16[256,768]{1,0:T(8,128)(2,1)S(1)} collective-permute-done((bf16[256,768]{1,0:T(8,128)(2,1)S(1)}, bf16[256,768]{1,0:T(8,128)(2,1)S(1)}, u32[]{:S(2)}, u32[]{:S(2)}) %collective-permute-start.10) | collective-permute-done | bytes 393248 | tf_op jit(solution)/shard_map/ppermute | solution.py:392
  89.1 0.9 collective-permute-done.11.right_last
  90.1 1.3 %shard_map.104 = (f32[256,1024]{1,0:T(8,128)}, f32[256,512]{1,0:T(8,128)}) custom-call(f32[256,768]{1,0:T(8,128)S(1)} %get-tuple-element.94.left, bf16[256,768]{1,0:T(8,128)(2,1)S(1)} %collective-permute-done.10.left_last, f32[256,768]{1,0:T(8,128)S(1)} %get-tuple-element.96.right, bf16[256,768]{1,0:T(8,128)(2,1)S(1)} %collective-permute-done.11.right_last), custom_call_target="tpu_custom_call" | custom-call | flops 1024 | bytes 1024 | tf_op jit(solution)/shard_map/pallas_call | solution.py:466
  91.4 5.6 %collective-permute-done.14.refs_2_ = bf16[64,2048]{1,0:T(8,128)(2,1)S(1)} collective-permute-done((bf16[64,2048]{1,0:T(8,128)(2,1)S(1)}, bf16[64,2048]{1,0:T(8,128)(2,1)S(1)}, u32[]{:S(2)}, u32[]{:S(2)}) %collective-permute-start.14) | collective-permute-done | bytes 262176 | tf_op jit(solution)/shard_map/ppermute | solution.py:566
  97.0 0.0 collective-permute-done.12.refs_0_
  97.0 1.0 collective-permute-done.13.refs_1_
  98.0 1.3 %shard_map.106 = (bf16[128,2048]{1,0:T(8,128)(2,1)}, bf16[128,2048]{1,0:T(8,128)(2,1)}) custom-call(bf16[384,192]{1,0:T(8,128)(2,1)S(1)} %get-tuple-element.99.picker, f32[2,128,128]{2,1,0:T(8,128)S(1)} %get-tuple-element.89.scales, f32[128,2048]{1,0:T(8,128)S(1)} %get-tuple-element.102.mixed_part, f32[128,2048]{1,0:T(8,128)S(1)} %get-tuple-element.103.back_part, ...), custom_call_target="tpu_custom_call" | custom-call | flops 1024 | bytes 1024 | tf_op jit(solution)/shard_map/pallas_call | solution.py:506
  (11 shorter events, 0.0 us)
Async XLA Ops:
  3.0 7.4 %collective-permute-start = (bf16[64,2048]{1,0:T(8,128)(2,1)}, bf16[64,2048]{1,0:T(8,128)(2,1)S(1)}, u32[]{:S(2)}, u32[]{:S(2)}) collective-permute-start(bf16[64,2048]{1,0:T(8,128)(2,1)} %get-tuple-element.58), channel_id=1, source_target_pairs={{0,1},{1,2},{2,3},{3,0},{4,5},{5,6},{6,7},{7,4},{8,9},{9,10},{10,1... | collective-permute-start | bytes 786440 | tf_op jit(solution)/shard_map/ppermute | solution.py:566
  4.3 14.5 %collective-permute-start.2 = (bf16[64,2048]{1,0:T(8,128)(2,1)}, bf16[64,2048]{1,0:T(8,128)(2,1)S(1)}, u32[]{:S(2)}, u32[]{:S(2)}) collective-permute-start(bf16[64,2048]{1,0:T(8,128)(2,1)} %get-tuple-element.60), channel_id=1, source_target_pairs={{0,3},{1,0},{2,1},{3,2},{4,7},{5,4},{6,5},{7,6},{8,11},{9,8},{10,9... | collective-permute-start | bytes 786440 | tf_op jit(solution)/shard_map/ppermute | solution.py:566
  4.5 24.2 %collective-permute-start.1 = (bf16[64,2048]{1,0:T(8,128)(2,1)}, bf16[64,2048]{1,0:T(8,128)(2,1)S(1)}, u32[]{:S(2)}, u32[]{:S(2)}) collective-permute-start(bf16[64,2048]{1,0:T(8,128)(2,1)} %get-tuple-element.59), channel_id=1, source_target_pairs={{0,2},{1,3},{2,0},{3,1},{4,6},{5,7},{6,4},{7,5},{8,10},{9,11},{10,... | collective-permute-start | bytes 786440 | tf_op jit(solution)/shard_map/ppermute | solution.py:566
  18.9 29.0 %collective-permute-start.3 = (bf16[64,2048]{1,0:T(8,128)(2,1)}, bf16[64,2048]{1,0:T(8,128)(2,1)S(1)}, u32[]{:S(2)}, u32[]{:S(2)}) collective-permute-start(bf16[64,2048]{1,0:T(8,128)(2,1)} %get-tuple-element.71), channel_id=1, source_target_pairs={{0,1},{1,2},{2,3},{3,0},{4,5},{5,6},{6,7},{7,4},{8,9},{9,10},{10,1... | collective-permute-start | bytes 786440 | tf_op jit(solution)/shard_map/ppermute | solution.py:566
  18.9 30.1 %collective-permute-start.4 = (bf16[64,2048]{1,0:T(8,128)(2,1)}, bf16[64,2048]{1,0:T(8,128)(2,1)S(1)}, u32[]{:S(2)}, u32[]{:S(2)}) collective-permute-start(bf16[64,2048]{1,0:T(8,128)(2,1)} %get-tuple-element.72), channel_id=1, source_target_pairs={{0,2},{1,3},{2,0},{3,1},{4,6},{5,7},{6,4},{7,5},{8,10},{9,11},{10,... | collective-permute-start | bytes 786440 | tf_op jit(solution)/shard_map/ppermute | solution.py:566
  20.0 31.7 %collective-permute-start.5 = (bf16[64,2048]{1,0:T(8,128)(2,1)}, bf16[64,2048]{1,0:T(8,128)(2,1)S(1)}, u32[]{:S(2)}, u32[]{:S(2)}) collective-permute-start(bf16[64,2048]{1,0:T(8,128)(2,1)} %get-tuple-element.73), channel_id=1, source_target_pairs={{0,3},{1,0},{2,1},{3,2},{4,7},{5,4},{6,5},{7,6},{8,11},{9,8},{10,9... | collective-permute-start | bytes 786440 | tf_op jit(solution)/shard_map/ppermute | solution.py:566
  28.7 1.6 %copy-start.1 = (bf16[1,2048,512]{2,1,0:T(8,128)(2,1)S(1)}, bf16[1,2048,512]{2,1,0:T(8,128)(2,1)}, u32[]{:S(2)}) copy-start(bf16[1,2048,512]{2,1,0:T(8,128)(2,1)} %param.11) | copy-start | bytes 6291460
  30.3 0.9 copy-start.3
  31.2 5.1 %copy-start.4 = (s32[128,2]{0,1:T(2,128)S(1)}, s32[128,2]{0,1:T(2,128)}, u32[]{:S(2)}) copy-start(s32[128,2]{0,1:T(2,128)} %param.7) | copy-start | bytes 3076
  31.2 5.1 %copy-start.5 = (f32[128,2]{0,1:T(2,128)S(1)}, f32[128,2]{0,1:T(2,128)}, u32[]{:S(2)}) copy-start(f32[128,2]{0,1:T(2,128)} %param.8) | copy-start | bytes 3076
  31.2 20.5 %copy-start = (bf16[1,2048,1024]{2,1,0:T(8,128)(2,1)S(1)}, bf16[1,2048,1024]{2,1,0:T(8,128)(2,1)}, u32[]{:S(2)}) copy-start(bf16[1,2048,1024]{2,1,0:T(8,128)(2,1)} %param.10) | copy-start | bytes 12582916
  31.2 20.5 %copy-start.2 = (bf16[64,2048]{1,0:T(8,128)(2,1)S(1)}, bf16[64,2048]{1,0:T(8,128)(2,1)}, u32[]{:S(2)}) copy-start(bf16[64,2048]{1,0:T(8,128)(2,1)} %get-tuple-element.74.refs_0_) | copy-start | bytes 786436
  36.7 25.6 %collective-permute-start.6 = (bf16[64,2048]{1,0:T(8,128)(2,1)S(1)}, bf16[64,2048]{1,0:T(8,128)(2,1)S(1)}, u32[]{:S(2)}, u32[]{:S(2)}) collective-permute-start(bf16[64,2048]{1,0:T(8,128)(2,1)S(1)} %get-tuple-element.90.refs_3_), channel_id=1, source_target_pairs={{0,1},{1,2},{2,3},{3,0},{4,5},{5,6},{6,7},{7,4},{8,9},{9,10},{10,1... | collective-permute-start | bytes 786440 | tf_op jit(solution)/shard_map/ppermute | solution.py:566
  54.4 7.1 %collective-permute-start.7 = (bf16[8,256,768]{2,1,0:T(8,128)(2,1)S(1)}, bf16[8,256,768]{2,1,0:T(8,128)(2,1)S(1)}, u32[]{:S(2)}, u32[]{:S(2)}) collective-permute-start(bf16[8,256,768]{2,1,0:T(8,128)(2,1)S(1)} %get-tuple-element.79), channel_id=1, source_target_pairs={{0,4},{4,0},{8,12},{12,8},{16,20},{20,16},{24,28},{28,24},{1,5},{5... | collective-permute-start | bytes 9437192 | tf_op jit(solution)/shard_map/ppermute | solution.py:392
  56.4 40.6 %collective-permute-start.12 = (bf16[128,2048]{1,0:T(8,128)(2,1)S(1)}, bf16[128,2048]{1,0:T(8,128)(2,1)S(1)}, u32[]{:S(2)}, u32[]{:S(2)}) collective-permute-start(bf16[128,2048]{1,0:T(8,128)(2,1)S(1)} %get-tuple-element.104), channel_id=1, source_target_pairs={{0,2},{1,3},{2,0},{3,1},{4,6},{5,7},{6,4},{7,5},{8,10},{9,11},{10,... | collective-permute-start | bytes 1572872 | tf_op jit(solution)/shard_map/ppermute | solution.py:566
  58.9 39.0 %collective-permute-start.13 = (bf16[128,2048]{1,0:T(8,128)(2,1)S(1)}, bf16[128,2048]{1,0:T(8,128)(2,1)S(1)}, u32[]{:S(2)}, u32[]{:S(2)}) collective-permute-start(bf16[128,2048]{1,0:T(8,128)(2,1)S(1)} %get-tuple-element.105), channel_id=1, source_target_pairs={{0,3},{1,0},{2,1},{3,2},{4,7},{5,4},{6,5},{7,6},{8,11},{9,8},{10,9... | collective-permute-start | bytes 1572872 | tf_op jit(solution)/shard_map/ppermute | solution.py:566
  58.9 38.0 %collective-permute-start.14 = (bf16[64,2048]{1,0:T(8,128)(2,1)S(1)}, bf16[64,2048]{1,0:T(8,128)(2,1)S(1)}, u32[]{:S(2)}, u32[]{:S(2)}) collective-permute-start(bf16[64,2048]{1,0:T(8,128)(2,1)S(1)} %get-tuple-element.106), channel_id=1, source_target_pairs={{0,1},{1,2},{2,3},{3,0},{4,5},{5,6},{6,7},{7,4},{8,9},{9,10},{10,1... | collective-permute-start | bytes 786440 | tf_op jit(solution)/shard_map/ppermute | solution.py:566
  61.9 18.3 %collective-permute-start.8 = (bf16[2,256,768]{2,1,0:T(8,128)(2,1)S(1)}, bf16[2,256,768]{2,1,0:T(8,128)(2,1)S(1)}, u32[]{:S(2)}, u32[]{:S(2)}) collective-permute-start(bf16[2,256,768]{2,1,0:T(8,128)(2,1)S(1)} %get-tuple-element.92), channel_id=1, source_target_pairs={{0,8},{4,12},{8,0},{12,4},{16,24},{20,28},{24,16},{28,20},{1,9},{5... | collective-permute-start | bytes 2359304 | tf_op jit(solution)/shard_map/ppermute | solution.py:392
  62.2 18.0 %collective-permute-start.9 = (bf16[2,256,768]{2,1,0:T(8,128)(2,1)S(1)}, bf16[2,256,768]{2,1,0:T(8,128)(2,1)S(1)}, u32[]{:S(2)}, u32[]{:S(2)}) collective-permute-start(bf16[2,256,768]{2,1,0:T(8,128)(2,1)S(1)} %get-tuple-element.93), channel_id=1, source_target_pairs={{0,16},{4,20},{8,24},{12,28},{16,0},{20,4},{24,8},{28,12},{1,17},{... | collective-permute-start | bytes 2359304 | tf_op jit(solution)/shard_map/ppermute | solution.py:392
  80.5 8.7 %collective-permute-start.10 = (bf16[256,768]{1,0:T(8,128)(2,1)S(1)}, bf16[256,768]{1,0:T(8,128)(2,1)S(1)}, u32[]{:S(2)}, u32[]{:S(2)}) collective-permute-start(bf16[256,768]{1,0:T(8,128)(2,1)S(1)} %get-tuple-element.95), channel_id=1, source_target_pairs={{0,16},{4,20},{8,24},{12,28},{16,0},{20,4},{24,8},{28,12},{1,17},{... | collective-permute-start | bytes 1179656 | tf_op jit(solution)/shard_map/ppermute | solution.py:392
  81.8 8.3 %collective-permute-start.11 = (bf16[256,768]{1,0:T(8,128)(2,1)S(1)}, bf16[256,768]{1,0:T(8,128)(2,1)S(1)}, u32[]{:S(2)}, u32[]{:S(2)}) collective-permute-start(bf16[256,768]{1,0:T(8,128)(2,1)S(1)} %get-tuple-element.97), channel_id=1, source_target_pairs={{0,8},{4,12},{8,0},{12,4},{16,24},{20,28},{24,16},{28,20},{1,9},{5... | collective-permute-start | bytes 1179656 | tf_op jit(solution)/shard_map/ppermute | solution.py:392
